TPU v7x, 32 devices: a whole 2x2x4 slice. The times are simulated.
32 devices in a mesh: dp: 16 (over z, x, core), pair: 2 (over y).
Axes of the slice: x: 2, y: 2, z: 4, core: 2. Of those that a mesh axis runs over, the one named last changes fastest.
Arguments:
- tokens: bfloat16 [3072, 1792], P('dp'), may hold values from -6 to 6
- grad_out: bfloat16 [3072, 1792], P('dp'), may hold values from -6 to 6
- gate_probs: bfloat16 [3072, 2], P('dp'), may hold values from 0.049804688 to 1
- expert_ids: int32 [3072, 2], P('dp'), may hold values from 0 to 8, as said below
- route_slots: int32 [3072, 2], P('dp'), may hold values from 0 to 191, as said below
- hot_flags: int32 [9], replicated, may hold values from 0 to 1, as said below
- owner_slot: int32 [9], replicated, may hold values from 0 to 7, as said below
- cold_gate: bfloat16 [16, 640, 1792], P('dp', 'pair'), may hold values from -0.125 to 0.125
- cold_up: bfloat16 [16, 640, 1792], P('dp', 'pair'), may hold values from -0.125 to 0.125
- cold_down: bfloat16 [16, 640, 1792], P('dp', 'pair'), may hold values from -0.15625 to 0.15625
- hot_gate: bfloat16 [1280, 1792], P(('dp', 'pair')), may hold values from -0.125 to 0.125
- hot_up: bfloat16 [1280, 1792], P(('dp', 'pair')), may hold values from -0.125 to 0.125
- hot_down: bfloat16 [1280, 1792], P(('dp', 'pair')), may hold values from -0.15625 to 0.15625
Outputs:
- grad_tokens: bfloat16 [3072, 1792], P(('dp', 'pair'))
- grad_probs: float32 [3072, 2], P(('dp', 'pair'))
- grad_cold_gate: bfloat16 [16, 640, 1792], P('dp', 'pair')
- grad_cold_up: bfloat16 [16, 640, 1792], P('dp', 'pair')
- grad_cold_down: bfloat16 [16, 640, 1792], P('dp', 'pair')
- grad_hot_gate: bfloat16 [1280, 1792], P(('dp', 'pair'))
- grad_hot_up: bfloat16 [1280, 1792], P(('dp', 'pair'))
- grad_hot_down: bfloat16 [1280, 1792], P(('dp', 'pair'))
Inputs may be any that keep to these rules, and one draw needn't show every extreme that they name: `expert_ids`: each token names 2 different experts; on every device at least 48 tokens name the hot expert, on some device all of them do, and some cold expert is named by 4 or more tokens. `route_slots`: on one device the routes to one expert carry the slots 0, 1, 2 and so on, each once. `hot_flags`: exactly one entry is 1. `owner_slot`: the cold experts hold the slots 0 to 7, each once; the hot expert's entry is 0.
All inputs are finite; a program needn't handle non-finite values.
Results may differ from a plain program's by a relative error of at most 0.0049.
Values may be sent and summed in bfloat16 or wider, within the bound.
No kernel may reach another device: no remote copies, remote signals or barrier semaphores. Data moves between devices by JAX's collectives and lax.ppermute only.
A program may use at most 192 MiB of HBM per device.

v0:
```python
import functools

import jax
import jax.numpy as jnp
from jax import lax
from jax.experimental import pallas as pl
from jax.experimental.pallas import tpu as pltpu
from jax.sharding import PartitionSpec as P

TOP = 2
CAP = 4
HCAP = 48
HALF = HCAP // 2
TAIL = 128
CHUNK_BLOCK = 8
COLD_BLOCK = 64
COLD_ROWS = 128
UNIT_BLOCK = 128
BF = jnp.bfloat16
F32 = jnp.float32
VMEM_LIMIT = 56 * 1024 * 1024
VMEM_BASE = 12 * 1024 * 1024

NT = (((1,), (1,)), ((), ()))
TN = (((0,), (0,)), ((), ()))


def dot(a, b, dims=(((1,), (0,)), ((), ()))):
    return lax.dot_general(a, b, dims, preferred_element_type=F32)


def iota(shape, dim):
    return lax.broadcasted_iota(jnp.int32, shape, dim)


def positions(ids, slots, flags_ref, owner_ref, base):
    hot = jnp.zeros_like(ids)
    own = jnp.zeros_like(ids)
    for e in range(flags_ref.shape[0]):
        named = ids == e
        hot = jnp.where(named, flags_ref[e], hot)
        own = jnp.where(named, owner_ref[e], own)
    cold_pos = jnp.where(slots < CAP, own * CAP + slots, -1)
    hot_pos = jnp.where(slots < HCAP, base + slots, -1)
    return jnp.where(hot == 1, hot_pos, cold_pos)


def tail_lanes(first, second=None):
    lane = iota((first.shape[0], TAIL), 1)
    out = jnp.where(lane == 0, first, 0.0)
    if second is not None:
        out = jnp.where(lane == 1, second, out)
    return out


def split_tail(value):
    high = value.astype(BF).astype(F32)
    return tail_lanes(high, value - high)


def each_block(total, size, body):
    if total == size:
        body(0)
    else:

        def step(block, carry):
            body(pl.multiple_of(block * size, size))
            return carry

        lax.fori_loop(0, total // size, step, 0)


def add_to(ref, value, single):
    if single:
        ref[...] = value.astype(ref.dtype)
    else:
        ref[...] += value


def gather_rows(out_ref, start, target, is_grad, pos, prob, tok_ref, grad_ref):
    width = tok_ref.shape[1]
    at = pl.ds(start, target.shape[0])
    first = pos[0:1, :] == target
    second = pos[1:2, :] == target
    chosen = jnp.where(first | second, 1.0, 0.0)
    rows = dot(jnp.where(is_grad, 0.0, chosen).astype(BF), tok_ref[...]) + dot(
        jnp.where(is_grad, chosen, 0.0).astype(BF), grad_ref[...]
    )
    out_ref[at, :width] = rows.astype(BF)
    weight = jnp.where(first, prob[0:1, :], 0.0) + jnp.where(second, prob[1:2, :], 0.0)
    weight = jnp.sum(jnp.where(is_grad, 0.0, weight), axis=1, keepdims=True)
    out_ref[at, width:] = tail_lanes(weight).astype(BF)


def dispatch_kernel(base, *refs):
    tok_ref, grad_ref, prob_ref, ids_ref, slot_ref, flags_ref, owner_ref = refs[:7]
    gate_ref, up_ref, down_ref, pos_ref, weight_ref, *messages, cold_ref = refs[7:]
    pair = lax.axis_index("pair")
    me = lax.axis_index("dp")
    z, x = me // 4, (me // 2) % 2
    pos = positions(ids_ref[...], slot_ref[...], flags_ref, owner_ref, base)
    pos_ref[...] = pos
    joined = [ref[...].astype(F32) for ref in (gate_ref, up_ref, down_ref)]
    weight_ref[...] = jnp.concatenate(joined, axis=0).astype(BF)
    prob = prob_ref[...].astype(F32)

    def gather(out_ref, start, target, is_grad):
        gather_rows(out_ref, start, target, is_grad, pos, prob, tok_ref, grad_ref)

    row = iota((HCAP, tok_ref.shape[0]), 0)
    target = base + HALF * pair + jnp.where(row >= HALF, row - HALF, row)
    gather(messages[0], 0, target, row >= HALF)

    def block(start):
        row = start + iota((COLD_BLOCK, tok_ref.shape[0]), 0)
        chip = 2 * (z ^ (row >> 4)) + (x ^ ((row >> 3) & 1))
        gather(cold_ref, start, chip * CAP + (row & 3), (row & 4) != 0)

    each_block(cold_ref.shape[0], COLD_BLOCK, block)
    for k, message in enumerate(messages):
        if k:
            message[:HCAP, :] = messages[0][:HCAP, :]
        message[HCAP:, :] = cold_ref[k * 16 : (k + 1) * 16, :]


def away_kernel(*refs):
    *messages, out_ref = refs
    rows = [ref[HCAP:, :].astype(F32)[2 * CAP :] for ref in messages]
    out_ref[...] = jnp.concatenate(rows, axis=0).astype(BF)


def swiglu_back(pre_gate, pre_up, back, prob):
    sig = 1.0 / (1.0 + jnp.exp(-pre_gate))
    act = pre_gate * sig
    hidden = act * pre_up
    scaled = prob * back
    gate_grad = scaled * pre_up * sig * (1.0 + pre_gate * (1.0 - sig))
    return gate_grad, scaled * act, prob * hidden, hidden * back


def write_rows(out_ref, rows, prob):
    width = rows.shape[1]
    out_ref[:, :width] = rows.astype(out_ref.dtype)
    tail = tail_lanes(prob) if out_ref.dtype == F32 else split_tail(prob).astype(BF)
    out_ref[:, width:] = tail


def read_rows(value):
    value = value.astype(F32)
    width = value.shape[1] - TAIL
    return value[:, :width], value[:, width : width + 1] + value[:, width + 1 : width + 2]


def hot_kernel(chunk_count, units, *refs):
    chunks = refs[:chunk_count]
    weights = refs[chunk_count : chunk_count + 4]
    own_ref, send_ref, *terms = refs[chunk_count + 4 : chunk_count + 10]
    rows_ref, tail_ref, wide_ref, sum_ref = refs[chunk_count + 10 :]
    width = rows_ref.shape[1]
    for k, chunk in enumerate(chunks):
        rows_ref[k * HCAP : (k + 1) * HCAP, :] = chunk[:HCAP, :width]
        tail_ref[k * HCAP : (k + 1) * HCAP, :] = chunk[:HCAP, width:]
    used = 3 * units
    for j, w_ref in enumerate(weights):
        start = j * UNIT_BLOCK
        clear = used // 16 * 16
        if clear < UNIT_BLOCK:
            wide_ref[start + clear : start + UNIT_BLOCK, :] = jnp.zeros((UNIT_BLOCK - clear, width), BF)
        wide_ref[start : start + used, :] = w_ref[...]
    columns = 4 * UNIT_BLOCK
    block_chunks = min(CHUNK_BLOCK, chunk_count)
    block_rows = block_chunks * HCAP
    half_rows = block_rows // 2
    single = block_chunks == chunk_count

    def block(start):
        at = pl.ds(start, block_rows)
        prob = tail_ref[at, :].astype(F32).reshape(block_chunks, HCAP, TAIL)[:, :HALF, 0:1]
        prob = prob.reshape(half_rows, 1)
        pre = dot(rows_ref[at, :], wide_ref[...], NT).reshape(block_chunks, HCAP, columns)
        pre_x = pre[:, :HALF].reshape(half_rows, columns)
        pre_g = pre[:, HALF:].reshape(half_rows, columns)
        first = (iota(pre_x.shape, 1) & (UNIT_BLOCK - 1)) < units
        gate_grad, up_grad, weighted, prob_term = swiglu_back(
            pre_x,
            pltpu.roll(pre_x, columns - units, 1),
            pltpu.roll(pre_g, columns - 2 * units, 1),
            prob,
        )
        gate_grad, up_grad, weighted, prob_term = (
            jnp.where(first, value, 0.0) for value in (gate_grad, up_grad, weighted, prob_term)
        )
        grad_prob = jnp.sum(prob_term, axis=1, keepdims=True)
        x_side = gate_grad + pltpu.roll(up_grad, units, 1)
        g_side = pltpu.roll(weighted, 2 * units, 1)
        both = jnp.concatenate(
            [x_side.reshape(block_chunks, HALF, columns), g_side.reshape(block_chunks, HALF, columns)],
            axis=1,
        )
        both = both.reshape(block_rows, columns).astype(BF)
        dx = dot(x_side.astype(BF), wide_ref[...])
        for j in range(4):
            term = dot(both[:, j * UNIT_BLOCK : (j + 1) * UNIT_BLOCK], rows_ref[at, :], TN)
            add_to(terms[j] if single else sum_ref.at[j], term[:used], single)
        return dx, grad_prob

    if single:
        dx, grad_prob = block(0)
        write_rows(own_ref, dx[: half_rows // 2], grad_prob[: half_rows // 2])
        write_rows(send_ref, dx[half_rows // 2 :], grad_prob[half_rows // 2 :])
    else:
        sum_ref[...] = jnp.zeros_like(sum_ref)
        for out_ref, offset in ((own_ref, 0), (send_ref, chunk_count * HCAP // 2)):

            def step(index, carry, out_ref=out_ref, offset=offset):
                dx, grad_prob = block(pl.multiple_of(offset + index * block_rows, 16))
                at = pl.ds(pl.multiple_of(index * half_rows, 16), half_rows)
                write_rows(out_ref.at[at], dx, grad_prob)
                return carry

            lax.fori_loop(0, chunk_count // block_chunks // 2, step, 0)
        for j, out_ref in enumerate(terms):
            out_ref[...] = sum_ref[j].astype(out_ref.dtype)


def cold_kernel(message_count, *refs):
    messages = refs[:message_count]
    mine_x_ref, other_x_ref, gate_hbm, up_hbm, down_hbm = refs[message_count : message_count + 5]
    own_ref, send_ref, *outs = refs[message_count + 5 : message_count + 10]
    data_ref, dx_ref, w_ref, grad_ref, sum_ref, in_sem, out_sem = refs[message_count + 10 :]
    total, width = data_ref.shape[0], gate_hbm.shape[2]
    rows = COLD_ROWS
    single = rows == total
    loads = [
        pltpu.make_async_copy(ref.at[0], w_ref.at[j], in_sem.at[j])
        for j, ref in enumerate((gate_hbm, up_hbm, down_hbm))
    ]
    stores = [
        pltpu.make_async_copy(grad_ref.at[j], ref.at[0], out_sem.at[j]) for j, ref in enumerate(outs)
    ]
    for load in loads:
        load.start()
    quarter = total // 4
    z_count = message_count // 2
    for flip, away_ref in enumerate((mine_x_ref, other_x_ref)):
        near = [ref[HCAP:, :].astype(F32)[: 2 * CAP] for ref in messages[flip * z_count :][:z_count]]
        start = 2 * flip * quarter
        data_ref[start : start + quarter, :] = jnp.concatenate(near, axis=0).astype(BF)
        data_ref[start + quarter : start + 2 * quarter, :] = away_ref[...]
    if not single:
        sum_ref[...] = jnp.zeros_like(sum_ref)
        for load in loads:
            load.wait()

    def weight(j):
        if single:
            loads[j].wait()
        return w_ref[j]

    def block(start):
        at = pl.ds(start, rows)
        data = data_ref[at, :width]
        prob = data_ref[at, width:].astype(F32)[:, 0:1]
        gate = weight(0)
        pre_gate = dot(data, gate, NT)
        up = weight(1)
        pre_up = dot(data, up, NT)
        back = pltpu.roll(dot(data, weight(2), NT), rows - CAP, 0)
        gate_grad, up_grad, weighted, prob_term = swiglu_back(pre_gate, pre_up, back, prob)
        x_row = (iota(pre_gate.shape, 0) & 4) == 0
        gate_grad = jnp.where(x_row, gate_grad, 0.0).astype(BF)
        up_grad = jnp.where(x_row, up_grad, 0.0).astype(BF)
        weighted = pltpu.roll(jnp.where(x_row, weighted, 0.0), CAP, 0).astype(BF)
        prob_term = jnp.where(x_row, prob_term, 0.0)
        for j, grad in enumerate((gate_grad, up_grad, weighted)):
            term = dot(grad, data, TN)
            if single:
                grad_ref[j] = term.astype(BF)
                stores[j].start()
            else:
                sum_ref[j] += term
        shape = (rows // 2, rows)
        row, col = iota(shape, 0), iota(shape, 1)
        pick = jnp.where(col == (row >> 2) * 8 + (row & 3), 1.0, 0.0).astype(BF)
        gate_rows = dot(pick, gate_grad).astype(BF)
        up_rows = dot(pick, up_grad).astype(BF)
        dx = dot(gate_rows, gate) + dot(up_rows, up)
        tail = dot(pick, split_tail(jnp.sum(prob_term, axis=1, keepdims=True)).astype(BF))
        grad_prob = tail[:, 0:1] + tail[:, 1:2]
        half_at = pl.ds(start // 2 if single else pl.multiple_of(start // 2, 16), rows // 2)
        write_rows(dx_ref.at[half_at], dx, grad_prob)

    each_block(total, rows, block)
    own_ref[...] = dx_ref[: total // 4, :]
    dx_rows, dx_prob = read_rows(dx_ref[total // 4 :, :])
    write_rows(send_ref, dx_rows, dx_prob)
    if not single:
        for j in range(3):
            grad_ref[j] = sum_ref[j].astype(BF)
            stores[j].start()
    for store in stores:
        store.wait()


def add_kernel(hot_own_ref, hot_got_ref, cold_own_ref, cold_got_ref, *outs):
    def added(own_ref, got_ref):
        rows, prob = read_rows(own_ref[...])
        got_rows, got_prob = read_rows(got_ref[...])
        return jnp.concatenate([rows + got_rows, tail_lanes(prob + got_prob)], axis=1)

    hot = added(hot_own_ref, hot_got_ref)
    cold = added(cold_own_ref, cold_got_ref)
    half = cold.shape[0] // 2
    width = cold.shape[1] - TAIL
    for k, out_ref in enumerate(outs):
        at = k // 2 * 2 * CAP
        near, far = cold[at : at + 2 * CAP], cold[half + at : half + at + 2 * CAP]
        low = (iota(near.shape, 0) & 4) == 0
        if k % 2:
            part = jnp.where(low, pltpu.roll(near, CAP, 0), far)
        else:
            part = jnp.where(low, near, pltpu.roll(far, CAP, 0))
        rows = jnp.concatenate([hot[k * HALF : (k + 1) * HALF], part], axis=0)
        write_rows(out_ref, rows[:, :width], rows[:, width : width + 1])


def combine_kernel(*refs):
    *parts, own_ref, send_y_ref, send_x_ref = refs
    hot, cold = 0.0, []
    for ref in parts:
        rows, prob = read_rows(ref[...])
        both = jnp.concatenate([rows, tail_lanes(prob)], axis=1)
        hot = hot + both[:HALF]
        cold.append(both[HALF:])
    low = (iota(cold[0].shape, 0) & 4) == 0
    mine, other = [], []
    for even, odd in zip(cold[0::2], cold[1::2]):
        mine.append(jnp.where(low, even, pltpu.roll(odd, CAP, 0)))
        other.append(jnp.where(low, pltpu.roll(even, CAP, 0), odd))
    rows = jnp.concatenate([hot] + mine, axis=0)
    away = jnp.concatenate(other, axis=0)
    width = rows.shape[1] - TAIL
    own_ref[...] = rows
    write_rows(send_y_ref, rows[:, :width], rows[:, width : width + 1])
    write_rows(send_x_ref, away[:, :width], away[:, width : width + 1])


def finish_kernel(base, own_ref, y_ref, x_ref, xy_ref, pos_ref, dx_ref, prob_ref):
    pair = lax.axis_index("pair")
    me = lax.axis_index("dp")
    z, x = me // 4, (me // 2) % 2
    half = dx_ref.shape[0]
    pos = jnp.where(pair == 0, pos_ref[:, :half], pos_ref[:, half:])

    def cold_target(row, side):
        return (2 * (z ^ (row >> 2)) + side) * CAP + (row & 3)

    def with_hot(side):
        row = iota((own_ref.shape[0], half), 0)
        return jnp.where(row < HALF, base + HALF * side + row, cold_target(row - HALF, x))

    away = cold_target(iota((x_ref.shape[0], half), 0), 1 - x)
    total = 0.0
    grad_prob = [0.0] * TOP
    for ref, target in (
        (own_ref, with_hot(pair)),
        (y_ref, with_hot(1 - pair)),
        (x_ref, away),
        (xy_ref, away),
    ):
        routes = [pos[k : k + 1, :] == target for k in range(TOP)]
        onehot = jnp.where(routes[0] | routes[1], 1.0, 0.0).astype(BF)
        rows, prob = read_rows(ref[...])
        high = rows.astype(BF)
        total = total + dot(onehot, high, TN)
        if ref.dtype == F32:
            total = total + dot(onehot, (rows - high.astype(F32)).astype(BF), TN)
        for k in range(TOP):
            terms = jnp.sum(jnp.where(routes[k], prob, 0.0), axis=0, keepdims=True)
            grad_prob[k] = grad_prob[k] + terms
    dx_ref[...] = total.astype(BF)
    for k in range(TOP):
        prob_ref[k : k + 1, :] = grad_prob[k]


def sum_kernel(own_ref, a_ref, b_ref, c_ref, gate_ref, up_ref, down_ref):
    total = own_ref[...] + a_ref[...].astype(F32) + b_ref[...].astype(F32) + c_ref[...].astype(F32)
    units = gate_ref.shape[0]
    for index, out_ref in enumerate((gate_ref, up_ref, down_ref)):
        out_ref[...] = total[index * units : (index + 1) * units].astype(BF)


def call(kernel, outs, name, scratch=(), smem=(), hbm=(), out_hbm=(), limit=0):
    def run(*args):
        def space(index, far, smem=()):
            return pltpu.SMEM if index in smem else pltpu.HBM if index in far else pltpu.VMEM

        moved = sum(a.size * a.dtype.itemsize for a in args)
        moved += sum(o.size * o.dtype.itemsize for o in outs)
        return pl.pallas_call(
            kernel,
            out_shape=outs,
            in_specs=[pl.BlockSpec(memory_space=space(i, hbm, smem)) for i in range(len(args))],
            out_specs=[pl.BlockSpec(memory_space=space(i, out_hbm)) for i in range(len(outs))],
            scratch_shapes=[pltpu.VMEM(*s) if isinstance(s, tuple) else s for s in scratch],
            compiler_params=pltpu.CompilerParams(
                vmem_limit_bytes=limit or min(VMEM_LIMIT, VMEM_BASE + 3 * moved // 2)
            ),
            cost_estimate=pl.CostEstimate(flops=1024, bytes_accessed=1024, transcendentals=0),
            name=name,
        )(*args)

    return run


def local(
    tokens,
    grad_out,
    gate_probs,
    expert_ids,
    route_slots,
    hot_flags,
    owner_slot,
    cold_gate,
    cold_up,
    cold_down,
    hot_gate,
    hot_up,
    hot_down,
):
    count = lax.axis_size("dp")
    z_count = count // 4
    chunk_count = 2 * z_count
    token_count, width = tokens.shape
    lanes = width + TAIL
    units = hot_gate.shape[0]
    base = (count // 2) * CAP
    shape = jax.ShapeDtypeStruct
    half = token_count // 2
    pad = -units % 8

    def swap(value, mask):
        flip_dp, flip_pair = 2 * (mask & 1), mask >> 1
        perm = [
            (2 * i + p, 2 * (i ^ flip_dp) + (p ^ flip_pair)) for i in range(count) for p in range(2)
        ]
        return lax.ppermute(value, ("dp", "pair"), perm)

    def along_z(value, k):
        perm = [(i, 4 * ((i // 4) ^ k) + i % 4) for i in range(count)]
        return lax.ppermute(value, "dp", perm)

    def other_core(value):
        return lax.ppermute(value, "dp", [(i, i ^ 1) for i in range(count)])

    hot_weights = [jnp.pad(w, ((0, pad), (0, 0))) if pad else w for w in (hot_gate, hot_up, hot_down)]
    units_padded = units + pad
    used = 3 * units_padded
    cold_rows = z_count * 2 * 2 * CAP
    message = shape((HCAP + 4 * CAP, lanes), BF)
    pos, hot_own, *messages = call(
        functools.partial(dispatch_kernel, base),
        [shape((TOP, token_count), jnp.int32), shape((used, width), BF)] + [message] * z_count,
        "dispatch",
        scratch=[((cold_rows, lanes), BF)],
        smem=(5, 6),
        limit=VMEM_LIMIT,
    )(
        tokens,
        grad_out,
        gate_probs.T,
        expert_ids.T,
        route_slots.T,
        hot_flags,
        owner_slot,
        *hot_weights,
    )

    chunks = [messages[0]] + [along_z(messages[k], k) for k in range(1, z_count)]
    by_pair = swap(hot_own, 2)
    by_x = swap(hot_own, 1)
    first_out, by_pair_out, _ = lax.optimization_barrier((messages[0], by_pair, chunks[1]))
    weights = [hot_own, by_x, by_pair, swap(by_pair_out, 1)]
    (away,) = call(away_kernel, [shape((cold_rows // 2, lanes), BF)], "cold_away")(*chunks)
    chunks = chunks + [other_core(first_out)] + [other_core(chunk) for chunk in chunks[1:]]
    cold_mine = swap(away, 1)
    cold_other = other_core(cold_mine)

    cold_units = cold_gate.shape[1]
    cold_shape = shape(cold_gate.shape, BF)
    all_rows = chunk_count * HCAP
    half_rows = chunk_count * HALF // 2
    term = shape((used, width), BF)
    hot_dx, hot_dx_out, own_term, *sent_terms = call(
        functools.partial(hot_kernel, chunk_count, units_padded),
        [
            shape((half_rows, lanes), F32),
            shape((half_rows, lanes), BF),
            shape(term.shape, F32),
            term,
            term,
            term,
        ],
        "hot",
        scratch=[
            ((all_rows, width), BF),
            ((all_rows, TAIL), BF),
            ((4 * UNIT_BLOCK, width), BF),
            ((4, used, width) if chunk_count > CHUNK_BLOCK else (8, 128), F32),
        ],
    )(*chunks, *weights)

    cold_mine, hot_dx = lax.optimization_barrier((cold_mine, hot_dx))
    cold_own, cold_out, grad_cold_gate, grad_cold_up, grad_cold_down = call(
        functools.partial(cold_kernel, chunk_count),
        [shape((cold_rows // 2, lanes), F32), shape((cold_rows // 2, lanes), BF)] + [cold_shape] * 3,
        "cold",
        scratch=[
            ((2 * cold_rows, lanes), BF),
            ((cold_rows, lanes), F32),
            ((3, cold_units, width), BF),
            ((3, cold_units, width), BF),
            ((3, cold_units, width) if 2 * cold_rows > COLD_ROWS else (8, 128), F32),
            pltpu.SemaphoreType.DMA((3,)),
            pltpu.SemaphoreType.DMA((3,)),
        ],
        hbm=range(chunk_count + 2, chunk_count + 5),
        out_hbm=(2, 3, 4),
    )(*chunks, cold_mine, cold_other, cold_gate, cold_up, cold_down)

    hot_got, cold_got = other_core(hot_dx_out), other_core(cold_out)
    part = (HALF + 2 * CAP, lanes)
    parts = call(
        add_kernel, [shape(part, F32)] + [shape(part, BF)] * (z_count - 1), "add_cores"
    )(hot_dx, hot_got, cold_own, cold_got)
    got_x, got_y = swap(sent_terms[0], 1), swap(sent_terms[1], 2)
    *parts, got_x, got_y, last_term = lax.optimization_barrier((*parts, got_x, got_y, sent_terms[2]))
    parts = [parts[0]] + [along_z(parts[k], k) for k in range(1, z_count)]
    got_terms = [got_x, got_y, swap(last_term, 3)]

    cold_back = z_count * CAP
    own_rows, send_y, send_x = call(
        combine_kernel,
        [
            shape((HALF + cold_back, lanes), F32),
            shape((HALF + cold_back, lanes), BF),
            shape((cold_back, lanes), BF),
        ],
        "combine",
    )(*parts)
    rows_y, rows_x, rows_xy = swap(send_y, 2), swap(send_x, 1), swap(send_x, 3)
    dx, prob_t = call(
        functools.partial(finish_kernel, base),
        [shape((half, width), BF), shape((TOP, half), F32)],
        "finish",
    )(own_rows, rows_y, rows_x, rows_xy, pos)

    out_shape = shape((units_padded, width), BF)
    hot_grads = call(sum_kernel, [out_shape] * 3, "hot_sum")(
        own_term, *got_terms
    )
    if pad:
        hot_grads = [value[:units] for value in hot_grads]
    return (dx, prob_t.T, grad_cold_gate, grad_cold_up, grad_cold_down, *hot_grads)


def solution(mesh):
    return jax.shard_map(
        local,
        mesh=mesh,
        in_specs=(
            P("dp", None),
            P("dp", None),
            P("dp", None),
            P("dp", None),
            P("dp", None),
            P(),
            P(),
            P("dp", "pair", None),
            P("dp", "pair", None),
            P("dp", "pair", None),
            P(("dp", "pair"), None),
            P(("dp", "pair"), None),
            P(("dp", "pair"), None),
        ),
        out_specs=(
            P(("dp", "pair"), None),
            P(("dp", "pair"), None),
            P("dp", "pair", None),
            P("dp", "pair", None),
            P("dp", "pair", None),
            P(("dp", "pair"), None),
            P(("dp", "pair"), None),
            P(("dp", "pair"), None),
        ),
        check_vma=False,
    )
```

profile of v0, /device:TPU:0, one launch (start us, length us, event | category | flops | bytes accessed | tf_op | source)
XLA Modules:
  0.0 86.8 jit_solution(6786039713051312476)
XLA Ops:
  0.6 3.1 %dispatch.1 = (s32[2,192]{1,0:T(2,128)}, bf16[120,1792]{1,0:T(8,128)(2,1)}, bf16[64,1920]{1,0:T(8,128)(2,1)}, bf16[64,1920]{1,0:T(8,128)(2,1)}, bf16[64,1920]{1,0:T(8,128)(2,1)}, /*index=5*/bf16[64,1920]{1,0:T(8,128)(2,1)}) custom-call(bf16[192,1792]{1,0:T(8,128)(2,1)} %refs_0_.1, bf16[192,1792]{1,0:T(8,128)(2,1)} %refs_1_.1, bf16[2,192]{1,0:T(2,128)(2,1)} %bitcast.6, ...), custom_call_target="tpu_custom_call" | custom-call | flops 1024 | bytes 1024 | tf_op jit(solution)/shard_map/dispatch/pallas_call | solution.py:400
  3.8 3.0 %collective-permute-start.4 = (bf16[120,1792]{1,0:T(8,128)(2,1)}, bf16[120,1792]{1,0:T(8,128)(2,1)S(1)}, u32[]{:S(2)}, u32[]{:S(2)}) collective-permute-start(bf16[120,1792]{1,0:T(8,128)(2,1)} %get-tuple-element.52.refs_8_), channel_id=1, source_target_pairs={{0,1},{1,0},{2,3},{3,2},{4,5},{5,4},{6,7},{7,6},{8,9},{9,8},{10,11... | collective-permute-start | bytes 1290248 | tf_op jit(solution)/shard_map/ppermute | solution.py:447
  6.7 1.6 %collective-permute-start = (bf16[64,1920]{1,0:T(8,128)(2,1)}, bf16[64,1920]{1,0:T(8,128)(2,1)S(1)}, u32[]{:S(2)}, u32[]{:S(2)}) collective-permute-start(bf16[64,1920]{1,0:T(8,128)(2,1)} %get-tuple-element.49), channel_id=1, source_target_pairs={{0,8},{2,10},{4,12},{6,14},{8,0},{10,2},{12,4},{14,6},{16,24},{18,... | collective-permute-start | bytes 737288 | tf_op jit(solution)/shard_map/ppermute | solution.py:451
  8.3 1.5 %collective-permute-start.9 = (bf16[120,1792]{1,0:T(8,128)(2,1)}, bf16[120,1792]{1,0:T(8,128)(2,1)S(1)}, u32[]{:S(2)}, u32[]{:S(2)}) collective-permute-start(bf16[120,1792]{1,0:T(8,128)(2,1)} %get-tuple-element.52.refs_8_), channel_id=1, source_target_pairs={{0,4},{1,5},{2,6},{3,7},{4,0},{5,1},{6,2},{7,3},{8,12},{9,13},{10,... | collective-permute-start | bytes 1290248 | tf_op jit(solution)/shard_map/ppermute | solution.py:447
  9.8 2.6 %collective-permute-start.1 = (bf16[64,1920]{1,0:T(8,128)(2,1)}, bf16[64,1920]{1,0:T(8,128)(2,1)S(1)}, u32[]{:S(2)}, u32[]{:S(2)}) collective-permute-start(bf16[64,1920]{1,0:T(8,128)(2,1)} %get-tuple-element.50), channel_id=1, source_target_pairs={{0,16},{2,18},{4,20},{6,22},{8,24},{10,26},{12,28},{14,30},{16,0},... | collective-permute-start | bytes 737288 | tf_op jit(solution)/shard_map/ppermute | solution.py:451
  12.4 0.2 collective-permute-start.2
  12.6 5.3 %collective-permute-done.refs_1_ = bf16[64,1920]{1,0:T(8,128)(2,1)S(1)} collective-permute-done((bf16[64,1920]{1,0:T(8,128)(2,1)}, bf16[64,1920]{1,0:T(8,128)(2,1)S(1)}, u32[]{:S(2)}, u32[]{:S(2)}) %collective-permute-start) | collective-permute-done | bytes 245792 | tf_op jit(solution)/shard_map/ppermute | solution.py:451
  17.9 0.0 collective-permute-done.4.refs_10_
  17.9 2.0 %collective-permute-start.10 = (bf16[120,1792]{1,0:T(8,128)(2,1)S(1)}, bf16[120,1792]{1,0:T(8,128)(2,1)S(1)}, u32[]{:S(2)}, u32[]{:S(2)}) collective-permute-start(bf16[120,1792]{1,0:T(8,128)(2,1)S(1)} %collective-permute-done.4.refs_10_), channel_id=1, source_target_pairs={{0,4},{1,5},{2,6},{3,7},{4,0},{5,1},{6,2},{7,3},{8,12},{9,13},{10,... | collective-permute-start | bytes 1290248 | tf_op jit(solution)/shard_map/ppermute | solution.py:447
  19.9 0.0 collective-permute-start.6
  19.9 10.4 %collective-permute-done.1.refs_2_ = bf16[64,1920]{1,0:T(8,128)(2,1)S(1)} collective-permute-done((bf16[64,1920]{1,0:T(8,128)(2,1)}, bf16[64,1920]{1,0:T(8,128)(2,1)S(1)}, u32[]{:S(2)}, u32[]{:S(2)}) %collective-permute-start.1) | collective-permute-done | bytes 245792 | tf_op jit(solution)/shard_map/ppermute | solution.py:451
  30.3 0.0 collective-permute-start.7
  30.3 0.0 collective-permute-done.2.refs_3_
  30.3 0.5 collective-permute-start.8
  30.8 0.0 collective-permute-done.9.refs_9_
  30.8 0.1 collective-permute-start.5
  30.9 0.0 collective-permute-done.6.refs_5_
  30.9 0.9 %collective-permute-done.7.refs_6_ = bf16[64,1920]{1,0:T(8,128)(2,1)S(1)} collective-permute-done((bf16[64,1920]{1,0:T(8,128)(2,1)S(1)}, bf16[64,1920]{1,0:T(8,128)(2,1)S(1)}, u32[]{:S(2)}, u32[]{:S(2)}) %collective-permute-start.7) | collective-permute-done | bytes 245792 | tf_op jit(solution)/shard_map/ppermute | solution.py:454
  31.8 0.4 collective-permute-done.8.refs_7_
  32.2 0.6 collective-permute-done.5.refs_4_
  32.8 0.0 collective-permute-done.10.refs_11_
  32.8 0.0 copy-start
  32.8 0.9 %copy-done = bf16[64,1920]{1,0:T(8,128)(2,1)S(1)} copy-done((bf16[64,1920]{1,0:T(8,128)(2,1)S(1)}, bf16[64,1920]{1,0:T(8,128)(2,1)}, u32[]{:S(2)}) %copy-start) | copy-done | bytes 245784
  33.7 0.0 copy-start.5
  33.7 1.0 %copy-done.5 = bf16[120,1792]{1,0:T(8,128)(2,1)S(1)} copy-done((bf16[120,1792]{1,0:T(8,128)(2,1)S(1)}, bf16[120,1792]{1,0:T(8,128)(2,1)}, u32[]{:S(2)}) %copy-start.5) | copy-done | bytes 430104
  34.7 2.7 %hot.1 = (f32[96,1920]{1,0:T(8,128)S(1)}, bf16[96,1920]{1,0:T(8,128)(2,1)S(1)}, f32[120,1792]{1,0:T(8,128)S(1)}, bf16[120,1792]{1,0:T(8,128)(2,1)S(1)}, bf16[120...) custom-call(bf16[64,1920]{1,0:T(8,128)(2,1)S(1)} %copy-done, bf16[64,1920]{1,0:T(8,128)(2,1)S(1)} %collective-permute-done.refs_1_, ...), custom_call_target="tpu_custom_call" | custom-call | flops 1024 | bytes 1024 | tf_op jit(solution)/shard_map/hot/pallas_call | solution.py:400
  37.4 0.0 copy-start.1
  37.4 0.6 collective-permute-start.14
  38.0 0.5 collective-permute-start.15
  38.5 1.6 %collective-permute-start.3 = (bf16[32,1920]{1,0:T(8,128)(2,1)S(1)}, bf16[32,1920]{1,0:T(8,128)(2,1)S(1)}, u32[]{:S(2)}, u32[]{:S(2)}) collective-permute-start(bf16[32,1920]{1,0:T(8,128)(2,1)S(1)} %cold_away.1), channel_id=1, source_target_pairs={{0,4},{1,5},{2,6},{3,7},{4,0},{5,1},{6,2},{7,3},{8,12},{9,13},{10,... | collective-permute-start | bytes 368648 | tf_op jit(solution)/shard_map/ppermute | solution.py:447
  40.1 0.0 collective-permute-start.11
  40.1 12.0 %collective-permute-done.3.refs_8_ = bf16[32,1920]{1,0:T(8,128)(2,1)S(1)} collective-permute-done((bf16[32,1920]{1,0:T(8,128)(2,1)S(1)}, bf16[32,1920]{1,0:T(8,128)(2,1)S(1)}, u32[]{:S(2)}, u32[]{:S(2)}) %collective-permute-start.3) | collective-permute-done | bytes 122912 | tf_op jit(solution)/shard_map/ppermute | solution.py:447
  52.1 0.0 collective-permute-start.12
  52.1 1.3 %collective-permute-done.12.refs_9_ = bf16[32,1920]{1,0:T(8,128)(2,1)S(1)} collective-permute-done((bf16[32,1920]{1,0:T(8,128)(2,1)S(1)}, bf16[32,1920]{1,0:T(8,128)(2,1)S(1)}, u32[]{:S(2)}, u32[]{:S(2)}) %collective-permute-start.12) | collective-permute-done | bytes 122912 | tf_op jit(solution)/shard_map/ppermute | solution.py:454
  53.4 0.0 copy-done.2
  53.4 0.0 copy-done.3
  53.4 0.0 copy-done.4
  53.4 0.0 copy-done.1
  53.4 5.5 %cold.1 = (f32[32,1920]{1,0:T(8,128)S(1)}, bf16[32,1920]{1,0:T(8,128)(2,1)S(1)}, bf16[1,320,1792]{2,1,0:T(8,128)(2,1)}, bf16[1,320,1792]{2,1,0:T(8,128)(2,1)}, bf16[1,320,1792]{2,1,0:T(8,128)(2,1)}) custom-call(bf16[64,1920]{1,0:T(8,128)(2,1)S(1)} %copy-done.1, bf16[64,1920]{1,0:T(8,128)(2,1)S(1)} %collective-permute-done.refs_1_, ...), custom_call_target="tpu_custom_call" | custom-call | flops 1024 | bytes 1024 | tf_op jit(solution)/shard_map/cold/pallas_call | solution.py:400
  58.9 0.0 copy-start.6
  58.9 0.2 collective-permute-start.13
  59.1 1.2 %collective-permute-done.13.cold_got_ref = bf16[32,1920]{1,0:T(8,128)(2,1)S(1)} collective-permute-done((bf16[32,1920]{1,0:T(8,128)(2,1)S(1)}, bf16[32,1920]{1,0:T(8,128)(2,1)S(1)}, u32[]{:S(2)}, u32[]{:S(2)}) %collective-permute-start.13) | collective-permute-done | bytes 122912 | tf_op jit(solution)/shard_map/ppermute | solution.py:454
  60.3 0.0 collective-permute-done.11.hot_got_ref
  60.3 0.3 add_cores.1
  60.6 0.0 collective-permute-done.14.a_ref
  60.6 0.0 collective-permute-done.15.b_ref
  60.6 0.5 collective-permute-start.22
  61.2 3.5 %collective-permute-start.16 = (bf16[32,1920]{1,0:T(8,128)(2,1)S(1)}, bf16[32,1920]{1,0:T(8,128)(2,1)S(1)}, u32[]{:S(2)}, u32[]{:S(2)}) collective-permute-start(bf16[32,1920]{1,0:T(8,128)(2,1)S(1)} %get-tuple-element.69), channel_id=1, source_target_pairs={{0,8},{2,10},{4,12},{6,14},{8,0},{10,2},{12,4},{14,6},{16,24},{18,... | collective-permute-start | bytes 368648 | tf_op jit(solution)/shard_map/ppermute | solution.py:451
  64.7 1.0 %collective-permute-start.17 = (bf16[32,1920]{1,0:T(8,128)(2,1)S(1)}, bf16[32,1920]{1,0:T(8,128)(2,1)S(1)}, u32[]{:S(2)}, u32[]{:S(2)}) collective-permute-start(bf16[32,1920]{1,0:T(8,128)(2,1)S(1)} %get-tuple-element.70), channel_id=1, source_target_pairs={{0,16},{2,18},{4,20},{6,22},{8,24},{10,26},{12,28},{14,30},{16,0},... | collective-permute-start | bytes 368648 | tf_op jit(solution)/shard_map/ppermute | solution.py:451
  65.7 1.5 %collective-permute-start.18 = (bf16[32,1920]{1,0:T(8,128)(2,1)S(1)}, bf16[32,1920]{1,0:T(8,128)(2,1)S(1)}, u32[]{:S(2)}, u32[]{:S(2)}) collective-permute-start(bf16[32,1920]{1,0:T(8,128)(2,1)S(1)} %get-tuple-element.71), channel_id=1, source_target_pairs={{0,24},{2,26},{4,28},{6,30},{8,16},{10,18},{12,20},{14,22},{16,8},... | collective-permute-start | bytes 368648 | tf_op jit(solution)/shard_map/ppermute | solution.py:451
  67.1 2.2 %collective-permute-done.16.refs_1_ = bf16[32,1920]{1,0:T(8,128)(2,1)S(1)} collective-permute-done((bf16[32,1920]{1,0:T(8,128)(2,1)S(1)}, bf16[32,1920]{1,0:T(8,128)(2,1)S(1)}, u32[]{:S(2)}, u32[]{:S(2)}) %collective-permute-start.16) | collective-permute-done | bytes 122912 | tf_op jit(solution)/shard_map/ppermute | solution.py:451
  69.4 7.6 %collective-permute-done.17.refs_2_ = bf16[32,1920]{1,0:T(8,128)(2,1)S(1)} collective-permute-done((bf16[32,1920]{1,0:T(8,128)(2,1)S(1)}, bf16[32,1920]{1,0:T(8,128)(2,1)S(1)}, u32[]{:S(2)}, u32[]{:S(2)}) %collective-permute-start.17) | collective-permute-done | bytes 122912 | tf_op jit(solution)/shard_map/ppermute | solution.py:451
  77.0 0.0 collective-permute-done.18.refs_3_
  77.0 0.3 combine.1
  77.3 1.6 %collective-permute-start.19 = (bf16[40,1920]{1,0:T(8,128)(2,1)S(1)}, bf16[40,1920]{1,0:T(8,128)(2,1)S(1)}, u32[]{:S(2)}, u32[]{:S(2)}) collective-permute-start(bf16[40,1920]{1,0:T(8,128)(2,1)S(1)} %get-tuple-element.73), channel_id=1, source_target_pairs={{0,1},{1,0},{2,3},{3,2},{4,5},{5,4},{6,7},{7,6},{8,9},{9,8},{10,11... | collective-permute-start | bytes 460808 | tf_op jit(solution)/shard_map/ppermute | solution.py:447
  78.8 1.4 %collective-permute-start.21 = (bf16[16,1920]{1,0:T(8,128)(2,1)S(1)}, bf16[16,1920]{1,0:T(8,128)(2,1)S(1)}, u32[]{:S(2)}, u32[]{:S(2)}) collective-permute-start(bf16[16,1920]{1,0:T(8,128)(2,1)S(1)} %get-tuple-element.74), channel_id=1, source_target_pairs={{0,5},{1,4},{2,7},{3,6},{4,1},{5,0},{6,3},{7,2},{8,13},{9,12},{10,... | collective-permute-start | bytes 184328 | tf_op jit(solution)/shard_map/ppermute | solution.py:447
  80.3 0.5 collective-permute-start.20
  80.8 3.1 %collective-permute-done.21.xy_ref = bf16[16,1920]{1,0:T(8,128)(2,1)S(1)} collective-permute-done((bf16[16,1920]{1,0:T(8,128)(2,1)S(1)}, bf16[16,1920]{1,0:T(8,128)(2,1)S(1)}, u32[]{:S(2)}, u32[]{:S(2)}) %collective-permute-start.21) | collective-permute-done | bytes 61472 | tf_op jit(solution)/shard_map/ppermute | solution.py:447
  84.0 0.5 collective-permute-done.20.x_ref
  84.5 0.0 collective-permute-done.19.y_ref
  84.5 0.0 copy-done.6
  84.5 1.4 %finish.1 = (bf16[96,1792]{1,0:T(8,128)(2,1)}, f32[2,96]{1,0:T(2,128)}) custom-call(f32[40,1920]{1,0:T(8,128)S(1)} %get-tuple-element.72.own_ref, bf16[40,1920]{1,0:T(8,128)(2,1)S(1)} %collective-permute-done.19.y_ref, bf16[16,1920]{1,0:T(8,128)(2,1)S(1)} %collective-permute-done.20.x_ref, bf16[16,1920]{1,0:T(8,128)(2,1)S(1)} %collective-permute-done.21.xy_ref, ...), custom_call_target="tpu_custom_call" | custom-call | flops 1024 | bytes 1024 | tf_op jit(solution)/shard_map/finish/pallas_call | solution.py:400
  86.0 0.0 collective-permute-done.22.c_ref
  86.0 0.9 hot_sum.1
  (4 shorter events, 0.0 us)
Async XLA Ops:
  3.8 14.2 %collective-permute-start.4 = (bf16[120,1792]{1,0:T(8,128)(2,1)}, bf16[120,1792]{1,0:T(8,128)(2,1)S(1)}, u32[]{:S(2)}, u32[]{:S(2)}) collective-permute-start(bf16[120,1792]{1,0:T(8,128)(2,1)} %get-tuple-element.52.refs_8_), channel_id=1, source_target_pairs={{0,1},{1,0},{2,3},{3,2},{4,5},{5,4},{6,7},{7,6},{8,9},{9,8},{10,11... | collective-permute-start | bytes 1290248 | tf_op jit(solution)/shard_map/ppermute | solution.py:447
  6.7 11.2 %collective-permute-start = (bf16[64,1920]{1,0:T(8,128)(2,1)}, bf16[64,1920]{1,0:T(8,128)(2,1)S(1)}, u32[]{:S(2)}, u32[]{:S(2)}) collective-permute-start(bf16[64,1920]{1,0:T(8,128)(2,1)} %get-tuple-element.49), channel_id=1, source_target_pairs={{0,8},{2,10},{4,12},{6,14},{8,0},{10,2},{12,4},{14,6},{16,24},{18,... | collective-permute-start | bytes 737288 | tf_op jit(solution)/shard_map/ppermute | solution.py:451
  8.3 22.5 %collective-permute-start.9 = (bf16[120,1792]{1,0:T(8,128)(2,1)}, bf16[120,1792]{1,0:T(8,128)(2,1)S(1)}, u32[]{:S(2)}, u32[]{:S(2)}) collective-permute-start(bf16[120,1792]{1,0:T(8,128)(2,1)} %get-tuple-element.52.refs_8_), channel_id=1, source_target_pairs={{0,4},{1,5},{2,6},{3,7},{4,0},{5,1},{6,2},{7,3},{8,12},{9,13},{10,... | collective-permute-start | bytes 1290248 | tf_op jit(solution)/shard_map/ppermute | solution.py:447
  9.8 20.5 %collective-permute-start.1 = (bf16[64,1920]{1,0:T(8,128)(2,1)}, bf16[64,1920]{1,0:T(8,128)(2,1)S(1)}, u32[]{:S(2)}, u32[]{:S(2)}) collective-permute-start(bf16[64,1920]{1,0:T(8,128)(2,1)} %get-tuple-element.50), channel_id=1, source_target_pairs={{0,16},{2,18},{4,20},{6,22},{8,24},{10,26},{12,28},{14,30},{16,0},... | collective-permute-start | bytes 737288 | tf_op jit(solution)/shard_map/ppermute | solution.py:451
  12.4 18.0 %collective-permute-start.2 = (bf16[64,1920]{1,0:T(8,128)(2,1)}, bf16[64,1920]{1,0:T(8,128)(2,1)S(1)}, u32[]{:S(2)}, u32[]{:S(2)}) collective-permute-start(bf16[64,1920]{1,0:T(8,128)(2,1)} %get-tuple-element.51), channel_id=1, source_target_pairs={{0,24},{2,26},{4,28},{6,30},{8,16},{10,18},{12,20},{14,22},{16,8},... | collective-permute-start | bytes 737288 | tf_op jit(solution)/shard_map/ppermute | solution.py:451
  17.9 14.8 %collective-permute-start.10 = (bf16[120,1792]{1,0:T(8,128)(2,1)S(1)}, bf16[120,1792]{1,0:T(8,128)(2,1)S(1)}, u32[]{:S(2)}, u32[]{:S(2)}) collective-permute-start(bf16[120,1792]{1,0:T(8,128)(2,1)S(1)} %collective-permute-done.4.refs_10_), channel_id=1, source_target_pairs={{0,4},{1,5},{2,6},{3,7},{4,0},{5,1},{6,2},{7,3},{8,12},{9,13},{10,... | collective-permute-start | bytes 1290248 | tf_op jit(solution)/shard_map/ppermute | solution.py:447
  19.9 11.0 %collective-permute-start.6 = (bf16[64,1920]{1,0:T(8,128)(2,1)S(1)}, bf16[64,1920]{1,0:T(8,128)(2,1)S(1)}, u32[]{:S(2)}, u32[]{:S(2)}) collective-permute-start(bf16[64,1920]{1,0:T(8,128)(2,1)S(1)} %collective-permute-done.refs_1_), channel_id=1, source_target_pairs={{0,2},{2,0},{4,6},{6,4},{8,10},{10,8},{12,14},{14,12},{16,18},{18,... | collective-permute-start | bytes 737288 | tf_op jit(solution)/shard_map/ppermute | solution.py:454
  30.3 1.5 %collective-permute-start.7 = (bf16[64,1920]{1,0:T(8,128)(2,1)S(1)}, bf16[64,1920]{1,0:T(8,128)(2,1)S(1)}, u32[]{:S(2)}, u32[]{:S(2)}) collective-permute-start(bf16[64,1920]{1,0:T(8,128)(2,1)S(1)} %collective-permute-done.1.refs_2_), channel_id=1, source_target_pairs={{0,2},{2,0},{4,6},{6,4},{8,10},{10,8},{12,14},{14,12},{16,18},{18,... | collective-permute-start | bytes 737288 | tf_op jit(solution)/shard_map/ppermute | solution.py:454
  30.3 1.9 %collective-permute-start.8 = (bf16[64,1920]{1,0:T(8,128)(2,1)S(1)}, bf16[64,1920]{1,0:T(8,128)(2,1)S(1)}, u32[]{:S(2)}, u32[]{:S(2)}) collective-permute-start(bf16[64,1920]{1,0:T(8,128)(2,1)S(1)} %collective-permute-done.2.refs_3_), channel_id=1, source_target_pairs={{0,2},{2,0},{4,6},{6,4},{8,10},{10,8},{12,14},{14,12},{16,18},{18,... | collective-permute-start | bytes 737288 | tf_op jit(solution)/shard_map/ppermute | solution.py:454
  30.8 1.9 %collective-permute-start.5 = (bf16[64,1920]{1,0:T(8,128)(2,1)}, bf16[64,1920]{1,0:T(8,128)(2,1)S(1)}, u32[]{:S(2)}, u32[]{:S(2)}) collective-permute-start(bf16[64,1920]{1,0:T(8,128)(2,1)} %get-tuple-element.53.refs_0_), channel_id=1, source_target_pairs={{0,2},{2,0},{4,6},{6,4},{8,10},{10,8},{12,14},{14,12},{16,18},{18,... | collective-permute-start | bytes 737288 | tf_op jit(solution)/shard_map/ppermute | solution.py:454
  32.8 0.9 %copy-start = (bf16[64,1920]{1,0:T(8,128)(2,1)S(1)}, bf16[64,1920]{1,0:T(8,128)(2,1)}, u32[]{:S(2)}) copy-start(bf16[64,1920]{1,0:T(8,128)(2,1)} %get-tuple-element.53.refs_0_) | copy-start | bytes 737284
  33.7 1.0 %copy-start.5 = (bf16[120,1792]{1,0:T(8,128)(2,1)S(1)}, bf16[120,1792]{1,0:T(8,128)(2,1)}, u32[]{:S(2)}) copy-start(bf16[120,1792]{1,0:T(8,128)(2,1)} %get-tuple-element.52.refs_8_) | copy-start | bytes 1290244
  34.7 18.7 %copy-start.2 = (bf16[1,320,1792]{2,1,0:T(8,128)(2,1)S(1)}, bf16[1,320,1792]{2,1,0:T(8,128)(2,1)}, u32[]{:S(2)}) copy-start(bf16[1,320,1792]{2,1,0:T(8,128)(2,1)} %refs_10_.1) | copy-start | bytes 3440644
  34.7 18.7 %copy-start.3 = (bf16[1,320,1792]{2,1,0:T(8,128)(2,1)S(1)}, bf16[1,320,1792]{2,1,0:T(8,128)(2,1)}, u32[]{:S(2)}) copy-start(bf16[1,320,1792]{2,1,0:T(8,128)(2,1)} %refs_11_.1) | copy-start | bytes 3440644
  34.7 18.7 %copy-start.4 = (bf16[1,320,1792]{2,1,0:T(8,128)(2,1)S(1)}, bf16[1,320,1792]{2,1,0:T(8,128)(2,1)}, u32[]{:S(2)}) copy-start(bf16[1,320,1792]{2,1,0:T(8,128)(2,1)} %refs_12_.1) | copy-start | bytes 3440644
  37.4 16.0 %copy-start.1 = (bf16[64,1920]{1,0:T(8,128)(2,1)S(1)}, bf16[64,1920]{1,0:T(8,128)(2,1)}, u32[]{:S(2)}) copy-start(bf16[64,1920]{1,0:T(8,128)(2,1)} %get-tuple-element.53.refs_0_) | copy-start | bytes 737284
  37.4 23.2 %collective-permute-start.14 = (bf16[120,1792]{1,0:T(8,128)(2,1)S(1)}, bf16[120,1792]{1,0:T(8,128)(2,1)S(1)}, u32[]{:S(2)}, u32[]{:S(2)}) collective-permute-start(bf16[120,1792]{1,0:T(8,128)(2,1)S(1)} %get-tuple-element.65), channel_id=1, source_target_pairs={{0,4},{1,5},{2,6},{3,7},{4,0},{5,1},{6,2},{7,3},{8,12},{9,13},{10,... | collective-permute-start | bytes 1290248 | tf_op jit(solution)/shard_map/ppermute | solution.py:447
  38.0 22.6 %collective-permute-start.15 = (bf16[120,1792]{1,0:T(8,128)(2,1)S(1)}, bf16[120,1792]{1,0:T(8,128)(2,1)S(1)}, u32[]{:S(2)}, u32[]{:S(2)}) collective-permute-start(bf16[120,1792]{1,0:T(8,128)(2,1)S(1)} %get-tuple-element.66), channel_id=1, source_target_pairs={{0,1},{1,0},{2,3},{3,2},{4,5},{5,4},{6,7},{7,6},{8,9},{9,8},{10,11... | collective-permute-start | bytes 1290248 | tf_op jit(solution)/shard_map/ppermute | solution.py:447
  38.5 13.5 %collective-permute-start.3 = (bf16[32,1920]{1,0:T(8,128)(2,1)S(1)}, bf16[32,1920]{1,0:T(8,128)(2,1)S(1)}, u32[]{:S(2)}, u32[]{:S(2)}) collective-permute-start(bf16[32,1920]{1,0:T(8,128)(2,1)S(1)} %cold_away.1), channel_id=1, source_target_pairs={{0,4},{1,5},{2,6},{3,7},{4,0},{5,1},{6,2},{7,3},{8,12},{9,13},{10,... | collective-permute-start | bytes 368648 | tf_op jit(solution)/shard_map/ppermute | solution.py:447
  40.1 20.2 %collective-permute-start.11 = (bf16[96,1920]{1,0:T(8,128)(2,1)S(1)}, bf16[96,1920]{1,0:T(8,128)(2,1)S(1)}, u32[]{:S(2)}, u32[]{:S(2)}) collective-permute-start(bf16[96,1920]{1,0:T(8,128)(2,1)S(1)} %get-tuple-element.57), channel_id=1, source_target_pairs={{0,2},{2,0},{4,6},{6,4},{8,10},{10,8},{12,14},{14,12},{16,18},{18,... | collective-permute-start | bytes 1105928 | tf_op jit(solution)/shard_map/ppermute | solution.py:454
  52.1 1.3 %collective-permute-start.12 = (bf16[32,1920]{1,0:T(8,128)(2,1)S(1)}, bf16[32,1920]{1,0:T(8,128)(2,1)S(1)}, u32[]{:S(2)}, u32[]{:S(2)}) collective-permute-start(bf16[32,1920]{1,0:T(8,128)(2,1)S(1)} %collective-permute-done.3.refs_8_), channel_id=1, source_target_pairs={{0,2},{2,0},{4,6},{6,4},{8,10},{10,8},{12,14},{14,12},{16,18},{18,... | collective-permute-start | bytes 368648 | tf_op jit(solution)/shard_map/ppermute | solution.py:454
  58.9 25.6 %copy-start.6 = (s32[2,192]{1,0:T(2,128)S(1)}, s32[2,192]{1,0:T(2,128)}, u32[]{:S(2)}) copy-start(s32[2,192]{1,0:T(2,128)} %get-tuple-element.75.pos_ref) | copy-start | bytes 4612
  58.9 1.4 %collective-permute-start.13 = (bf16[32,1920]{1,0:T(8,128)(2,1)S(1)}, bf16[32,1920]{1,0:T(8,128)(2,1)S(1)}, u32[]{:S(2)}, u32[]{:S(2)}) collective-permute-start(bf16[32,1920]{1,0:T(8,128)(2,1)S(1)} %get-tuple-element.60), channel_id=1, source_target_pairs={{0,2},{2,0},{4,6},{6,4},{8,10},{10,8},{12,14},{14,12},{16,18},{18,... | collective-permute-start | bytes 368648 | tf_op jit(solution)/shard_map/ppermute | solution.py:454
  60.6 25.3 %collective-permute-start.22 = (bf16[120,1792]{1,0:T(8,128)(2,1)S(1)}, bf16[120,1792]{1,0:T(8,128)(2,1)S(1)}, u32[]{:S(2)}, u32[]{:S(2)}) collective-permute-start(bf16[120,1792]{1,0:T(8,128)(2,1)S(1)} %get-tuple-element.84), channel_id=1, source_target_pairs={{0,5},{1,4},{2,7},{3,6},{4,1},{5,0},{6,3},{7,2},{8,13},{9,12},{10,... | collective-permute-start | bytes 1290248 | tf_op jit(solution)/shard_map/ppermute | solution.py:447
  61.2 8.2 %collective-permute-start.16 = (bf16[32,1920]{1,0:T(8,128)(2,1)S(1)}, bf16[32,1920]{1,0:T(8,128)(2,1)S(1)}, u32[]{:S(2)}, u32[]{:S(2)}) collective-permute-start(bf16[32,1920]{1,0:T(8,128)(2,1)S(1)} %get-tuple-element.69), channel_id=1, source_target_pairs={{0,8},{2,10},{4,12},{6,14},{8,0},{10,2},{12,4},{14,6},{16,24},{18,... | collective-permute-start | bytes 368648 | tf_op jit(solution)/shard_map/ppermute | solution.py:451
  64.7 12.3 %collective-permute-start.17 = (bf16[32,1920]{1,0:T(8,128)(2,1)S(1)}, bf16[32,1920]{1,0:T(8,128)(2,1)S(1)}, u32[]{:S(2)}, u32[]{:S(2)}) collective-permute-start(bf16[32,1920]{1,0:T(8,128)(2,1)S(1)} %get-tuple-element.70), channel_id=1, source_target_pairs={{0,16},{2,18},{4,20},{6,22},{8,24},{10,26},{12,28},{14,30},{16,0},... | collective-permute-start | bytes 368648 | tf_op jit(solution)/shard_map/ppermute | solution.py:451
  65.7 11.3 %collective-permute-start.18 = (bf16[32,1920]{1,0:T(8,128)(2,1)S(1)}, bf16[32,1920]{1,0:T(8,128)(2,1)S(1)}, u32[]{:S(2)}, u32[]{:S(2)}) collective-permute-start(bf16[32,1920]{1,0:T(8,128)(2,1)S(1)} %get-tuple-element.71), channel_id=1, source_target_pairs={{0,24},{2,26},{4,28},{6,30},{8,16},{10,18},{12,20},{14,22},{16,8},... | collective-permute-start | bytes 368648 | tf_op jit(solution)/shard_map/ppermute | solution.py:451
  77.3 7.2 %collective-permute-start.19 = (bf16[40,1920]{1,0:T(8,128)(2,1)S(1)}, bf16[40,1920]{1,0:T(8,128)(2,1)S(1)}, u32[]{:S(2)}, u32[]{:S(2)}) collective-permute-start(bf16[40,1920]{1,0:T(8,128)(2,1)S(1)} %get-tuple-element.73), channel_id=1, source_target_pairs={{0,1},{1,0},{2,3},{3,2},{4,5},{5,4},{6,7},{7,6},{8,9},{9,8},{10,11... | collective-permute-start | bytes 460808 | tf_op jit(solution)/shard_map/ppermute | solution.py:447
  78.8 5.1 %collective-permute-start.21 = (bf16[16,1920]{1,0:T(8,128)(2,1)S(1)}, bf16[16,1920]{1,0:T(8,128)(2,1)S(1)}, u32[]{:S(2)}, u32[]{:S(2)}) collective-permute-start(bf16[16,1920]{1,0:T(8,128)(2,1)S(1)} %get-tuple-element.74), channel_id=1, source_target_pairs={{0,5},{1,4},{2,7},{3,6},{4,1},{5,0},{6,3},{7,2},{8,13},{9,12},{10,... | collective-permute-start | bytes 184328 | tf_op jit(solution)/shard_map/ppermute | solution.py:447
  80.3 4.2 %collective-permute-start.20 = (bf16[16,1920]{1,0:T(8,128)(2,1)S(1)}, bf16[16,1920]{1,0:T(8,128)(2,1)S(1)}, u32[]{:S(2)}, u32[]{:S(2)}) collective-permute-start(bf16[16,1920]{1,0:T(8,128)(2,1)S(1)} %get-tuple-element.74), channel_id=1, source_target_pairs={{0,4},{1,5},{2,6},{3,7},{4,0},{5,1},{6,2},{7,3},{8,12},{9,13},{10,... | collective-permute-start | bytes 184328 | tf_op jit(solution)/shard_map/ppermute | solution.py:447
where the time goes:
time: 87 us; the launch traced here: 86.8 us
  waiting for transfers between devices  45.7 us (53%)
  starting transfers between devices  24.3 us (28%)
  Pallas kernels  14.1 us (16%)
  local copies, waits for them, and re-layouts  1.98 us (2%)
    ppermute x6, waiting for transfers between devices, along_z(): return lax.ppermute(value, 'dp', perm)  25.6 us
    ppermute x10, waiting for transfers between devices, swap(): return lax.ppermute(value, ('dp', 'pair'), perm)  15.7 us
    pallas_call x8, Pallas kernels, run(): pl.pallas_call(kernel, out_shape=outs, in_specs=[pl.BlockSpec(memory_spac...  14.1 us
    ppermute x10, starting transfers between devices, swap(): return lax.ppermute(value, ('dp', 'pair'), perm)  13.2 us
    ppermute x6, starting transfers between devices, along_z(): return lax.ppermute(value, 'dp', perm)  10.4 us
    ppermute x7, waiting for transfers between devices, other_core(): return lax.ppermute(value, 'dp', [(i, i ^ 1) for i in range(count)])  4.37 us
    unnamed x14, local copies, waits for them, and re-layouts  1.98 us
  transfers between devices with their start and end apart: 23, of which 12 were waited for; matrix products, arithmetic and copies ran while one was open for 0% of the time, Pallas kernels for 9%

commit v1 on v0

--- a/solution.py
+++ b/solution.py
@@ -450,6 +450,11 @@
         perm = [(i, 4 * ((i // 4) ^ k) + i % 4) for i in range(count)]
         return lax.ppermute(value, "dp", perm)
 
+    def all_along_z(values):
+        order = sorted(range(1, z_count), key=lambda k: (k == 1, k))
+        got = {k: along_z(values[k], k) for k in order}
+        return [values[0]] + [got[k] for k in range(1, z_count)]
+
     def other_core(value):
         return lax.ppermute(value, "dp", [(i, i ^ 1) for i in range(count)])
 
@@ -476,7 +481,7 @@
         *hot_weights,
     )
 
-    chunks = [messages[0]] + [along_z(messages[k], k) for k in range(1, z_count)]
+    chunks = all_along_z(messages)
     by_pair = swap(hot_own, 2)
     by_x = swap(hot_own, 1)
     first_out, by_pair_out, _ = lax.optimization_barrier((messages[0], by_pair, chunks[1]))
@@ -533,9 +538,10 @@
     parts = call(
         add_kernel, [shape(part, F32)] + [shape(part, BF)] * (z_count - 1), "add_cores"
     )(hot_dx, hot_got, cold_own, cold_got)
-    got_x, got_y = swap(sent_terms[0], 1), swap(sent_terms[1], 2)
+    term_x, _ = lax.optimization_barrier((sent_terms[0], cold_mine))
+    got_x, got_y = swap(term_x, 1), swap(sent_terms[1], 2)
     *parts, got_x, got_y, last_term = lax.optimization_barrier((*parts, got_x, got_y, sent_terms[2]))
-    parts = [parts[0]] + [along_z(parts[k], k) for k in range(1, z_count)]
+    parts = all_along_z(parts)
     got_terms = [got_x, got_y, swap(last_term, 3)]
 
     cold_back = z_count * CAP

time: 87 us -> 75.1 us (0.86)
  waiting for transfers between devices: 45.7 us -> 34.9 us
    ppermute x10, waiting for transfers between devices: 15.7 us -> 6.47 us  [swap(): return lax.ppermute(value, ('dp', 'pair'), perm)]
    ppermute x7, waiting for transfers between devices: 4.37 us -> 2.8 us  [other_core(): return lax.ppermute(value, 'dp', [(i, i ^ 1) for i in range(count)])]
  transfers between devices with their start and end apart: 23 -> 23, of which waited for: 12 -> 12; matrix products, arithmetic and copies ran while one was open for 0% -> 0% of each run, Pallas kernels for 9% -> 14%
where the time goes in v1:
time: 75.1 us; the launch traced here: 74.9 us
  waiting for transfers between devices  34.9 us (46%)
  starting transfers between devices  24 us (32%)
  Pallas kernels  14.1 us (19%)
  local copies, waits for them, and re-layouts  1.21 us (2%)
    ppermute x6, waiting for transfers between devices, along_z(): return lax.ppermute(value, 'dp', perm)  25.6 us
    pallas_call x8, Pallas kernels, run(): pl.pallas_call(kernel, out_shape=outs, in_specs=[pl.BlockSpec(memory_spac...  14.1 us
    ppermute x10, starting transfers between devices, swap(): return lax.ppermute(value, ('dp', 'pair'), perm)  13 us
    ppermute x6, starting transfers between devices, along_z(): return lax.ppermute(value, 'dp', perm)  9.69 us
    ppermute x10, waiting for transfers between devices, swap(): return lax.ppermute(value, ('dp', 'pair'), perm)  6.47 us
    ppermute x7, waiting for transfers between devices, other_core(): return lax.ppermute(value, 'dp', [(i, i ^ 1) for i in range(count)])  2.8 us
  transfers between devices with their start and end apart: 23, of which 12 were waited for; matrix products, arithmetic and copies ran while one was open for 0% of the time, Pallas kernels for 14%

profile of v1, /device:TPU:0, one launch (start us, length us, event | category | flops | bytes accessed | tf_op | source)
XLA Modules:
  0.0 74.9 jit_solution(12264158063198670401)
XLA Ops:
  0.6 3.1 %dispatch.1 = (s32[2,192]{1,0:T(2,128)}, bf16[120,1792]{1,0:T(8,128)(2,1)}, bf16[64,1920]{1,0:T(8,128)(2,1)}, bf16[64,1920]{1,0:T(8,128)(2,1)}, bf16[64,1920]{1,0:T(8,128)(2,1)}, /*index=5*/bf16[64,1920]{1,0:T(8,128)(2,1)}) custom-call(bf16[192,1792]{1,0:T(8,128)(2,1)} %refs_0_.1, bf16[192,1792]{1,0:T(8,128)(2,1)} %refs_1_.1, bf16[2,192]{1,0:T(2,128)(2,1)} %bitcast.6, ...), custom_call_target="tpu_custom_call" | custom-call | flops 1024 | bytes 1024 | tf_op jit(solution)/shard_map/dispatch/pallas_call | solution.py:400
  3.8 3.0 %collective-permute-start.4 = (bf16[120,1792]{1,0:T(8,128)(2,1)}, bf16[120,1792]{1,0:T(8,128)(2,1)S(1)}, u32[]{:S(2)}, u32[]{:S(2)}) collective-permute-start(bf16[120,1792]{1,0:T(8,128)(2,1)} %get-tuple-element.53.refs_8_), channel_id=1, source_target_pairs={{0,1},{1,0},{2,3},{3,2},{4,5},{5,4},{6,7},{7,6},{8,9},{9,8},{10,11... | collective-permute-start | bytes 1290248 | tf_op jit(solution)/shard_map/ppermute | solution.py:447
  6.7 1.6 %collective-permute-start = (bf16[64,1920]{1,0:T(8,128)(2,1)}, bf16[64,1920]{1,0:T(8,128)(2,1)S(1)}, u32[]{:S(2)}, u32[]{:S(2)}) collective-permute-start(bf16[64,1920]{1,0:T(8,128)(2,1)} %get-tuple-element.50), channel_id=1, source_target_pairs={{0,8},{2,10},{4,12},{6,14},{8,0},{10,2},{12,4},{14,6},{16,24},{18,... | collective-permute-start | bytes 737288 | tf_op jit(solution)/shard_map/ppermute | solution.py:451
  8.3 1.5 %collective-permute-start.9 = (bf16[120,1792]{1,0:T(8,128)(2,1)}, bf16[120,1792]{1,0:T(8,128)(2,1)S(1)}, u32[]{:S(2)}, u32[]{:S(2)}) collective-permute-start(bf16[120,1792]{1,0:T(8,128)(2,1)} %get-tuple-element.53.refs_8_), channel_id=1, source_target_pairs={{0,4},{1,5},{2,6},{3,7},{4,0},{5,1},{6,2},{7,3},{8,12},{9,13},{10,... | collective-permute-start | bytes 1290248 | tf_op jit(solution)/shard_map/ppermute | solution.py:447
  9.8 2.6 %collective-permute-start.1 = (bf16[64,1920]{1,0:T(8,128)(2,1)}, bf16[64,1920]{1,0:T(8,128)(2,1)S(1)}, u32[]{:S(2)}, u32[]{:S(2)}) collective-permute-start(bf16[64,1920]{1,0:T(8,128)(2,1)} %get-tuple-element.51), channel_id=1, source_target_pairs={{0,16},{2,18},{4,20},{6,22},{8,24},{10,26},{12,28},{14,30},{16,0},... | collective-permute-start | bytes 737288 | tf_op jit(solution)/shard_map/ppermute | solution.py:451
  12.4 0.2 collective-permute-start.2
  12.6 5.3 %collective-permute-done.refs_1_ = bf16[64,1920]{1,0:T(8,128)(2,1)S(1)} collective-permute-done((bf16[64,1920]{1,0:T(8,128)(2,1)}, bf16[64,1920]{1,0:T(8,128)(2,1)S(1)}, u32[]{:S(2)}, u32[]{:S(2)}) %collective-permute-start) | collective-permute-done | bytes 245792 | tf_op jit(solution)/shard_map/ppermute | solution.py:451
  17.9 0.0 collective-permute-done.4.refs_10_
  17.9 2.0 %collective-permute-start.10 = (bf16[120,1792]{1,0:T(8,128)(2,1)S(1)}, bf16[120,1792]{1,0:T(8,128)(2,1)S(1)}, u32[]{:S(2)}, u32[]{:S(2)}) collective-permute-start(bf16[120,1792]{1,0:T(8,128)(2,1)S(1)} %collective-permute-done.4.refs_10_), channel_id=1, source_target_pairs={{0,4},{1,5},{2,6},{3,7},{4,0},{5,1},{6,2},{7,3},{8,12},{9,13},{10,... | collective-permute-start | bytes 1290248 | tf_op jit(solution)/shard_map/ppermute | solution.py:447
  19.9 0.0 collective-permute-start.6
  19.9 10.4 %collective-permute-done.1.refs_2_ = bf16[64,1920]{1,0:T(8,128)(2,1)S(1)} collective-permute-done((bf16[64,1920]{1,0:T(8,128)(2,1)}, bf16[64,1920]{1,0:T(8,128)(2,1)S(1)}, u32[]{:S(2)}, u32[]{:S(2)}) %collective-permute-start.1) | collective-permute-done | bytes 245792 | tf_op jit(solution)/shard_map/ppermute | solution.py:451
  30.3 0.0 collective-permute-start.7
  30.3 0.0 collective-permute-done.2.refs_3_
  30.3 0.5 collective-permute-start.8
  30.8 0.0 collective-permute-done.9.refs_9_
  30.8 0.1 collective-permute-start.5
  30.9 0.9 %copy-done = bf16[64,1920]{1,0:T(8,128)(2,1)S(1)} copy-done((bf16[64,1920]{1,0:T(8,128)(2,1)S(1)}, bf16[64,1920]{1,0:T(8,128)(2,1)}, u32[]{:S(2)}) %copy-start) | copy-done | bytes 245784
  31.9 0.0 copy-start.2
  31.9 0.0 copy-start.3
  31.9 0.0 copy-start.4
  31.9 0.0 collective-permute-done.6.refs_5_
  31.9 0.6 collective-permute-start.3
  32.5 0.0 collective-permute-done.7.refs_6_
  32.5 0.0 collective-permute-done.8.refs_7_
  32.5 0.2 collective-permute-done.5.refs_4_
  32.8 0.0 collective-permute-done.10.refs_11_
  32.8 0.0 copy-done.1
  32.8 0.2 copy-done.5
  33.0 2.7 %hot.1 = (f32[96,1920]{1,0:T(8,128)S(1)}, bf16[96,1920]{1,0:T(8,128)(2,1)S(1)}, f32[120,1792]{1,0:T(8,128)S(1)}, bf16[120,1792]{1,0:T(8,128)(2,1)S(1)}, bf16[120...) custom-call(bf16[64,1920]{1,0:T(8,128)(2,1)S(1)} %copy-done.1, bf16[64,1920]{1,0:T(8,128)(2,1)S(1)} %collective-permute-done.refs_1_, ...), custom_call_target="tpu_custom_call" | custom-call | flops 1024 | bytes 1024 | tf_op jit(solution)/shard_map/hot/pallas_call | solution.py:400
  35.7 2.0 %collective-permute-done.3.refs_8_ = bf16[32,1920]{1,0:T(8,128)(2,1)S(1)} collective-permute-done((bf16[32,1920]{1,0:T(8,128)(2,1)S(1)}, bf16[32,1920]{1,0:T(8,128)(2,1)S(1)}, u32[]{:S(2)}, u32[]{:S(2)}) %collective-permute-start.3) | collective-permute-done | bytes 122912 | tf_op jit(solution)/shard_map/ppermute | solution.py:447
  37.7 0.5 collective-permute-start.14
  38.2 0.5 collective-permute-start.15
  38.7 0.0 collective-permute-start.11
  38.7 0.5 collective-permute-start.12
  39.2 1.4 %collective-permute-done.12.refs_9_ = bf16[32,1920]{1,0:T(8,128)(2,1)S(1)} collective-permute-done((bf16[32,1920]{1,0:T(8,128)(2,1)S(1)}, bf16[32,1920]{1,0:T(8,128)(2,1)S(1)}, u32[]{:S(2)}, u32[]{:S(2)}) %collective-permute-start.12) | collective-permute-done | bytes 122912 | tf_op jit(solution)/shard_map/ppermute | solution.py:459
  40.6 0.0 copy-done.2
  40.6 0.0 copy-done.3
  40.6 0.0 copy-done.4
  40.6 5.5 %cold.1 = (f32[32,1920]{1,0:T(8,128)S(1)}, bf16[32,1920]{1,0:T(8,128)(2,1)S(1)}, bf16[1,320,1792]{2,1,0:T(8,128)(2,1)}, bf16[1,320,1792]{2,1,0:T(8,128)(2,1)}, bf16[1,320,1792]{2,1,0:T(8,128)(2,1)}) custom-call(bf16[64,1920]{1,0:T(8,128)(2,1)S(1)} %copy-done.1, bf16[64,1920]{1,0:T(8,128)(2,1)S(1)} %collective-permute-done.refs_1_, ...), custom_call_target="tpu_custom_call" | custom-call | flops 1024 | bytes 1024 | tf_op jit(solution)/shard_map/cold/pallas_call | solution.py:400
  46.0 0.0 copy-start.6
  46.0 0.2 collective-permute-start.13
  46.2 1.2 %collective-permute-done.13.cold_got_ref = bf16[32,1920]{1,0:T(8,128)(2,1)S(1)} collective-permute-done((bf16[32,1920]{1,0:T(8,128)(2,1)S(1)}, bf16[32,1920]{1,0:T(8,128)(2,1)S(1)}, u32[]{:S(2)}, u32[]{:S(2)}) %collective-permute-start.13) | collective-permute-done | bytes 122912 | tf_op jit(solution)/shard_map/ppermute | solution.py:459
  47.5 0.0 collective-permute-done.11.hot_got_ref
  47.5 0.3 add_cores.1
  47.7 1.4 %collective-permute-done.14.a_ref = bf16[120,1792]{1,0:T(8,128)(2,1)S(1)} collective-permute-done((bf16[120,1792]{1,0:T(8,128)(2,1)S(1)}, bf16[120,1792]{1,0:T(8,128)(2,1)S(1)}, u32[]{:S(2)}, u32[]{:S(2)}) %collective-permute-start.14) | collective-permute-done | bytes 430112 | tf_op jit(solution)/shard_map/ppermute | solution.py:447
  49.1 0.3 collective-permute-done.15.b_ref
  49.4 1.4 %collective-permute-start.22 = (bf16[120,1792]{1,0:T(8,128)(2,1)S(1)}, bf16[120,1792]{1,0:T(8,128)(2,1)S(1)}, u32[]{:S(2)}, u32[]{:S(2)}) collective-permute-start(bf16[120,1792]{1,0:T(8,128)(2,1)S(1)} %get-tuple-element.86), channel_id=1, source_target_pairs={{0,5},{1,4},{2,7},{3,6},{4,1},{5,0},{6,3},{7,2},{8,13},{9,12},{10,... | collective-permute-start | bytes 1290248 | tf_op jit(solution)/shard_map/ppermute | solution.py:447
  50.8 2.8 %collective-permute-start.16 = (bf16[32,1920]{1,0:T(8,128)(2,1)S(1)}, bf16[32,1920]{1,0:T(8,128)(2,1)S(1)}, u32[]{:S(2)}, u32[]{:S(2)}) collective-permute-start(bf16[32,1920]{1,0:T(8,128)(2,1)S(1)} %get-tuple-element.71), channel_id=1, source_target_pairs={{0,8},{2,10},{4,12},{6,14},{8,0},{10,2},{12,4},{14,6},{16,24},{18,... | collective-permute-start | bytes 368648 | tf_op jit(solution)/shard_map/ppermute | solution.py:451
  53.6 1.0 %collective-permute-start.17 = (bf16[32,1920]{1,0:T(8,128)(2,1)S(1)}, bf16[32,1920]{1,0:T(8,128)(2,1)S(1)}, u32[]{:S(2)}, u32[]{:S(2)}) collective-permute-start(bf16[32,1920]{1,0:T(8,128)(2,1)S(1)} %get-tuple-element.72), channel_id=1, source_target_pairs={{0,16},{2,18},{4,20},{6,22},{8,24},{10,26},{12,28},{14,30},{16,0},... | collective-permute-start | bytes 368648 | tf_op jit(solution)/shard_map/ppermute | solution.py:451
  54.6 1.5 %collective-permute-start.18 = (bf16[32,1920]{1,0:T(8,128)(2,1)S(1)}, bf16[32,1920]{1,0:T(8,128)(2,1)S(1)}, u32[]{:S(2)}, u32[]{:S(2)}) collective-permute-start(bf16[32,1920]{1,0:T(8,128)(2,1)S(1)} %get-tuple-element.73), channel_id=1, source_target_pairs={{0,24},{2,26},{4,28},{6,30},{8,16},{10,18},{12,20},{14,22},{16,8},... | collective-permute-start | bytes 368648 | tf_op jit(solution)/shard_map/ppermute | solution.py:451
  56.1 2.2 %collective-permute-done.16.refs_1_ = bf16[32,1920]{1,0:T(8,128)(2,1)S(1)} collective-permute-done((bf16[32,1920]{1,0:T(8,128)(2,1)S(1)}, bf16[32,1920]{1,0:T(8,128)(2,1)S(1)}, u32[]{:S(2)}, u32[]{:S(2)}) %collective-permute-start.16) | collective-permute-done | bytes 122912 | tf_op jit(solution)/shard_map/ppermute | solution.py:451
  58.3 7.7 %collective-permute-done.17.refs_2_ = bf16[32,1920]{1,0:T(8,128)(2,1)S(1)} collective-permute-done((bf16[32,1920]{1,0:T(8,128)(2,1)S(1)}, bf16[32,1920]{1,0:T(8,128)(2,1)S(1)}, u32[]{:S(2)}, u32[]{:S(2)}) %collective-permute-start.17) | collective-permute-done | bytes 122912 | tf_op jit(solution)/shard_map/ppermute | solution.py:451
  66.0 0.0 collective-permute-done.18.refs_3_
  66.0 0.3 combine.1
  66.2 0.5 collective-permute-start.19
  66.8 1.5 %collective-permute-start.21 = (bf16[16,1920]{1,0:T(8,128)(2,1)S(1)}, bf16[16,1920]{1,0:T(8,128)(2,1)S(1)}, u32[]{:S(2)}, u32[]{:S(2)}) collective-permute-start(bf16[16,1920]{1,0:T(8,128)(2,1)S(1)} %get-tuple-element.76), channel_id=1, source_target_pairs={{0,5},{1,4},{2,7},{3,6},{4,1},{5,0},{6,3},{7,2},{8,13},{9,12},{10,... | collective-permute-start | bytes 184328 | tf_op jit(solution)/shard_map/ppermute | solution.py:447
  68.3 1.5 %collective-permute-start.20 = (bf16[16,1920]{1,0:T(8,128)(2,1)S(1)}, bf16[16,1920]{1,0:T(8,128)(2,1)S(1)}, u32[]{:S(2)}, u32[]{:S(2)}) collective-permute-start(bf16[16,1920]{1,0:T(8,128)(2,1)S(1)} %get-tuple-element.76), channel_id=1, source_target_pairs={{0,4},{1,5},{2,6},{3,7},{4,0},{5,1},{6,2},{7,3},{8,12},{9,13},{10,... | collective-permute-start | bytes 184328 | tf_op jit(solution)/shard_map/ppermute | solution.py:447
  69.8 2.2 %collective-permute-done.21.xy_ref = bf16[16,1920]{1,0:T(8,128)(2,1)S(1)} collective-permute-done((bf16[16,1920]{1,0:T(8,128)(2,1)S(1)}, bf16[16,1920]{1,0:T(8,128)(2,1)S(1)}, u32[]{:S(2)}, u32[]{:S(2)}) %collective-permute-start.21) | collective-permute-done | bytes 61472 | tf_op jit(solution)/shard_map/ppermute | solution.py:447
  72.0 0.6 collective-permute-done.20.x_ref
  72.6 0.0 collective-permute-done.19.y_ref
  72.6 0.0 copy-done.6
  72.6 1.4 %finish.1 = (bf16[96,1792]{1,0:T(8,128)(2,1)}, f32[2,96]{1,0:T(2,128)}) custom-call(f32[40,1920]{1,0:T(8,128)S(1)} %get-tuple-element.74.own_ref, bf16[40,1920]{1,0:T(8,128)(2,1)S(1)} %collective-permute-done.19.y_ref, bf16[16,1920]{1,0:T(8,128)(2,1)S(1)} %collective-permute-done.20.x_ref, bf16[16,1920]{1,0:T(8,128)(2,1)S(1)} %collective-permute-done.21.xy_ref, ...), custom_call_target="tpu_custom_call" | custom-call | flops 1024 | bytes 1024 | tf_op jit(solution)/shard_map/finish/pallas_call | solution.py:400
  74.1 0.0 collective-permute-done.22.c_ref
  74.1 0.9 %hot_sum.1 = (bf16[40,1792]{1,0:T(8,128)(2,1)}, bf16[40,1792]{1,0:T(8,128)(2,1)}, bf16[40,1792]{1,0:T(8,128)(2,1)}) custom-call(f32[120,1792]{1,0:T(8,128)S(1)} %get-tuple-element.83.own_ref, bf16[120,1792]{1,0:T(8,128)(2,1)S(1)} %collective-permute-done.14.a_ref, bf16[120,1792]{1,0:T(8,128)(2,1)S(1)} %collective-permute-done.15.b_ref, ...), custom_call_target="tpu_custom_call" | custom-call | flops 1024 | bytes 1024 | tf_op jit(solution)/shard_map/hot_sum/pallas_call | solution.py:400
  (4 shorter events, 0.0 us)
Async XLA Ops:
  3.8 14.2 %collective-permute-start.4 = (bf16[120,1792]{1,0:T(8,128)(2,1)}, bf16[120,1792]{1,0:T(8,128)(2,1)S(1)}, u32[]{:S(2)}, u32[]{:S(2)}) collective-permute-start(bf16[120,1792]{1,0:T(8,128)(2,1)} %get-tuple-element.53.refs_8_), channel_id=1, source_target_pairs={{0,1},{1,0},{2,3},{3,2},{4,5},{5,4},{6,7},{7,6},{8,9},{9,8},{10,11... | collective-permute-start | bytes 1290248 | tf_op jit(solution)/shard_map/ppermute | solution.py:447
  6.7 11.2 %collective-permute-start = (bf16[64,1920]{1,0:T(8,128)(2,1)}, bf16[64,1920]{1,0:T(8,128)(2,1)S(1)}, u32[]{:S(2)}, u32[]{:S(2)}) collective-permute-start(bf16[64,1920]{1,0:T(8,128)(2,1)} %get-tuple-element.50), channel_id=1, source_target_pairs={{0,8},{2,10},{4,12},{6,14},{8,0},{10,2},{12,4},{14,6},{16,24},{18,... | collective-permute-start | bytes 737288 | tf_op jit(solution)/shard_map/ppermute | solution.py:451
  8.3 22.5 %collective-permute-start.9 = (bf16[120,1792]{1,0:T(8,128)(2,1)}, bf16[120,1792]{1,0:T(8,128)(2,1)S(1)}, u32[]{:S(2)}, u32[]{:S(2)}) collective-permute-start(bf16[120,1792]{1,0:T(8,128)(2,1)} %get-tuple-element.53.refs_8_), channel_id=1, source_target_pairs={{0,4},{1,5},{2,6},{3,7},{4,0},{5,1},{6,2},{7,3},{8,12},{9,13},{10,... | collective-permute-start | bytes 1290248 | tf_op jit(solution)/shard_map/ppermute | solution.py:447
  9.8 20.5 %collective-permute-start.1 = (bf16[64,1920]{1,0:T(8,128)(2,1)}, bf16[64,1920]{1,0:T(8,128)(2,1)S(1)}, u32[]{:S(2)}, u32[]{:S(2)}) collective-permute-start(bf16[64,1920]{1,0:T(8,128)(2,1)} %get-tuple-element.51), channel_id=1, source_target_pairs={{0,16},{2,18},{4,20},{6,22},{8,24},{10,26},{12,28},{14,30},{16,0},... | collective-permute-start | bytes 737288 | tf_op jit(solution)/shard_map/ppermute | solution.py:451
  12.4 18.0 %collective-permute-start.2 = (bf16[64,1920]{1,0:T(8,128)(2,1)}, bf16[64,1920]{1,0:T(8,128)(2,1)S(1)}, u32[]{:S(2)}, u32[]{:S(2)}) collective-permute-start(bf16[64,1920]{1,0:T(8,128)(2,1)} %get-tuple-element.52), channel_id=1, source_target_pairs={{0,24},{2,26},{4,28},{6,30},{8,16},{10,18},{12,20},{14,22},{16,8},... | collective-permute-start | bytes 737288 | tf_op jit(solution)/shard_map/ppermute | solution.py:451
  17.9 14.8 %collective-permute-start.10 = (bf16[120,1792]{1,0:T(8,128)(2,1)S(1)}, bf16[120,1792]{1,0:T(8,128)(2,1)S(1)}, u32[]{:S(2)}, u32[]{:S(2)}) collective-permute-start(bf16[120,1792]{1,0:T(8,128)(2,1)S(1)} %collective-permute-done.4.refs_10_), channel_id=1, source_target_pairs={{0,4},{1,5},{2,6},{3,7},{4,0},{5,1},{6,2},{7,3},{8,12},{9,13},{10,... | collective-permute-start | bytes 1290248 | tf_op jit(solution)/shard_map/ppermute | solution.py:447
  19.9 12.0 %collective-permute-start.6 = (bf16[64,1920]{1,0:T(8,128)(2,1)S(1)}, bf16[64,1920]{1,0:T(8,128)(2,1)S(1)}, u32[]{:S(2)}, u32[]{:S(2)}) collective-permute-start(bf16[64,1920]{1,0:T(8,128)(2,1)S(1)} %collective-permute-done.refs_1_), channel_id=1, source_target_pairs={{0,2},{2,0},{4,6},{6,4},{8,10},{10,8},{12,14},{14,12},{16,18},{18,... | collective-permute-start | bytes 737288 | tf_op jit(solution)/shard_map/ppermute | solution.py:459
  30.3 2.2 %collective-permute-start.7 = (bf16[64,1920]{1,0:T(8,128)(2,1)S(1)}, bf16[64,1920]{1,0:T(8,128)(2,1)S(1)}, u32[]{:S(2)}, u32[]{:S(2)}) collective-permute-start(bf16[64,1920]{1,0:T(8,128)(2,1)S(1)} %collective-permute-done.1.refs_2_), channel_id=1, source_target_pairs={{0,2},{2,0},{4,6},{6,4},{8,10},{10,8},{12,14},{14,12},{16,18},{18,... | collective-permute-start | bytes 737288 | tf_op jit(solution)/shard_map/ppermute | solution.py:459
  30.3 2.2 %collective-permute-start.8 = (bf16[64,1920]{1,0:T(8,128)(2,1)S(1)}, bf16[64,1920]{1,0:T(8,128)(2,1)S(1)}, u32[]{:S(2)}, u32[]{:S(2)}) collective-permute-start(bf16[64,1920]{1,0:T(8,128)(2,1)S(1)} %collective-permute-done.2.refs_3_), channel_id=1, source_target_pairs={{0,2},{2,0},{4,6},{6,4},{8,10},{10,8},{12,14},{14,12},{16,18},{18,... | collective-permute-start | bytes 737288 | tf_op jit(solution)/shard_map/ppermute | solution.py:459
  30.8 1.9 %collective-permute-start.5 = (bf16[64,1920]{1,0:T(8,128)(2,1)}, bf16[64,1920]{1,0:T(8,128)(2,1)S(1)}, u32[]{:S(2)}, u32[]{:S(2)}) collective-permute-start(bf16[64,1920]{1,0:T(8,128)(2,1)} %get-tuple-element.54.refs_0_), channel_id=1, source_target_pairs={{0,2},{2,0},{4,6},{6,4},{8,10},{10,8},{12,14},{14,12},{16,18},{18,... | collective-permute-start | bytes 737288 | tf_op jit(solution)/shard_map/ppermute | solution.py:459
  30.9 0.9 %copy-start = (bf16[64,1920]{1,0:T(8,128)(2,1)S(1)}, bf16[64,1920]{1,0:T(8,128)(2,1)}, u32[]{:S(2)}) copy-start(bf16[64,1920]{1,0:T(8,128)(2,1)} %get-tuple-element.54.refs_0_) | copy-start | bytes 737284
  31.9 0.9 %copy-start.1 = (bf16[64,1920]{1,0:T(8,128)(2,1)S(1)}, bf16[64,1920]{1,0:T(8,128)(2,1)}, u32[]{:S(2)}) copy-start(bf16[64,1920]{1,0:T(8,128)(2,1)} %get-tuple-element.54.refs_0_) | copy-start | bytes 737284
  31.9 1.1 %copy-start.5 = (bf16[120,1792]{1,0:T(8,128)(2,1)S(1)}, bf16[120,1792]{1,0:T(8,128)(2,1)}, u32[]{:S(2)}) copy-start(bf16[120,1792]{1,0:T(8,128)(2,1)} %get-tuple-element.53.refs_8_) | copy-start | bytes 1290244
  31.9 8.7 %copy-start.2 = (bf16[1,320,1792]{2,1,0:T(8,128)(2,1)S(1)}, bf16[1,320,1792]{2,1,0:T(8,128)(2,1)}, u32[]{:S(2)}) copy-start(bf16[1,320,1792]{2,1,0:T(8,128)(2,1)} %refs_10_.1) | copy-start | bytes 3440644
  31.9 8.7 %copy-start.3 = (bf16[1,320,1792]{2,1,0:T(8,128)(2,1)S(1)}, bf16[1,320,1792]{2,1,0:T(8,128)(2,1)}, u32[]{:S(2)}) copy-start(bf16[1,320,1792]{2,1,0:T(8,128)(2,1)} %refs_11_.1) | copy-start | bytes 3440644
  31.9 8.7 %copy-start.4 = (bf16[1,320,1792]{2,1,0:T(8,128)(2,1)S(1)}, bf16[1,320,1792]{2,1,0:T(8,128)(2,1)}, u32[]{:S(2)}) copy-start(bf16[1,320,1792]{2,1,0:T(8,128)(2,1)} %refs_12_.1) | copy-start | bytes 3440644
  31.9 5.7 %collective-permute-start.3 = (bf16[32,1920]{1,0:T(8,128)(2,1)S(1)}, bf16[32,1920]{1,0:T(8,128)(2,1)S(1)}, u32[]{:S(2)}, u32[]{:S(2)}) collective-permute-start(bf16[32,1920]{1,0:T(8,128)(2,1)S(1)} %cold_away.1), channel_id=1, source_target_pairs={{0,4},{1,5},{2,6},{3,7},{4,0},{5,1},{6,2},{7,3},{8,12},{9,13},{10,... | collective-permute-start | bytes 368648 | tf_op jit(solution)/shard_map/ppermute | solution.py:447
  37.7 11.5 %collective-permute-start.14 = (bf16[120,1792]{1,0:T(8,128)(2,1)S(1)}, bf16[120,1792]{1,0:T(8,128)(2,1)S(1)}, u32[]{:S(2)}, u32[]{:S(2)}) collective-permute-start(bf16[120,1792]{1,0:T(8,128)(2,1)S(1)} %get-tuple-element.67), channel_id=1, source_target_pairs={{0,4},{1,5},{2,6},{3,7},{4,0},{5,1},{6,2},{7,3},{8,12},{9,13},{10,... | collective-permute-start | bytes 1290248 | tf_op jit(solution)/shard_map/ppermute | solution.py:447
  38.2 11.2 %collective-permute-start.15 = (bf16[120,1792]{1,0:T(8,128)(2,1)S(1)}, bf16[120,1792]{1,0:T(8,128)(2,1)S(1)}, u32[]{:S(2)}, u32[]{:S(2)}) collective-permute-start(bf16[120,1792]{1,0:T(8,128)(2,1)S(1)} %get-tuple-element.68), channel_id=1, source_target_pairs={{0,1},{1,0},{2,3},{3,2},{4,5},{5,4},{6,7},{7,6},{8,9},{9,8},{10,11... | collective-permute-start | bytes 1290248 | tf_op jit(solution)/shard_map/ppermute | solution.py:447
  38.7 8.8 %collective-permute-start.11 = (bf16[96,1920]{1,0:T(8,128)(2,1)S(1)}, bf16[96,1920]{1,0:T(8,128)(2,1)S(1)}, u32[]{:S(2)}, u32[]{:S(2)}) collective-permute-start(bf16[96,1920]{1,0:T(8,128)(2,1)S(1)} %get-tuple-element.58), channel_id=1, source_target_pairs={{0,2},{2,0},{4,6},{6,4},{8,10},{10,8},{12,14},{14,12},{16,18},{18,... | collective-permute-start | bytes 1105928 | tf_op jit(solution)/shard_map/ppermute | solution.py:459
  38.7 1.9 %collective-permute-start.12 = (bf16[32,1920]{1,0:T(8,128)(2,1)S(1)}, bf16[32,1920]{1,0:T(8,128)(2,1)S(1)}, u32[]{:S(2)}, u32[]{:S(2)}) collective-permute-start(bf16[32,1920]{1,0:T(8,128)(2,1)S(1)} %collective-permute-done.3.refs_8_), channel_id=1, source_target_pairs={{0,2},{2,0},{4,6},{6,4},{8,10},{10,8},{12,14},{14,12},{16,18},{18,... | collective-permute-start | bytes 368648 | tf_op jit(solution)/shard_map/ppermute | solution.py:459
  46.0 26.6 %copy-start.6 = (s32[2,192]{1,0:T(2,128)S(1)}, s32[2,192]{1,0:T(2,128)}, u32[]{:S(2)}) copy-start(s32[2,192]{1,0:T(2,128)} %get-tuple-element.77.pos_ref) | copy-start | bytes 4612
  46.0 1.4 %collective-permute-start.13 = (bf16[32,1920]{1,0:T(8,128)(2,1)S(1)}, bf16[32,1920]{1,0:T(8,128)(2,1)S(1)}, u32[]{:S(2)}, u32[]{:S(2)}) collective-permute-start(bf16[32,1920]{1,0:T(8,128)(2,1)S(1)} %get-tuple-element.61), channel_id=1, source_target_pairs={{0,2},{2,0},{4,6},{6,4},{8,10},{10,8},{12,14},{14,12},{16,18},{18,... | collective-permute-start | bytes 368648 | tf_op jit(solution)/shard_map/ppermute | solution.py:459
  49.4 24.7 %collective-permute-start.22 = (bf16[120,1792]{1,0:T(8,128)(2,1)S(1)}, bf16[120,1792]{1,0:T(8,128)(2,1)S(1)}, u32[]{:S(2)}, u32[]{:S(2)}) collective-permute-start(bf16[120,1792]{1,0:T(8,128)(2,1)S(1)} %get-tuple-element.86), channel_id=1, source_target_pairs={{0,5},{1,4},{2,7},{3,6},{4,1},{5,0},{6,3},{7,2},{8,13},{9,12},{10,... | collective-permute-start | bytes 1290248 | tf_op jit(solution)/shard_map/ppermute | solution.py:447
  50.8 7.5 %collective-permute-start.16 = (bf16[32,1920]{1,0:T(8,128)(2,1)S(1)}, bf16[32,1920]{1,0:T(8,128)(2,1)S(1)}, u32[]{:S(2)}, u32[]{:S(2)}) collective-permute-start(bf16[32,1920]{1,0:T(8,128)(2,1)S(1)} %get-tuple-element.71), channel_id=1, source_target_pairs={{0,8},{2,10},{4,12},{6,14},{8,0},{10,2},{12,4},{14,6},{16,24},{18,... | collective-permute-start | bytes 368648 | tf_op jit(solution)/shard_map/ppermute | solution.py:451
  53.6 12.3 %collective-permute-start.17 = (bf16[32,1920]{1,0:T(8,128)(2,1)S(1)}, bf16[32,1920]{1,0:T(8,128)(2,1)S(1)}, u32[]{:S(2)}, u32[]{:S(2)}) collective-permute-start(bf16[32,1920]{1,0:T(8,128)(2,1)S(1)} %get-tuple-element.72), channel_id=1, source_target_pairs={{0,16},{2,18},{4,20},{6,22},{8,24},{10,26},{12,28},{14,30},{16,0},... | collective-permute-start | bytes 368648 | tf_op jit(solution)/shard_map/ppermute | solution.py:451
  54.6 11.3 %collective-permute-start.18 = (bf16[32,1920]{1,0:T(8,128)(2,1)S(1)}, bf16[32,1920]{1,0:T(8,128)(2,1)S(1)}, u32[]{:S(2)}, u32[]{:S(2)}) collective-permute-start(bf16[32,1920]{1,0:T(8,128)(2,1)S(1)} %get-tuple-element.73), channel_id=1, source_target_pairs={{0,24},{2,26},{4,28},{6,30},{8,16},{10,18},{12,20},{14,22},{16,8},... | collective-permute-start | bytes 368648 | tf_op jit(solution)/shard_map/ppermute | solution.py:451
  66.2 6.4 %collective-permute-start.19 = (bf16[40,1920]{1,0:T(8,128)(2,1)S(1)}, bf16[40,1920]{1,0:T(8,128)(2,1)S(1)}, u32[]{:S(2)}, u32[]{:S(2)}) collective-permute-start(bf16[40,1920]{1,0:T(8,128)(2,1)S(1)} %get-tuple-element.75), channel_id=1, source_target_pairs={{0,1},{1,0},{2,3},{3,2},{4,5},{5,4},{6,7},{7,6},{8,9},{9,8},{10,11... | collective-permute-start | bytes 460808 | tf_op jit(solution)/shard_map/ppermute | solution.py:447
  66.8 5.2 %collective-permute-start.21 = (bf16[16,1920]{1,0:T(8,128)(2,1)S(1)}, bf16[16,1920]{1,0:T(8,128)(2,1)S(1)}, u32[]{:S(2)}, u32[]{:S(2)}) collective-permute-start(bf16[16,1920]{1,0:T(8,128)(2,1)S(1)} %get-tuple-element.76), channel_id=1, source_target_pairs={{0,5},{1,4},{2,7},{3,6},{4,1},{5,0},{6,3},{7,2},{8,13},{9,12},{10,... | collective-permute-start | bytes 184328 | tf_op jit(solution)/shard_map/ppermute | solution.py:447
  68.3 4.4 %collective-permute-start.20 = (bf16[16,1920]{1,0:T(8,128)(2,1)S(1)}, bf16[16,1920]{1,0:T(8,128)(2,1)S(1)}, u32[]{:S(2)}, u32[]{:S(2)}) collective-permute-start(bf16[16,1920]{1,0:T(8,128)(2,1)S(1)} %get-tuple-element.76), channel_id=1, source_target_pairs={{0,4},{1,5},{2,6},{3,7},{4,0},{5,1},{6,2},{7,3},{8,12},{9,13},{10,... | collective-permute-start | bytes 184328 | tf_op jit(solution)/shard_map/ppermute | solution.py:447

commit v2 on v1

--- a/solution.py
+++ b/solution.py
@@ -121,6 +121,12 @@
         if k:
             message[:HCAP, :] = messages[0][:HCAP, :]
         message[HCAP:, :] = cold_ref[k * 16 : (k + 1) * 16, :]
+
+
+def copy_kernel(*refs):
+    half = len(refs) // 2
+    for in_ref, out_ref in zip(refs[:half], refs[half:]):
+        out_ref[...] = in_ref[...]
 
 
 def away_kernel(*refs):
@@ -228,11 +234,11 @@
     mine_x_ref, other_x_ref, gate_hbm, up_hbm, down_hbm = refs[message_count : message_count + 5]
     own_ref, send_ref, *outs = refs[message_count + 5 : message_count + 10]
     data_ref, dx_ref, w_ref, grad_ref, sum_ref, in_sem, out_sem = refs[message_count + 10 :]
-    total, width = data_ref.shape[0], gate_hbm.shape[2]
+    total, units, width = data_ref.shape[0], gate_hbm.shape[1], gate_hbm.shape[2]
     rows = COLD_ROWS
     single = rows == total
     loads = [
-        pltpu.make_async_copy(ref.at[0], w_ref.at[j], in_sem.at[j])
+        pltpu.make_async_copy(ref.at[0], w_ref.at[pl.ds(j * units, units)], in_sem.at[j])
         for j, ref in enumerate((gate_hbm, up_hbm, down_hbm))
     ]
     stores = [
@@ -255,38 +261,42 @@
     def weight(j):
         if single:
             loads[j].wait()
-        return w_ref[j]
+        return w_ref[j * units : (j + 1) * units, :]
 
     def block(start):
         at = pl.ds(start, rows)
         data = data_ref[at, :width]
-        prob = data_ref[at, width:].astype(F32)[:, 0:1]
-        gate = weight(0)
-        pre_gate = dot(data, gate, NT)
-        up = weight(1)
-        pre_up = dot(data, up, NT)
-        back = pltpu.roll(dot(data, weight(2), NT), rows - CAP, 0)
+        first = jnp.where((iota((8, TAIL), 0) == 0) & (iota((8, TAIL), 1) == 0), 1.0, 0.0)
+        prob = dot(first.astype(BF), data_ref[at, width:], NT)[0:1, :]
+        pre_gate = dot(weight(0), data, NT)
+        pre_up = dot(weight(1), data, NT)
+        back = pltpu.roll(dot(weight(2), data, NT), rows - CAP, 1)
         gate_grad, up_grad, weighted, prob_term = swiglu_back(pre_gate, pre_up, back, prob)
-        x_row = (iota(pre_gate.shape, 0) & 4) == 0
-        gate_grad = jnp.where(x_row, gate_grad, 0.0).astype(BF)
-        up_grad = jnp.where(x_row, up_grad, 0.0).astype(BF)
-        weighted = pltpu.roll(jnp.where(x_row, weighted, 0.0), CAP, 0).astype(BF)
-        prob_term = jnp.where(x_row, prob_term, 0.0)
+        x_lane = (iota(pre_gate.shape, 1) & 4) == 0
+        gate_grad = jnp.where(x_lane, gate_grad, 0.0)
+        up_grad = jnp.where(x_lane, up_grad, 0.0)
+        weighted = pltpu.roll(jnp.where(x_lane, weighted, 0.0), CAP, 1)
+        grad_prob = jnp.sum(jnp.where(x_lane, prob_term, 0.0), axis=0, keepdims=True)
+        inner = jnp.concatenate([gate_grad, up_grad], axis=0).astype(BF)
         for j, grad in enumerate((gate_grad, up_grad, weighted)):
-            term = dot(grad, data, TN)
+            term = dot(grad.astype(BF), data)
             if single:
                 grad_ref[j] = term.astype(BF)
                 stores[j].start()
             else:
                 sum_ref[j] += term
+        shape = (rows, rows // 2)
+        row, col = iota(shape, 0), iota(shape, 1)
+        pick = jnp.where(row == (col >> 2) * 8 + (col & 3), 1.0, 0.0).astype(BF)
+        dx = dot(dot(inner, pick).astype(BF), w_ref[: 2 * units, :], TN)
         shape = (rows // 2, rows)
         row, col = iota(shape, 0), iota(shape, 1)
         pick = jnp.where(col == (row >> 2) * 8 + (row & 3), 1.0, 0.0).astype(BF)
-        gate_rows = dot(pick, gate_grad).astype(BF)
-        up_rows = dot(pick, up_grad).astype(BF)
-        dx = dot(gate_rows, gate) + dot(up_rows, up)
-        tail = dot(pick, split_tail(jnp.sum(prob_term, axis=1, keepdims=True)).astype(BF))
-        grad_prob = tail[:, 0:1] + tail[:, 1:2]
+        high = grad_prob.astype(BF).astype(F32)
+        row = iota((8, rows), 0)
+        both = jnp.where(row == 0, high, jnp.where(row == 1, grad_prob - high, 0.0))
+        both = dot(pick, both.astype(BF), NT)
+        grad_prob = both[:, 0:1] + both[:, 1:2]
         half_at = pl.ds(start // 2 if single else pl.multiple_of(start // 2, 16), rows // 2)
         write_rows(dx_ref.at[half_at], dx, grad_prob)
 
@@ -484,7 +494,12 @@
     chunks = all_along_z(messages)
     by_pair = swap(hot_own, 2)
     by_x = swap(hot_own, 1)
-    first_out, by_pair_out, _ = lax.optimization_barrier((messages[0], by_pair, chunks[1]))
+    first_out, hot_own, _ = lax.optimization_barrier((messages[0], hot_own, chunks[1]))
+    first_out, hot_own = call(
+        copy_kernel, [message, shape(hot_own.shape, BF)], "own_rows"
+    )(first_out, hot_own)
+    chunks[0] = first_out
+    by_pair_out, first_out, hot_own = lax.optimization_barrier((by_pair, first_out, hot_own))
     weights = [hot_own, by_x, by_pair, swap(by_pair_out, 1)]
     (away,) = call(away_kernel, [shape((cold_rows // 2, lanes), BF)], "cold_away")(*chunks)
     chunks = chunks + [other_core(first_out)] + [other_core(chunk) for chunk in chunks[1:]]
@@ -523,7 +538,7 @@
         scratch=[
             ((2 * cold_rows, lanes), BF),
             ((cold_rows, lanes), F32),
-            ((3, cold_units, width), BF),
+            ((3 * cold_units, width), BF),
             ((3, cold_units, width), BF),
             ((3, cold_units, width) if 2 * cold_rows > COLD_ROWS else (8, 128), F32),
             pltpu.SemaphoreType.DMA((3,)),
@@ -540,7 +555,8 @@
     )(hot_dx, hot_got, cold_own, cold_got)
     term_x, _ = lax.optimization_barrier((sent_terms[0], cold_mine))
     got_x, got_y = swap(term_x, 1), swap(sent_terms[1], 2)
-    *parts, got_x, got_y, last_term = lax.optimization_barrier((*parts, got_x, got_y, sent_terms[2]))
+    last_term, cold_out = lax.optimization_barrier((sent_terms[2], cold_out))
+    *parts, got_x, got_y = lax.optimization_barrier((*parts, got_x, got_y))
     parts = all_along_z(parts)
     got_terms = [got_x, got_y, swap(last_term, 3)]
 
@@ -555,16 +571,17 @@
         "combine",
     )(*parts)
     rows_y, rows_x, rows_xy = swap(send_y, 2), swap(send_x, 1), swap(send_x, 3)
+    out_shape = shape((units_padded, width), BF)
+    hot_grads = call(sum_kernel, [out_shape] * 3, "hot_sum")(
+        own_term, *got_terms
+    )
+    own_rows, *hot_grads = lax.optimization_barrier((own_rows, *hot_grads))
     dx, prob_t = call(
         functools.partial(finish_kernel, base),
         [shape((half, width), BF), shape((TOP, half), F32)],
         "finish",
     )(own_rows, rows_y, rows_x, rows_xy, pos)
 
-    out_shape = shape((units_padded, width), BF)
-    hot_grads = call(sum_kernel, [out_shape] * 3, "hot_sum")(
-        own_term, *got_terms
-    )
     if pad:
         hot_grads = [value[:units] for value in hot_grads]
     return (dx, prob_t.T, grad_cold_gate, grad_cold_up, grad_cold_down, *hot_grads)

time: 75.1 us -> 73.4 us (0.977)
  waiting for transfers between devices: 34.9 us -> 30.7 us
  starting transfers between devices: 24 us -> 25.6 us
  local copies, waits for them, and re-layouts: 1.21 us -> 1.97 us
    ppermute x10, waiting for transfers between devices: 6.47 us -> 3.46 us  [swap(): return lax.ppermute(value, ('dp', 'pair'), perm)]
    ppermute x6, waiting for transfers between devices: 25.6 us -> 23.6 us  [along_z(): return lax.ppermute(value, 'dp', perm)]
    ppermute x10, starting transfers between devices: 13 us -> 14.2 us  [swap(): return lax.ppermute(value, ('dp', 'pair'), perm)]
    ppermute x7, waiting for transfers between devices: 2.8 us -> 3.66 us  [other_core(): return lax.ppermute(value, 'dp', [(i, i ^ 1) for i in range(count)])]
    unnamed x14 -> x12, local copies, waits for them, and re-layouts: 1.21 us -> 1.97 us
    pallas_call x8 -> x9, Pallas kernels: 14.1 us -> 14.2 us  [run(): pl.pallas_call(kernel, out_shape=outs, in_specs=[pl.BlockSpec(memory_spac...]
  transfers between devices with their start and end apart: 23 -> 23, of which waited for: 12 -> 12; matrix products, arithmetic and copies ran while one was open for 0% -> 0% of each run, Pallas kernels for 14% -> 13%
where the time goes in v2:
time: 73.4 us; the launch traced here: 73.2 us
  waiting for transfers between devices  30.7 us (42%)
  starting transfers between devices  25.6 us (35%)
  Pallas kernels  14.2 us (19%)
  local copies, waits for them, and re-layouts  1.97 us (3%)
  between operations  0.75 us (1%)
    ppermute x6, waiting for transfers between devices, along_z(): return lax.ppermute(value, 'dp', perm)  23.6 us
    pallas_call x9, Pallas kernels, run(): pl.pallas_call(kernel, out_shape=outs, in_specs=[pl.BlockSpec(memory_spac...  14.2 us
    ppermute x10, starting transfers between devices, swap(): return lax.ppermute(value, ('dp', 'pair'), perm)  14.2 us
    ppermute x6, starting transfers between devices, along_z(): return lax.ppermute(value, 'dp', perm)  10.2 us
    ppermute x7, waiting for transfers between devices, other_core(): return lax.ppermute(value, 'dp', [(i, i ^ 1) for i in range(count)])  3.66 us
    ppermute x10, waiting for transfers between devices, swap(): return lax.ppermute(value, ('dp', 'pair'), perm)  3.46 us
    unnamed x12, local copies, waits for them, and re-layouts  1.97 us
  transfers between devices with their start and end apart: 23, of which 12 were waited for; matrix products, arithmetic and copies ran while one was open for 0% of the time, Pallas kernels for 13%

profile of v2, /device:TPU:0, one launch (start us, length us, event | category | flops | bytes accessed | tf_op | source)
XLA Modules:
  0.0 73.2 jit_solution(6953355427425954668)
XLA Ops:
  0.6 3.1 %dispatch.1 = (s32[2,192]{1,0:T(2,128)}, bf16[120,1792]{1,0:T(8,128)(2,1)}, bf16[64,1920]{1,0:T(8,128)(2,1)}, bf16[64,1920]{1,0:T(8,128)(2,1)}, bf16[64,1920]{1,0:T(8,128)(2,1)}, /*index=5*/bf16[64,1920]{1,0:T(8,128)(2,1)}) custom-call(bf16[192,1792]{1,0:T(8,128)(2,1)} %refs_0_.1, bf16[192,1792]{1,0:T(8,128)(2,1)} %refs_1_.1, bf16[2,192]{1,0:T(2,128)(2,1)} %bitcast.6, ...), custom_call_target="tpu_custom_call" | custom-call | flops 1024 | bytes 1024 | tf_op jit(solution)/shard_map/dispatch/pallas_call | solution.py:410
  3.8 3.0 %collective-permute-start.4 = (bf16[120,1792]{1,0:T(8,128)(2,1)}, bf16[120,1792]{1,0:T(8,128)(2,1)S(1)}, u32[]{:S(2)}, u32[]{:S(2)}) collective-permute-start(bf16[120,1792]{1,0:T(8,128)(2,1)} %get-tuple-element.62.refs_1_), channel_id=1, source_target_pairs={{0,1},{1,0},{2,3},{3,2},{4,5},{5,4},{6,7},{7,6},{8,9},{9,8},{10,11... | collective-permute-start | bytes 1290248 | tf_op jit(solution)/shard_map/ppermute | solution.py:457
  6.7 1.6 %collective-permute-start = (bf16[64,1920]{1,0:T(8,128)(2,1)}, bf16[64,1920]{1,0:T(8,128)(2,1)S(1)}, u32[]{:S(2)}, u32[]{:S(2)}) collective-permute-start(bf16[64,1920]{1,0:T(8,128)(2,1)} %get-tuple-element.60), channel_id=1, source_target_pairs={{0,8},{2,10},{4,12},{6,14},{8,0},{10,2},{12,4},{14,6},{16,24},{18,... | collective-permute-start | bytes 737288 | tf_op jit(solution)/shard_map/ppermute | solution.py:461
  8.3 1.5 %collective-permute-start.9 = (bf16[120,1792]{1,0:T(8,128)(2,1)}, bf16[120,1792]{1,0:T(8,128)(2,1)S(1)}, u32[]{:S(2)}, u32[]{:S(2)}) collective-permute-start(bf16[120,1792]{1,0:T(8,128)(2,1)} %get-tuple-element.62.refs_1_), channel_id=1, source_target_pairs={{0,4},{1,5},{2,6},{3,7},{4,0},{5,1},{6,2},{7,3},{8,12},{9,13},{10,... | collective-permute-start | bytes 1290248 | tf_op jit(solution)/shard_map/ppermute | solution.py:457
  9.8 2.6 %collective-permute-start.1 = (bf16[64,1920]{1,0:T(8,128)(2,1)}, bf16[64,1920]{1,0:T(8,128)(2,1)S(1)}, u32[]{:S(2)}, u32[]{:S(2)}) collective-permute-start(bf16[64,1920]{1,0:T(8,128)(2,1)} %get-tuple-element.64), channel_id=1, source_target_pairs={{0,16},{2,18},{4,20},{6,22},{8,24},{10,26},{12,28},{14,30},{16,0},... | collective-permute-start | bytes 737288 | tf_op jit(solution)/shard_map/ppermute | solution.py:461
  12.4 0.2 collective-permute-start.2
  12.6 5.3 %collective-permute-done.refs_1_ = bf16[64,1920]{1,0:T(8,128)(2,1)S(1)} collective-permute-done((bf16[64,1920]{1,0:T(8,128)(2,1)}, bf16[64,1920]{1,0:T(8,128)(2,1)S(1)}, u32[]{:S(2)}, u32[]{:S(2)}) %collective-permute-start) | collective-permute-done | bytes 245792 | tf_op jit(solution)/shard_map/ppermute | solution.py:461
  17.9 0.0 copy-start.3
  17.9 1.0 %copy-done.3 = bf16[120,1792]{1,0:T(8,128)(2,1)S(1)} copy-done((bf16[120,1792]{1,0:T(8,128)(2,1)S(1)}, bf16[120,1792]{1,0:T(8,128)(2,1)}, u32[]{:S(2)}) %copy-start.3) | copy-done | bytes 430104
  19.0 0.0 copy-start.4
  19.0 0.9 %copy-done.4 = bf16[64,1920]{1,0:T(8,128)(2,1)S(1)} copy-done((bf16[64,1920]{1,0:T(8,128)(2,1)S(1)}, bf16[64,1920]{1,0:T(8,128)(2,1)}, u32[]{:S(2)}) %copy-start.4) | copy-done | bytes 245784
  19.9 0.0 collective-permute-done.4.refs_10_
  20.0 2.0 %collective-permute-start.10 = (bf16[120,1792]{1,0:T(8,128)(2,1)S(1)}, bf16[120,1792]{1,0:T(8,128)(2,1)S(1)}, u32[]{:S(2)}, u32[]{:S(2)}) collective-permute-start(bf16[120,1792]{1,0:T(8,128)(2,1)S(1)} %collective-permute-done.4.refs_10_), channel_id=1, source_target_pairs={{0,4},{1,5},{2,6},{3,7},{4,0},{5,1},{6,2},{7,3},{8,12},{9,13},{10,... | collective-permute-start | bytes 1290248 | tf_op jit(solution)/shard_map/ppermute | solution.py:457
  22.0 0.0 collective-permute-start.6
  22.0 8.3 %collective-permute-done.1.refs_2_ = bf16[64,1920]{1,0:T(8,128)(2,1)S(1)} collective-permute-done((bf16[64,1920]{1,0:T(8,128)(2,1)}, bf16[64,1920]{1,0:T(8,128)(2,1)S(1)}, u32[]{:S(2)}, u32[]{:S(2)}) %collective-permute-start.1) | collective-permute-done | bytes 245792 | tf_op jit(solution)/shard_map/ppermute | solution.py:461
  30.3 0.0 collective-permute-start.7
  30.3 0.0 collective-permute-done.2.refs_3_
  30.3 0.5 collective-permute-start.8
  30.8 0.0 collective-permute-done.9.refs_9_
  30.8 0.1 collective-permute-start.5
  30.9 0.0 copy-start
  30.9 0.0 copy-start.1
  31.0 0.0 copy-start.2
  31.0 0.0 collective-permute-done.6.refs_5_
  31.0 0.6 collective-permute-start.3
  31.6 0.3 collective-permute-done.7.refs_6_
  31.8 0.4 collective-permute-done.8.refs_7_
  32.2 0.4 collective-permute-done.5.refs_4_
  32.5 0.0 collective-permute-done.10.refs_11_
  32.5 2.7 %hot.1 = (f32[96,1920]{1,0:T(8,128)S(1)}, bf16[96,1920]{1,0:T(8,128)(2,1)S(1)}, f32[120,1792]{1,0:T(8,128)S(1)}, bf16[120,1792]{1,0:T(8,128)(2,1)S(1)}, bf16[120...) custom-call(bf16[64,1920]{1,0:T(8,128)(2,1)S(1)} %get-tuple-element.67.refs_0_, ...), custom_call_target="tpu_custom_call" | custom-call | flops 1024 | bytes 1024 | tf_op jit(solution)/shard_map/hot/pallas_call | solution.py:410
  35.2 1.5 %collective-permute-done.3.refs_8_ = bf16[32,1920]{1,0:T(8,128)(2,1)S(1)} collective-permute-done((bf16[32,1920]{1,0:T(8,128)(2,1)S(1)}, bf16[32,1920]{1,0:T(8,128)(2,1)S(1)}, u32[]{:S(2)}, u32[]{:S(2)}) %collective-permute-start.3) | collective-permute-done | bytes 122912 | tf_op jit(solution)/shard_map/ppermute | solution.py:457
  36.7 0.5 collective-permute-start.14
  37.2 0.5 collective-permute-start.15
  37.7 0.0 collective-permute-start.11
  37.7 0.5 collective-permute-start.12
  38.3 1.4 %collective-permute-done.12.refs_9_ = bf16[32,1920]{1,0:T(8,128)(2,1)S(1)} collective-permute-done((bf16[32,1920]{1,0:T(8,128)(2,1)S(1)}, bf16[32,1920]{1,0:T(8,128)(2,1)S(1)}, u32[]{:S(2)}, u32[]{:S(2)}) %collective-permute-start.12) | collective-permute-done | bytes 122912 | tf_op jit(solution)/shard_map/ppermute | solution.py:469
  39.6 0.0 copy-done
  39.6 0.0 copy-done.1
  39.6 0.0 copy-done.2
  39.6 5.5 %cold.1 = (f32[32,1920]{1,0:T(8,128)S(1)}, bf16[32,1920]{1,0:T(8,128)(2,1)S(1)}, bf16[1,320,1792]{2,1,0:T(8,128)(2,1)}, bf16[1,320,1792]{2,1,0:T(8,128)(2,1)}, bf16[1,320,1792]{2,1,0:T(8,128)(2,1)}) custom-call(bf16[64,1920]{1,0:T(8,128)(2,1)S(1)} %get-tuple-element.67.refs_0_, bf16[64,1920]{1,0:T(8,128)(2,1)S(1)} %collective-permute-done.refs_1_, ...), custom_call_target="tpu_custom_call" | custom-call | flops 1024 | bytes 1024 | tf_op jit(solution)/shard_map/cold/pallas_call | solution.py:410
  45.2 2.5 %collective-permute-start.19 = (bf16[120,1792]{1,0:T(8,128)(2,1)S(1)}, bf16[120,1792]{1,0:T(8,128)(2,1)S(1)}, u32[]{:S(2)}, u32[]{:S(2)}) collective-permute-start(bf16[120,1792]{1,0:T(8,128)(2,1)S(1)} %get-tuple-element.92), channel_id=1, source_target_pairs={{0,5},{1,4},{2,7},{3,6},{4,1},{5,0},{6,3},{7,2},{8,13},{9,12},{10,... | collective-permute-start | bytes 1290248 | tf_op jit(solution)/shard_map/ppermute | solution.py:457
  47.7 0.0 collective-permute-start.13
  47.7 1.3 %collective-permute-done.13.cold_got_ref = bf16[32,1920]{1,0:T(8,128)(2,1)S(1)} collective-permute-done((bf16[32,1920]{1,0:T(8,128)(2,1)S(1)}, bf16[32,1920]{1,0:T(8,128)(2,1)S(1)}, u32[]{:S(2)}, u32[]{:S(2)}) %collective-permute-start.13) | collective-permute-done | bytes 122912 | tf_op jit(solution)/shard_map/ppermute | solution.py:469
  49.0 0.0 collective-permute-done.11.hot_got_ref
  49.0 0.3 add_cores.1
  49.3 0.0 collective-permute-done.14.a_ref
  49.3 0.0 collective-permute-done.15.b_ref
  49.3 3.4 %collective-permute-start.16 = (bf16[32,1920]{1,0:T(8,128)(2,1)S(1)}, bf16[32,1920]{1,0:T(8,128)(2,1)S(1)}, u32[]{:S(2)}, u32[]{:S(2)}) collective-permute-start(bf16[32,1920]{1,0:T(8,128)(2,1)S(1)} %get-tuple-element.84), channel_id=1, source_target_pairs={{0,8},{2,10},{4,12},{6,14},{8,0},{10,2},{12,4},{14,6},{16,24},{18,... | collective-permute-start | bytes 368648 | tf_op jit(solution)/shard_map/ppermute | solution.py:461
  52.7 1.1 %collective-permute-start.17 = (bf16[32,1920]{1,0:T(8,128)(2,1)S(1)}, bf16[32,1920]{1,0:T(8,128)(2,1)S(1)}, u32[]{:S(2)}, u32[]{:S(2)}) collective-permute-start(bf16[32,1920]{1,0:T(8,128)(2,1)S(1)} %get-tuple-element.85), channel_id=1, source_target_pairs={{0,16},{2,18},{4,20},{6,22},{8,24},{10,26},{12,28},{14,30},{16,0},... | collective-permute-start | bytes 368648 | tf_op jit(solution)/shard_map/ppermute | solution.py:461
  53.8 1.4 %collective-permute-start.18 = (bf16[32,1920]{1,0:T(8,128)(2,1)S(1)}, bf16[32,1920]{1,0:T(8,128)(2,1)S(1)}, u32[]{:S(2)}, u32[]{:S(2)}) collective-permute-start(bf16[32,1920]{1,0:T(8,128)(2,1)S(1)} %get-tuple-element.86), channel_id=1, source_target_pairs={{0,24},{2,26},{4,28},{6,30},{8,16},{10,18},{12,20},{14,22},{16,8},... | collective-permute-start | bytes 368648 | tf_op jit(solution)/shard_map/ppermute | solution.py:461
  55.2 2.8 %collective-permute-done.16.refs_1_ = bf16[32,1920]{1,0:T(8,128)(2,1)S(1)} collective-permute-done((bf16[32,1920]{1,0:T(8,128)(2,1)S(1)}, bf16[32,1920]{1,0:T(8,128)(2,1)S(1)}, u32[]{:S(2)}, u32[]{:S(2)}) %collective-permute-start.16) | collective-permute-done | bytes 122912 | tf_op jit(solution)/shard_map/ppermute | solution.py:461
  58.0 7.1 %collective-permute-done.17.refs_2_ = bf16[32,1920]{1,0:T(8,128)(2,1)S(1)} collective-permute-done((bf16[32,1920]{1,0:T(8,128)(2,1)S(1)}, bf16[32,1920]{1,0:T(8,128)(2,1)S(1)}, u32[]{:S(2)}, u32[]{:S(2)}) %collective-permute-start.17) | collective-permute-done | bytes 122912 | tf_op jit(solution)/shard_map/ppermute | solution.py:461
  65.1 0.0 collective-permute-done.18.refs_3_
  65.1 0.3 combine.1
  65.4 0.6 collective-permute-start.20
  65.9 1.5 %collective-permute-start.22 = (bf16[16,1920]{1,0:T(8,128)(2,1)S(1)}, bf16[16,1920]{1,0:T(8,128)(2,1)S(1)}, u32[]{:S(2)}, u32[]{:S(2)}) collective-permute-start(bf16[16,1920]{1,0:T(8,128)(2,1)S(1)} %get-tuple-element.98), channel_id=1, source_target_pairs={{0,5},{1,4},{2,7},{3,6},{4,1},{5,0},{6,3},{7,2},{8,13},{9,12},{10,... | collective-permute-start | bytes 184328 | tf_op jit(solution)/shard_map/ppermute | solution.py:457
  67.4 1.5 %collective-permute-start.21 = (bf16[16,1920]{1,0:T(8,128)(2,1)S(1)}, bf16[16,1920]{1,0:T(8,128)(2,1)S(1)}, u32[]{:S(2)}, u32[]{:S(2)}) collective-permute-start(bf16[16,1920]{1,0:T(8,128)(2,1)S(1)} %get-tuple-element.98), channel_id=1, source_target_pairs={{0,4},{1,5},{2,6},{3,7},{4,0},{5,1},{6,2},{7,3},{8,12},{9,13},{10,... | collective-permute-start | bytes 184328 | tf_op jit(solution)/shard_map/ppermute | solution.py:457
  68.9 0.0 collective-permute-done.19.c_ref
  68.9 0.9 %hot_sum.1 = (bf16[40,1792]{1,0:T(8,128)(2,1)}, bf16[40,1792]{1,0:T(8,128)(2,1)}, bf16[40,1792]{1,0:T(8,128)(2,1)}) custom-call(f32[120,1792]{1,0:T(8,128)S(1)} %get-tuple-element.88.own_ref, bf16[120,1792]{1,0:T(8,128)(2,1)S(1)} %collective-permute-done.14.a_ref, bf16[120,1792]{1,0:T(8,128)(2,1)S(1)} %collective-permute-done.15.b_ref, ...), custom_call_target="tpu_custom_call" | custom-call | flops 1024 | bytes 1024 | tf_op jit(solution)/shard_map/hot_sum/pallas_call | solution.py:410
  69.8 1.4 %collective-permute-done.22.xy_ref = bf16[16,1920]{1,0:T(8,128)(2,1)S(1)} collective-permute-done((bf16[16,1920]{1,0:T(8,128)(2,1)S(1)}, bf16[16,1920]{1,0:T(8,128)(2,1)S(1)}, u32[]{:S(2)}, u32[]{:S(2)}) %collective-permute-start.22) | collective-permute-done | bytes 61472 | tf_op jit(solution)/shard_map/ppermute | solution.py:457
  71.2 0.6 collective-permute-done.21.x_ref
  71.8 0.0 collective-permute-done.20.y_ref
  71.8 0.0 copy-done.5
  71.8 1.4 %finish.1 = (bf16[96,1792]{1,0:T(8,128)(2,1)}, f32[2,96]{1,0:T(2,128)}) custom-call(f32[40,1920]{1,0:T(8,128)S(1)} %get-tuple-element.96.own_ref, bf16[40,1920]{1,0:T(8,128)(2,1)S(1)} %collective-permute-done.20.y_ref, bf16[16,1920]{1,0:T(8,128)(2,1)S(1)} %collective-permute-done.21.x_ref, bf16[16,1920]{1,0:T(8,128)(2,1)S(1)} %collective-permute-done.22.xy_ref, ...), custom_call_target="tpu_custom_call" | custom-call | flops 1024 | bytes 1024 | tf_op jit(solution)/shard_map/finish/pallas_call | solution.py:410
  (3 shorter events, 0.1 us)
Async XLA Ops:
  3.8 16.2 %collective-permute-start.4 = (bf16[120,1792]{1,0:T(8,128)(2,1)}, bf16[120,1792]{1,0:T(8,128)(2,1)S(1)}, u32[]{:S(2)}, u32[]{:S(2)}) collective-permute-start(bf16[120,1792]{1,0:T(8,128)(2,1)} %get-tuple-element.62.refs_1_), channel_id=1, source_target_pairs={{0,1},{1,0},{2,3},{3,2},{4,5},{5,4},{6,7},{7,6},{8,9},{9,8},{10,11... | collective-permute-start | bytes 1290248 | tf_op jit(solution)/shard_map/ppermute | solution.py:457
  6.7 11.2 %collective-permute-start = (bf16[64,1920]{1,0:T(8,128)(2,1)}, bf16[64,1920]{1,0:T(8,128)(2,1)S(1)}, u32[]{:S(2)}, u32[]{:S(2)}) collective-permute-start(bf16[64,1920]{1,0:T(8,128)(2,1)} %get-tuple-element.60), channel_id=1, source_target_pairs={{0,8},{2,10},{4,12},{6,14},{8,0},{10,2},{12,4},{14,6},{16,24},{18,... | collective-permute-start | bytes 737288 | tf_op jit(solution)/shard_map/ppermute | solution.py:461
  8.3 22.5 %collective-permute-start.9 = (bf16[120,1792]{1,0:T(8,128)(2,1)}, bf16[120,1792]{1,0:T(8,128)(2,1)S(1)}, u32[]{:S(2)}, u32[]{:S(2)}) collective-permute-start(bf16[120,1792]{1,0:T(8,128)(2,1)} %get-tuple-element.62.refs_1_), channel_id=1, source_target_pairs={{0,4},{1,5},{2,6},{3,7},{4,0},{5,1},{6,2},{7,3},{8,12},{9,13},{10,... | collective-permute-start | bytes 1290248 | tf_op jit(solution)/shard_map/ppermute | solution.py:457
  9.8 20.5 %collective-permute-start.1 = (bf16[64,1920]{1,0:T(8,128)(2,1)}, bf16[64,1920]{1,0:T(8,128)(2,1)S(1)}, u32[]{:S(2)}, u32[]{:S(2)}) collective-permute-start(bf16[64,1920]{1,0:T(8,128)(2,1)} %get-tuple-element.64), channel_id=1, source_target_pairs={{0,16},{2,18},{4,20},{6,22},{8,24},{10,26},{12,28},{14,30},{16,0},... | collective-permute-start | bytes 737288 | tf_op jit(solution)/shard_map/ppermute | solution.py:461
  12.4 18.0 %collective-permute-start.2 = (bf16[64,1920]{1,0:T(8,128)(2,1)}, bf16[64,1920]{1,0:T(8,128)(2,1)S(1)}, u32[]{:S(2)}, u32[]{:S(2)}) collective-permute-start(bf16[64,1920]{1,0:T(8,128)(2,1)} %get-tuple-element.65), channel_id=1, source_target_pairs={{0,24},{2,26},{4,28},{6,30},{8,16},{10,18},{12,20},{14,22},{16,8},... | collective-permute-start | bytes 737288 | tf_op jit(solution)/shard_map/ppermute | solution.py:461
  17.9 1.0 %copy-start.3 = (bf16[120,1792]{1,0:T(8,128)(2,1)S(1)}, bf16[120,1792]{1,0:T(8,128)(2,1)}, u32[]{:S(2)}) copy-start(bf16[120,1792]{1,0:T(8,128)(2,1)} %get-tuple-element.62.refs_1_) | copy-start | bytes 1290244
  19.0 0.9 %copy-start.4 = (bf16[64,1920]{1,0:T(8,128)(2,1)S(1)}, bf16[64,1920]{1,0:T(8,128)(2,1)}, u32[]{:S(2)}) copy-start(bf16[64,1920]{1,0:T(8,128)(2,1)} %get-tuple-element.61.refs_0_) | copy-start | bytes 737284
  20.0 12.6 %collective-permute-start.10 = (bf16[120,1792]{1,0:T(8,128)(2,1)S(1)}, bf16[120,1792]{1,0:T(8,128)(2,1)S(1)}, u32[]{:S(2)}, u32[]{:S(2)}) collective-permute-start(bf16[120,1792]{1,0:T(8,128)(2,1)S(1)} %collective-permute-done.4.refs_10_), channel_id=1, source_target_pairs={{0,4},{1,5},{2,6},{3,7},{4,0},{5,1},{6,2},{7,3},{8,12},{9,13},{10,... | collective-permute-start | bytes 1290248 | tf_op jit(solution)/shard_map/ppermute | solution.py:457
  22.0 9.0 %collective-permute-start.6 = (bf16[64,1920]{1,0:T(8,128)(2,1)S(1)}, bf16[64,1920]{1,0:T(8,128)(2,1)S(1)}, u32[]{:S(2)}, u32[]{:S(2)}) collective-permute-start(bf16[64,1920]{1,0:T(8,128)(2,1)S(1)} %collective-permute-done.refs_1_), channel_id=1, source_target_pairs={{0,2},{2,0},{4,6},{6,4},{8,10},{10,8},{12,14},{14,12},{16,18},{18,... | collective-permute-start | bytes 737288 | tf_op jit(solution)/shard_map/ppermute | solution.py:469
  30.3 1.5 %collective-permute-start.7 = (bf16[64,1920]{1,0:T(8,128)(2,1)S(1)}, bf16[64,1920]{1,0:T(8,128)(2,1)S(1)}, u32[]{:S(2)}, u32[]{:S(2)}) collective-permute-start(bf16[64,1920]{1,0:T(8,128)(2,1)S(1)} %collective-permute-done.1.refs_2_), channel_id=1, source_target_pairs={{0,2},{2,0},{4,6},{6,4},{8,10},{10,8},{12,14},{14,12},{16,18},{18,... | collective-permute-start | bytes 737288 | tf_op jit(solution)/shard_map/ppermute | solution.py:469
  30.3 1.9 %collective-permute-start.8 = (bf16[64,1920]{1,0:T(8,128)(2,1)S(1)}, bf16[64,1920]{1,0:T(8,128)(2,1)S(1)}, u32[]{:S(2)}, u32[]{:S(2)}) collective-permute-start(bf16[64,1920]{1,0:T(8,128)(2,1)S(1)} %collective-permute-done.2.refs_3_), channel_id=1, source_target_pairs={{0,2},{2,0},{4,6},{6,4},{8,10},{10,8},{12,14},{14,12},{16,18},{18,... | collective-permute-start | bytes 737288 | tf_op jit(solution)/shard_map/ppermute | solution.py:469
  30.8 1.7 %collective-permute-start.5 = (bf16[64,1920]{1,0:T(8,128)(2,1)S(1)}, bf16[64,1920]{1,0:T(8,128)(2,1)S(1)}, u32[]{:S(2)}, u32[]{:S(2)}) collective-permute-start(bf16[64,1920]{1,0:T(8,128)(2,1)S(1)} %get-tuple-element.67.refs_0_), channel_id=1, source_target_pairs={{0,2},{2,0},{4,6},{6,4},{8,10},{10,8},{12,14},{14,12},{16,18},{18,... | collective-permute-start | bytes 737288 | tf_op jit(solution)/shard_map/ppermute | solution.py:469
  30.9 8.7 %copy-start = (bf16[1,320,1792]{2,1,0:T(8,128)(2,1)S(1)}, bf16[1,320,1792]{2,1,0:T(8,128)(2,1)}, u32[]{:S(2)}) copy-start(bf16[1,320,1792]{2,1,0:T(8,128)(2,1)} %refs_10_.1) | copy-start | bytes 3440644
  30.9 8.7 %copy-start.1 = (bf16[1,320,1792]{2,1,0:T(8,128)(2,1)S(1)}, bf16[1,320,1792]{2,1,0:T(8,128)(2,1)}, u32[]{:S(2)}) copy-start(bf16[1,320,1792]{2,1,0:T(8,128)(2,1)} %refs_11_.1) | copy-start | bytes 3440644
  31.0 8.7 %copy-start.2 = (bf16[1,320,1792]{2,1,0:T(8,128)(2,1)S(1)}, bf16[1,320,1792]{2,1,0:T(8,128)(2,1)}, u32[]{:S(2)}) copy-start(bf16[1,320,1792]{2,1,0:T(8,128)(2,1)} %refs_12_.1) | copy-start | bytes 3440644
  31.0 5.7 %collective-permute-start.3 = (bf16[32,1920]{1,0:T(8,128)(2,1)S(1)}, bf16[32,1920]{1,0:T(8,128)(2,1)S(1)}, u32[]{:S(2)}, u32[]{:S(2)}) collective-permute-start(bf16[32,1920]{1,0:T(8,128)(2,1)S(1)} %cold_away.1), channel_id=1, source_target_pairs={{0,4},{1,5},{2,6},{3,7},{4,0},{5,1},{6,2},{7,3},{8,12},{9,13},{10,... | collective-permute-start | bytes 368648 | tf_op jit(solution)/shard_map/ppermute | solution.py:457
  36.7 12.6 %collective-permute-start.14 = (bf16[120,1792]{1,0:T(8,128)(2,1)S(1)}, bf16[120,1792]{1,0:T(8,128)(2,1)S(1)}, u32[]{:S(2)}, u32[]{:S(2)}) collective-permute-start(bf16[120,1792]{1,0:T(8,128)(2,1)S(1)} %get-tuple-element.81), channel_id=1, source_target_pairs={{0,4},{1,5},{2,6},{3,7},{4,0},{5,1},{6,2},{7,3},{8,12},{9,13},{10,... | collective-permute-start | bytes 1290248 | tf_op jit(solution)/shard_map/ppermute | solution.py:457
  37.2 12.1 %collective-permute-start.15 = (bf16[120,1792]{1,0:T(8,128)(2,1)S(1)}, bf16[120,1792]{1,0:T(8,128)(2,1)S(1)}, u32[]{:S(2)}, u32[]{:S(2)}) collective-permute-start(bf16[120,1792]{1,0:T(8,128)(2,1)S(1)} %get-tuple-element.82), channel_id=1, source_target_pairs={{0,1},{1,0},{2,3},{3,2},{4,5},{5,4},{6,7},{7,6},{8,9},{9,8},{10,11... | collective-permute-start | bytes 1290248 | tf_op jit(solution)/shard_map/ppermute | solution.py:457
  37.7 11.3 %collective-permute-start.11 = (bf16[96,1920]{1,0:T(8,128)(2,1)S(1)}, bf16[96,1920]{1,0:T(8,128)(2,1)S(1)}, u32[]{:S(2)}, u32[]{:S(2)}) collective-permute-start(bf16[96,1920]{1,0:T(8,128)(2,1)S(1)} %get-tuple-element.72), channel_id=1, source_target_pairs={{0,2},{2,0},{4,6},{6,4},{8,10},{10,8},{12,14},{14,12},{16,18},{18,... | collective-permute-start | bytes 1105928 | tf_op jit(solution)/shard_map/ppermute | solution.py:469
  37.7 1.9 %collective-permute-start.12 = (bf16[32,1920]{1,0:T(8,128)(2,1)S(1)}, bf16[32,1920]{1,0:T(8,128)(2,1)S(1)}, u32[]{:S(2)}, u32[]{:S(2)}) collective-permute-start(bf16[32,1920]{1,0:T(8,128)(2,1)S(1)} %collective-permute-done.3.refs_8_), channel_id=1, source_target_pairs={{0,2},{2,0},{4,6},{6,4},{8,10},{10,8},{12,14},{14,12},{16,18},{18,... | collective-permute-start | bytes 368648 | tf_op jit(solution)/shard_map/ppermute | solution.py:469
  45.2 23.8 %collective-permute-start.19 = (bf16[120,1792]{1,0:T(8,128)(2,1)S(1)}, bf16[120,1792]{1,0:T(8,128)(2,1)S(1)}, u32[]{:S(2)}, u32[]{:S(2)}) collective-permute-start(bf16[120,1792]{1,0:T(8,128)(2,1)S(1)} %get-tuple-element.92), channel_id=1, source_target_pairs={{0,5},{1,4},{2,7},{3,6},{4,1},{5,0},{6,3},{7,2},{8,13},{9,12},{10,... | collective-permute-start | bytes 1290248 | tf_op jit(solution)/shard_map/ppermute | solution.py:457
  47.7 1.3 %collective-permute-start.13 = (bf16[32,1920]{1,0:T(8,128)(2,1)S(1)}, bf16[32,1920]{1,0:T(8,128)(2,1)S(1)}, u32[]{:S(2)}, u32[]{:S(2)}) collective-permute-start(bf16[32,1920]{1,0:T(8,128)(2,1)S(1)} %get-tuple-element.75), channel_id=1, source_target_pairs={{0,2},{2,0},{4,6},{6,4},{8,10},{10,8},{12,14},{14,12},{16,18},{18,... | collective-permute-start | bytes 368648 | tf_op jit(solution)/shard_map/ppermute | solution.py:469
  49.3 8.7 %collective-permute-start.16 = (bf16[32,1920]{1,0:T(8,128)(2,1)S(1)}, bf16[32,1920]{1,0:T(8,128)(2,1)S(1)}, u32[]{:S(2)}, u32[]{:S(2)}) collective-permute-start(bf16[32,1920]{1,0:T(8,128)(2,1)S(1)} %get-tuple-element.84), channel_id=1, source_target_pairs={{0,8},{2,10},{4,12},{6,14},{8,0},{10,2},{12,4},{14,6},{16,24},{18,... | collective-permute-start | bytes 368648 | tf_op jit(solution)/shard_map/ppermute | solution.py:461
  52.7 12.4 %collective-permute-start.17 = (bf16[32,1920]{1,0:T(8,128)(2,1)S(1)}, bf16[32,1920]{1,0:T(8,128)(2,1)S(1)}, u32[]{:S(2)}, u32[]{:S(2)}) collective-permute-start(bf16[32,1920]{1,0:T(8,128)(2,1)S(1)} %get-tuple-element.85), channel_id=1, source_target_pairs={{0,16},{2,18},{4,20},{6,22},{8,24},{10,26},{12,28},{14,30},{16,0},... | collective-permute-start | bytes 368648 | tf_op jit(solution)/shard_map/ppermute | solution.py:461
  53.8 11.3 %collective-permute-start.18 = (bf16[32,1920]{1,0:T(8,128)(2,1)S(1)}, bf16[32,1920]{1,0:T(8,128)(2,1)S(1)}, u32[]{:S(2)}, u32[]{:S(2)}) collective-permute-start(bf16[32,1920]{1,0:T(8,128)(2,1)S(1)} %get-tuple-element.86), channel_id=1, source_target_pairs={{0,24},{2,26},{4,28},{6,30},{8,16},{10,18},{12,20},{14,22},{16,8},... | collective-permute-start | bytes 368648 | tf_op jit(solution)/shard_map/ppermute | solution.py:461
  65.4 6.4 %copy-start.5 = (s32[2,192]{1,0:T(2,128)S(1)}, s32[2,192]{1,0:T(2,128)}, u32[]{:S(2)}) copy-start(s32[2,192]{1,0:T(2,128)} %get-tuple-element.99.pos_ref) | copy-start | bytes 4612
  65.4 6.4 %collective-permute-start.20 = (bf16[40,1920]{1,0:T(8,128)(2,1)S(1)}, bf16[40,1920]{1,0:T(8,128)(2,1)S(1)}, u32[]{:S(2)}, u32[]{:S(2)}) collective-permute-start(bf16[40,1920]{1,0:T(8,128)(2,1)S(1)} %get-tuple-element.97), channel_id=1, source_target_pairs={{0,1},{1,0},{2,3},{3,2},{4,5},{5,4},{6,7},{7,6},{8,9},{9,8},{10,11... | collective-permute-start | bytes 460808 | tf_op jit(solution)/shard_map/ppermute | solution.py:457
  65.9 5.2 %collective-permute-start.22 = (bf16[16,1920]{1,0:T(8,128)(2,1)S(1)}, bf16[16,1920]{1,0:T(8,128)(2,1)S(1)}, u32[]{:S(2)}, u32[]{:S(2)}) collective-permute-start(bf16[16,1920]{1,0:T(8,128)(2,1)S(1)} %get-tuple-element.98), channel_id=1, source_target_pairs={{0,5},{1,4},{2,7},{3,6},{4,1},{5,0},{6,3},{7,2},{8,13},{9,12},{10,... | collective-permute-start | bytes 184328 | tf_op jit(solution)/shard_map/ppermute | solution.py:457
  67.4 4.4 %collective-permute-start.21 = (bf16[16,1920]{1,0:T(8,128)(2,1)S(1)}, bf16[16,1920]{1,0:T(8,128)(2,1)S(1)}, u32[]{:S(2)}, u32[]{:S(2)}) collective-permute-start(bf16[16,1920]{1,0:T(8,128)(2,1)S(1)} %get-tuple-element.98), channel_id=1, source_target_pairs={{0,4},{1,5},{2,6},{3,7},{4,0},{5,1},{6,2},{7,3},{8,12},{9,13},{10,... | collective-permute-start | bytes 184328 | tf_op jit(solution)/shard_map/ppermute | solution.py:457

commit v3 on v2

--- a/solution.py
+++ b/solution.py
@@ -13,7 +13,8 @@
 HALF = HCAP // 2
 TAIL = 128
 CHUNK_BLOCK = 8
-COLD_BLOCK = 64
+GATHER_BLOCK = 112
+COLD_PART = 4 * CAP
 COLD_ROWS = 128
 UNIT_BLOCK = 128
 BF = jnp.bfloat16
@@ -94,7 +95,7 @@
 
 def dispatch_kernel(base, *refs):
     tok_ref, grad_ref, prob_ref, ids_ref, slot_ref, flags_ref, owner_ref = refs[:7]
-    gate_ref, up_ref, down_ref, pos_ref, weight_ref, *messages, cold_ref = refs[7:]
+    gate_ref, up_ref, down_ref, pos_ref, weight_ref, *messages, rows_ref = refs[7:]
     pair = lax.axis_index("pair")
     me = lax.axis_index("dp")
     z, x = me // 4, (me // 2) % 2
@@ -104,23 +105,22 @@
     weight_ref[...] = jnp.concatenate(joined, axis=0).astype(BF)
     prob = prob_ref[...].astype(F32)
 
-    def gather(out_ref, start, target, is_grad):
-        gather_rows(out_ref, start, target, is_grad, pos, prob, tok_ref, grad_ref)
-
-    row = iota((HCAP, tok_ref.shape[0]), 0)
-    target = base + HALF * pair + jnp.where(row >= HALF, row - HALF, row)
-    gather(messages[0], 0, target, row >= HALF)
-
     def block(start):
-        row = start + iota((COLD_BLOCK, tok_ref.shape[0]), 0)
-        chip = 2 * (z ^ (row >> 4)) + (x ^ ((row >> 3) & 1))
-        gather(cold_ref, start, chip * CAP + (row & 3), (row & 4) != 0)
-
-    each_block(cold_ref.shape[0], COLD_BLOCK, block)
+        row = start + iota((GATHER_BLOCK, tok_ref.shape[0]), 0)
+        hot = row < HCAP
+        cold_row = row - HCAP
+        chip = 2 * (z ^ (cold_row >> 4)) + (x ^ ((cold_row >> 3) & 1))
+        hot_target = base + HALF * pair + jnp.where(row >= HALF, row - HALF, row)
+        target = jnp.where(hot, hot_target, chip * CAP + (row & 3))
+        is_grad = (hot & (row >= HALF)) | (~hot & ((row & 4) != 0))
+        gather_rows(rows_ref, start, target, is_grad, pos, prob, tok_ref, grad_ref)
+
+    each_block(rows_ref.shape[0], GATHER_BLOCK, block)
     for k, message in enumerate(messages):
-        if k:
-            message[:HCAP, :] = messages[0][:HCAP, :]
-        message[HCAP:, :] = cold_ref[k * 16 : (k + 1) * 16, :]
+        rows = message.shape[0]
+        if rows > COLD_PART:
+            message[:HCAP, :] = rows_ref[:HCAP, :]
+        message[rows - COLD_PART :, :] = rows_ref[HCAP + k * COLD_PART : HCAP + (k + 1) * COLD_PART, :]
 
 
 def copy_kernel(*refs):
@@ -131,7 +131,7 @@
 
 def away_kernel(*refs):
     *messages, out_ref = refs
-    rows = [ref[HCAP:, :].astype(F32)[2 * CAP :] for ref in messages]
+    rows = [ref[ref.shape[0] - COLD_PART :, :].astype(F32)[2 * CAP :] for ref in messages]
     out_ref[...] = jnp.concatenate(rows, axis=0).astype(BF)
 
 
@@ -231,53 +231,42 @@
 
 def cold_kernel(message_count, *refs):
     messages = refs[:message_count]
-    mine_x_ref, other_x_ref, gate_hbm, up_hbm, down_hbm = refs[message_count : message_count + 5]
+    mine_x_ref, other_x_ref, gate_ref, up_ref, down_ref = refs[message_count : message_count + 5]
     own_ref, send_ref, *outs = refs[message_count + 5 : message_count + 10]
-    data_ref, dx_ref, w_ref, grad_ref, sum_ref, in_sem, out_sem = refs[message_count + 10 :]
-    total, units, width = data_ref.shape[0], gate_hbm.shape[1], gate_hbm.shape[2]
+    data_ref, dx_ref, grad_ref, sum_ref, out_sem = refs[message_count + 10 :]
+    total, width = data_ref.shape[0], gate_ref.shape[2]
     rows = COLD_ROWS
     single = rows == total
-    loads = [
-        pltpu.make_async_copy(ref.at[0], w_ref.at[pl.ds(j * units, units)], in_sem.at[j])
-        for j, ref in enumerate((gate_hbm, up_hbm, down_hbm))
-    ]
     stores = [
         pltpu.make_async_copy(grad_ref.at[j], ref.at[0], out_sem.at[j]) for j, ref in enumerate(outs)
     ]
-    for load in loads:
-        load.start()
     quarter = total // 4
     z_count = message_count // 2
     for flip, away_ref in enumerate((mine_x_ref, other_x_ref)):
-        near = [ref[HCAP:, :].astype(F32)[: 2 * CAP] for ref in messages[flip * z_count :][:z_count]]
+        near = [
+            ref[ref.shape[0] - COLD_PART :, :].astype(F32)[: 2 * CAP]
+            for ref in messages[flip * z_count :][:z_count]
+        ]
         start = 2 * flip * quarter
         data_ref[start : start + quarter, :] = jnp.concatenate(near, axis=0).astype(BF)
         data_ref[start + quarter : start + 2 * quarter, :] = away_ref[...]
     if not single:
         sum_ref[...] = jnp.zeros_like(sum_ref)
-        for load in loads:
-            load.wait()
-
-    def weight(j):
-        if single:
-            loads[j].wait()
-        return w_ref[j * units : (j + 1) * units, :]
 
     def block(start):
         at = pl.ds(start, rows)
         data = data_ref[at, :width]
         first = jnp.where((iota((8, TAIL), 0) == 0) & (iota((8, TAIL), 1) == 0), 1.0, 0.0)
         prob = dot(first.astype(BF), data_ref[at, width:], NT)[0:1, :]
-        pre_gate = dot(weight(0), data, NT)
-        pre_up = dot(weight(1), data, NT)
-        back = pltpu.roll(dot(weight(2), data, NT), rows - CAP, 1)
+        pre_gate = dot(gate_ref[0], data, NT)
+        pre_up = dot(up_ref[0], data, NT)
+        back = pltpu.roll(dot(down_ref[0], data, NT), rows - CAP, 1)
         gate_grad, up_grad, weighted, prob_term = swiglu_back(pre_gate, pre_up, back, prob)
         x_lane = (iota(pre_gate.shape, 1) & 4) == 0
         gate_grad = jnp.where(x_lane, gate_grad, 0.0)
         up_grad = jnp.where(x_lane, up_grad, 0.0)
         weighted = pltpu.roll(jnp.where(x_lane, weighted, 0.0), CAP, 1)
         grad_prob = jnp.sum(jnp.where(x_lane, prob_term, 0.0), axis=0, keepdims=True)
-        inner = jnp.concatenate([gate_grad, up_grad], axis=0).astype(BF)
         for j, grad in enumerate((gate_grad, up_grad, weighted)):
             term = dot(grad.astype(BF), data)
             if single:
@@ -288,7 +277,8 @@
         shape = (rows, rows // 2)
         row, col = iota(shape, 0), iota(shape, 1)
         pick = jnp.where(row == (col >> 2) * 8 + (col & 3), 1.0, 0.0).astype(BF)
-        dx = dot(dot(inner, pick).astype(BF), w_ref[: 2 * units, :], TN)
+        dx = dot(dot(gate_grad.astype(BF), pick).astype(BF), gate_ref[0], TN)
+        dx = dx + dot(dot(up_grad.astype(BF), pick).astype(BF), up_ref[0], TN)
         shape = (rows // 2, rows)
         row, col = iota(shape, 0), iota(shape, 1)
         pick = jnp.where(col == (row >> 2) * 8 + (row & 3), 1.0, 0.0).astype(BF)
@@ -400,18 +390,21 @@
         out_ref[...] = total[index * units : (index + 1) * units].astype(BF)
 
 
-def call(kernel, outs, name, scratch=(), smem=(), hbm=(), out_hbm=(), limit=0):
+def call(kernel, outs, name, scratch=(), smem=(), out_hbm=(), limit=0):
     def run(*args):
-        def space(index, far, smem=()):
-            return pltpu.SMEM if index in smem else pltpu.HBM if index in far else pltpu.VMEM
-
         moved = sum(a.size * a.dtype.itemsize for a in args)
         moved += sum(o.size * o.dtype.itemsize for o in outs)
         return pl.pallas_call(
             kernel,
             out_shape=outs,
-            in_specs=[pl.BlockSpec(memory_space=space(i, hbm, smem)) for i in range(len(args))],
-            out_specs=[pl.BlockSpec(memory_space=space(i, out_hbm)) for i in range(len(outs))],
+            in_specs=[
+                pl.BlockSpec(memory_space=pltpu.SMEM if i in smem else pltpu.VMEM)
+                for i in range(len(args))
+            ],
+            out_specs=[
+                pl.BlockSpec(memory_space=pltpu.HBM if i in out_hbm else pltpu.VMEM)
+                for i in range(len(outs))
+            ],
             scratch_shapes=[pltpu.VMEM(*s) if isinstance(s, tuple) else s for s in scratch],
             compiler_params=pltpu.CompilerParams(
                 vmem_limit_bytes=limit or min(VMEM_LIMIT, VMEM_BASE + 3 * moved // 2)
@@ -471,13 +464,15 @@
     hot_weights = [jnp.pad(w, ((0, pad), (0, 0))) if pad else w for w in (hot_gate, hot_up, hot_down)]
     units_padded = units + pad
     used = 3 * units_padded
-    cold_rows = z_count * 2 * 2 * CAP
-    message = shape((HCAP + 4 * CAP, lanes), BF)
+    cold_rows = z_count * COLD_PART
+    message = shape((HCAP + COLD_PART, lanes), BF)
+    by_relay = range(3, z_count, 2)
     pos, hot_own, *messages = call(
         functools.partial(dispatch_kernel, base),
-        [shape((TOP, token_count), jnp.int32), shape((used, width), BF)] + [message] * z_count,
+        [shape((TOP, token_count), jnp.int32), shape((used, width), BF)]
+        + [shape((COLD_PART, lanes), BF) if k in by_relay else message for k in range(z_count)],
         "dispatch",
-        scratch=[((cold_rows, lanes), BF)],
+        scratch=[((HCAP + cold_rows, lanes), BF)],
         smem=(5, 6),
         limit=VMEM_LIMIT,
     )(
@@ -502,7 +497,14 @@
     by_pair_out, first_out, hot_own = lax.optimization_barrier((by_pair, first_out, hot_own))
     weights = [hot_own, by_x, by_pair, swap(by_pair_out, 1)]
     (away,) = call(away_kernel, [shape((cold_rows // 2, lanes), BF)], "cold_away")(*chunks)
-    chunks = chunks + [other_core(first_out)] + [other_core(chunk) for chunk in chunks[1:]]
+    cold_chunks = list(chunks)
+    for k in by_relay:
+        chunks[k] = along_z(chunks[k - 1], 1)
+    other_chunks = [other_core(chunk) for chunk in chunks]
+    cold_chunks += [
+        other_core(cold_chunks[k]) if k in by_relay else other_chunks[k] for k in range(z_count)
+    ]
+    chunks = chunks + other_chunks
     cold_mine = swap(away, 1)
     cold_other = other_core(cold_mine)
 
@@ -538,15 +540,12 @@
         scratch=[
             ((2 * cold_rows, lanes), BF),
             ((cold_rows, lanes), F32),
-            ((3 * cold_units, width), BF),
             ((3, cold_units, width), BF),
             ((3, cold_units, width) if 2 * cold_rows > COLD_ROWS else (8, 128), F32),
             pltpu.SemaphoreType.DMA((3,)),
-            pltpu.SemaphoreType.DMA((3,)),
         ],
-        hbm=range(chunk_count + 2, chunk_count + 5),
         out_hbm=(2, 3, 4),
-    )(*chunks, cold_mine, cold_other, cold_gate, cold_up, cold_down)
+    )(*cold_chunks, cold_mine, cold_other, cold_gate, cold_up, cold_down)
 
     hot_got, cold_got = other_core(hot_dx_out), other_core(cold_out)
     part = (HALF + 2 * CAP, lanes)

time: 73.4 us -> 77.6 us (1.057)
  waiting for transfers between devices: 30.7 us -> 34.1 us
  starting transfers between devices: 25.6 us -> 27.6 us
  Pallas kernels: 14.2 us -> 12.9 us
    ppermute x10, waiting for transfers between devices: 3.46 us -> 14.5 us  [swap(): return lax.ppermute(value, ('dp', 'pair'), perm)]
    ppermute x6 -> x7, waiting for transfers between devices: 23.6 us -> 16.7 us  [along_z(): return lax.ppermute(value, 'dp', perm)]
    ppermute x6 -> x7, starting transfers between devices: 10.2 us -> 11.9 us  [along_z(): return lax.ppermute(value, 'dp', perm)]
    pallas_call x9, Pallas kernels: 14.2 us -> 12.9 us  [run(): pl.pallas_call(kernel, out_shape=outs, in_specs=[pl.BlockSpec(memory_spac...]
    ppermute x7 -> x8, waiting for transfers between devices: 3.66 us -> 2.9 us  [other_core(): return lax.ppermute(value, 'dp', [(i, i ^ 1) for i in range(count)])]
  transfers between devices with their start and end apart: 23 -> 25, of which waited for: 12 -> 12; matrix products, arithmetic and copies ran while one was open for 0% -> 0% of each run, Pallas kernels for 13% -> 11%
where the time goes in v3:
time: 77.6 us; the launch traced here: 77.3 us
  waiting for transfers between devices  34.1 us (44%)
  starting transfers between devices  27.6 us (36%)
  Pallas kernels  12.9 us (17%)
  local copies, waits for them, and re-layouts  1.98 us (3%)
    ppermute x7, waiting for transfers between devices, along_z(): return lax.ppermute(value, 'dp', perm)  16.7 us
    ppermute x10, starting transfers between devices, swap(): return lax.ppermute(value, ('dp', 'pair'), perm)  14.6 us
    ppermute x10, waiting for transfers between devices, swap(): return lax.ppermute(value, ('dp', 'pair'), perm)  14.5 us
    pallas_call x9, Pallas kernels, run(): pl.pallas_call(kernel, out_shape=outs, in_specs=[pl.BlockSpec(memory_spac...  12.9 us
    ppermute x7, starting transfers between devices, along_z(): return lax.ppermute(value, 'dp', perm)  11.9 us
    ppermute x8, waiting for transfers between devices, other_core(): return lax.ppermute(value, 'dp', [(i, i ^ 1) for i in range(count)])  2.9 us
    unnamed x12, local copies, waits for them, and re-layouts  1.98 us
  transfers between devices with their start and end apart: 25, of which 12 were waited for; matrix products, arithmetic and copies ran while one was open for 0% of the time, Pallas kernels for 11%

profile of v3, /device:TPU:0, one launch (start us, length us, event | category | flops | bytes accessed | tf_op | source)
XLA Modules:
  0.0 77.3 jit_solution(9733128651473155822)
XLA Ops:
  0.6 2.9 %dispatch.1 = (s32[2,192]{1,0:T(2,128)}, bf16[120,1792]{1,0:T(8,128)(2,1)}, bf16[64,1920]{1,0:T(8,128)(2,1)}, bf16[64,1920]{1,0:T(8,128)(2,1)}, bf16[64,1920]{1,0:T(8,128)(2,1)}, /*index=5*/bf16[16,1920]{1,0:T(8,128)(2,1)}) custom-call(bf16[192,1792]{1,0:T(8,128)(2,1)} %refs_0_.1, bf16[192,1792]{1,0:T(8,128)(2,1)} %refs_1_.1, bf16[2,192]{1,0:T(2,128)(2,1)} %bitcast.6, ...), custom_call_target="tpu_custom_call" | custom-call | flops 1024 | bytes 1024 | tf_op jit(solution)/shard_map/dispatch/pallas_call | solution.py:397
  3.5 3.0 %collective-permute-start.9 = (bf16[120,1792]{1,0:T(8,128)(2,1)}, bf16[120,1792]{1,0:T(8,128)(2,1)S(1)}, u32[]{:S(2)}, u32[]{:S(2)}) collective-permute-start(bf16[120,1792]{1,0:T(8,128)(2,1)} %get-tuple-element.61.refs_1_), channel_id=1, source_target_pairs={{0,1},{1,0},{2,3},{3,2},{4,5},{5,4},{6,7},{7,6},{8,9},{9,8},{10,11... | collective-permute-start | bytes 1290248 | tf_op jit(solution)/shard_map/ppermute | solution.py:450
  6.5 2.6 %collective-permute-start.1 = (bf16[64,1920]{1,0:T(8,128)(2,1)}, bf16[64,1920]{1,0:T(8,128)(2,1)S(1)}, u32[]{:S(2)}, u32[]{:S(2)}) collective-permute-start(bf16[64,1920]{1,0:T(8,128)(2,1)} %get-tuple-element.63), channel_id=1, source_target_pairs={{0,16},{2,18},{4,20},{6,22},{8,24},{10,26},{12,28},{14,30},{16,0},... | collective-permute-start | bytes 737288 | tf_op jit(solution)/shard_map/ppermute | solution.py:454
  9.1 1.6 %collective-permute-start = (bf16[64,1920]{1,0:T(8,128)(2,1)}, bf16[64,1920]{1,0:T(8,128)(2,1)S(1)}, u32[]{:S(2)}, u32[]{:S(2)}) collective-permute-start(bf16[64,1920]{1,0:T(8,128)(2,1)} %get-tuple-element.59), channel_id=1, source_target_pairs={{0,8},{2,10},{4,12},{6,14},{8,0},{10,2},{12,4},{14,6},{16,24},{18,... | collective-permute-start | bytes 737288 | tf_op jit(solution)/shard_map/ppermute | solution.py:454
  10.6 1.5 %collective-permute-start.10 = (bf16[120,1792]{1,0:T(8,128)(2,1)}, bf16[120,1792]{1,0:T(8,128)(2,1)S(1)}, u32[]{:S(2)}, u32[]{:S(2)}) collective-permute-start(bf16[120,1792]{1,0:T(8,128)(2,1)} %get-tuple-element.61.refs_1_), channel_id=1, source_target_pairs={{0,4},{1,5},{2,6},{3,7},{4,0},{5,1},{6,2},{7,3},{8,12},{9,13},{10,... | collective-permute-start | bytes 1290248 | tf_op jit(solution)/shard_map/ppermute | solution.py:450
  12.1 8.2 %collective-permute-done.1.refs_2_ = bf16[64,1920]{1,0:T(8,128)(2,1)S(1)} collective-permute-done((bf16[64,1920]{1,0:T(8,128)(2,1)}, bf16[64,1920]{1,0:T(8,128)(2,1)S(1)}, u32[]{:S(2)}, u32[]{:S(2)}) %collective-permute-start.1) | collective-permute-done | bytes 245792 | tf_op jit(solution)/shard_map/ppermute | solution.py:454
  20.4 0.7 collective-permute-start.4
  21.0 0.0 collective-permute-done.refs_1_
  21.0 1.0 %copy-done.3 = bf16[120,1792]{1,0:T(8,128)(2,1)S(1)} copy-done((bf16[120,1792]{1,0:T(8,128)(2,1)S(1)}, bf16[120,1792]{1,0:T(8,128)(2,1)}, u32[]{:S(2)}) %copy-start.3) | copy-done | bytes 430104
  22.1 0.9 %copy-done.4 = bf16[64,1920]{1,0:T(8,128)(2,1)S(1)} copy-done((bf16[64,1920]{1,0:T(8,128)(2,1)S(1)}, bf16[64,1920]{1,0:T(8,128)(2,1)}, u32[]{:S(2)}) %copy-start.4) | copy-done | bytes 245784
  23.0 0.0 collective-permute-done.9.refs_10_
  23.1 1.6 %collective-permute-start.11 = (bf16[120,1792]{1,0:T(8,128)(2,1)S(1)}, bf16[120,1792]{1,0:T(8,128)(2,1)S(1)}, u32[]{:S(2)}, u32[]{:S(2)}) collective-permute-start(bf16[120,1792]{1,0:T(8,128)(2,1)S(1)} %collective-permute-done.9.refs_10_), channel_id=1, source_target_pairs={{0,4},{1,5},{2,6},{3,7},{4,0},{5,1},{6,2},{7,3},{8,12},{9,13},{10,... | collective-permute-start | bytes 1290248 | tf_op jit(solution)/shard_map/ppermute | solution.py:450
  24.6 0.0 collective-permute-start.6
  24.6 2.7 %collective-permute-start.2 = (bf16[16,1920]{1,0:T(8,128)(2,1)}, bf16[16,1920]{1,0:T(8,128)(2,1)S(1)}, u32[]{:S(2)}, u32[]{:S(2)}) collective-permute-start(bf16[16,1920]{1,0:T(8,128)(2,1)} %get-tuple-element.64), channel_id=1, source_target_pairs={{0,24},{2,26},{4,28},{6,30},{8,16},{10,18},{12,20},{14,22},{16,8},... | collective-permute-start | bytes 184328 | tf_op jit(solution)/shard_map/ppermute | solution.py:454
  27.3 4.0 %collective-permute-done.2.refs_3_ = bf16[16,1920]{1,0:T(8,128)(2,1)S(1)} collective-permute-done((bf16[16,1920]{1,0:T(8,128)(2,1)}, bf16[16,1920]{1,0:T(8,128)(2,1)S(1)}, u32[]{:S(2)}, u32[]{:S(2)}) %collective-permute-start.2) | collective-permute-done | bytes 61472 | tf_op jit(solution)/shard_map/ppermute | solution.py:454
  31.3 0.0 collective-permute-start.5
  31.3 0.0 collective-permute-done.10.refs_9_
  31.3 0.5 collective-permute-start.7
  31.8 0.0 collective-permute-done.4.refs_3_
  31.8 0.1 collective-permute-start.8
  31.9 0.0 copy-start
  31.9 0.0 copy-start.1
  31.9 0.0 copy-start.2
  31.9 0.0 collective-permute-done.6.refs_5_
  31.9 1.4 %collective-permute-start.3 = (bf16[32,1920]{1,0:T(8,128)(2,1)S(1)}, bf16[32,1920]{1,0:T(8,128)(2,1)S(1)}, u32[]{:S(2)}, u32[]{:S(2)}) collective-permute-start(bf16[32,1920]{1,0:T(8,128)(2,1)S(1)} %cold_away.1), channel_id=1, source_target_pairs={{0,4},{1,5},{2,6},{3,7},{4,0},{5,1},{6,2},{7,3},{8,12},{9,13},{10,... | collective-permute-start | bytes 368648 | tf_op jit(solution)/shard_map/ppermute | solution.py:450
  33.4 0.0 collective-permute-done.7.refs_6_
  33.4 0.0 collective-permute-done.5.refs_4_
  33.4 0.1 collective-permute-done.8.refs_7_
  33.5 1.1 %collective-permute-done.11.refs_11_ = bf16[120,1792]{1,0:T(8,128)(2,1)S(1)} collective-permute-done((bf16[120,1792]{1,0:T(8,128)(2,1)S(1)}, bf16[120,1792]{1,0:T(8,128)(2,1)S(1)}, u32[]{:S(2)}, u32[]{:S(2)}) %collective-permute-start.11) | collective-permute-done | bytes 430112 | tf_op jit(solution)/shard_map/ppermute | solution.py:450
  34.7 2.7 %hot.1 = (f32[96,1920]{1,0:T(8,128)S(1)}, bf16[96,1920]{1,0:T(8,128)(2,1)S(1)}, f32[120,1792]{1,0:T(8,128)S(1)}, bf16[120,1792]{1,0:T(8,128)(2,1)S(1)}, bf16[120...) custom-call(bf16[64,1920]{1,0:T(8,128)(2,1)S(1)} %get-tuple-element.62.refs_0_, ...), custom_call_target="tpu_custom_call" | custom-call | flops 1024 | bytes 1024 | tf_op jit(solution)/shard_map/hot/pallas_call | solution.py:397
  37.4 0.3 collective-permute-done.3.refs_8_
  37.7 1.4 %collective-permute-start.16 = (bf16[120,1792]{1,0:T(8,128)(2,1)S(1)}, bf16[120,1792]{1,0:T(8,128)(2,1)S(1)}, u32[]{:S(2)}, u32[]{:S(2)}) collective-permute-start(bf16[120,1792]{1,0:T(8,128)(2,1)S(1)} %get-tuple-element.79), channel_id=1, source_target_pairs={{0,4},{1,5},{2,6},{3,7},{4,0},{5,1},{6,2},{7,3},{8,12},{9,13},{10,... | collective-permute-start | bytes 1290248 | tf_op jit(solution)/shard_map/ppermute | solution.py:450
  39.1 0.5 collective-permute-start.17
  39.6 0.0 collective-permute-start.12
  39.6 0.5 collective-permute-start.14
  40.1 0.0 collective-permute-start.13
  40.1 1.4 %collective-permute-done.13.refs_7_ = bf16[16,1920]{1,0:T(8,128)(2,1)S(1)} collective-permute-done((bf16[16,1920]{1,0:T(8,128)(2,1)S(1)}, bf16[16,1920]{1,0:T(8,128)(2,1)S(1)}, u32[]{:S(2)}, u32[]{:S(2)}) %collective-permute-start.13) | collective-permute-done | bytes 61472 | tf_op jit(solution)/shard_map/ppermute | solution.py:462
  41.5 0.0 collective-permute-done.14.refs_9_
  41.5 0.0 copy-done
  41.5 0.0 copy-done.1
  41.5 4.4 %cold.1 = (f32[32,1920]{1,0:T(8,128)S(1)}, bf16[32,1920]{1,0:T(8,128)(2,1)S(1)}, bf16[1,320,1792]{2,1,0:T(8,128)(2,1)}, bf16[1,320,1792]{2,1,0:T(8,128)(2,1)}, bf16[1,320,1792]{2,1,0:T(8,128)(2,1)}) custom-call(bf16[64,1920]{1,0:T(8,128)(2,1)S(1)} %get-tuple-element.62.refs_0_, bf16[64,1920]{1,0:T(8,128)(2,1)S(1)} %collective-permute-done.refs_1_, ...), custom_call_target="tpu_custom_call" | custom-call | flops 1024 | bytes 1024 | tf_op jit(solution)/shard_map/cold/pallas_call | solution.py:397
  45.9 1.7 %collective-permute-start.21 = (bf16[120,1792]{1,0:T(8,128)(2,1)S(1)}, bf16[120,1792]{1,0:T(8,128)(2,1)S(1)}, u32[]{:S(2)}, u32[]{:S(2)}) collective-permute-start(bf16[120,1792]{1,0:T(8,128)(2,1)S(1)} %get-tuple-element.90), channel_id=1, source_target_pairs={{0,5},{1,4},{2,7},{3,6},{4,1},{5,0},{6,3},{7,2},{8,13},{9,12},{10,... | collective-permute-start | bytes 1290248 | tf_op jit(solution)/shard_map/ppermute | solution.py:450
  47.6 0.0 collective-permute-start.15
  47.6 1.3 %collective-permute-done.15.cold_got_ref = bf16[32,1920]{1,0:T(8,128)(2,1)S(1)} collective-permute-done((bf16[32,1920]{1,0:T(8,128)(2,1)S(1)}, bf16[32,1920]{1,0:T(8,128)(2,1)S(1)}, u32[]{:S(2)}, u32[]{:S(2)}) %collective-permute-start.15) | collective-permute-done | bytes 122912 | tf_op jit(solution)/shard_map/ppermute | solution.py:462
  48.9 0.0 collective-permute-done.12.hot_got_ref
  48.9 0.3 add_cores.1
  49.2 0.0 collective-permute-done.16.a_ref
  49.2 10.2 %collective-permute-done.17.b_ref = bf16[120,1792]{1,0:T(8,128)(2,1)S(1)} collective-permute-done((bf16[120,1792]{1,0:T(8,128)(2,1)S(1)}, bf16[120,1792]{1,0:T(8,128)(2,1)S(1)}, u32[]{:S(2)}, u32[]{:S(2)}) %collective-permute-start.17) | collective-permute-done | bytes 430112 | tf_op jit(solution)/shard_map/ppermute | solution.py:450
  59.5 0.5 collective-permute-start.18
  59.9 0.0 collective-permute-start.19
  59.9 3.9 %collective-permute-start.20 = (bf16[32,1920]{1,0:T(8,128)(2,1)S(1)}, bf16[32,1920]{1,0:T(8,128)(2,1)S(1)}, u32[]{:S(2)}, u32[]{:S(2)}) collective-permute-start(bf16[32,1920]{1,0:T(8,128)(2,1)S(1)} %get-tuple-element.84), channel_id=1, source_target_pairs={{0,24},{2,26},{4,28},{6,30},{8,16},{10,18},{12,20},{14,22},{16,8},... | collective-permute-start | bytes 368648 | tf_op jit(solution)/shard_map/ppermute | solution.py:454
  63.9 0.5 collective-permute-done.18.refs_1_
  64.3 4.0 %collective-permute-done.19.refs_2_ = bf16[32,1920]{1,0:T(8,128)(2,1)S(1)} collective-permute-done((bf16[32,1920]{1,0:T(8,128)(2,1)S(1)}, bf16[32,1920]{1,0:T(8,128)(2,1)S(1)}, u32[]{:S(2)}, u32[]{:S(2)}) %collective-permute-start.19) | collective-permute-done | bytes 122912 | tf_op jit(solution)/shard_map/ppermute | solution.py:454
  68.3 0.0 collective-permute-done.20.refs_3_
  68.3 0.3 combine.1
  68.6 0.1 collective-permute-start.22
  68.7 3.0 %collective-permute-start.24 = (bf16[16,1920]{1,0:T(8,128)(2,1)S(1)}, bf16[16,1920]{1,0:T(8,128)(2,1)S(1)}, u32[]{:S(2)}, u32[]{:S(2)}) collective-permute-start(bf16[16,1920]{1,0:T(8,128)(2,1)S(1)} %get-tuple-element.96), channel_id=1, source_target_pairs={{0,5},{1,4},{2,7},{3,6},{4,1},{5,0},{6,3},{7,2},{8,13},{9,12},{10,... | collective-permute-start | bytes 184328 | tf_op jit(solution)/shard_map/ppermute | solution.py:450
  71.7 0.5 collective-permute-start.23
  72.2 0.0 collective-permute-done.21.c_ref
  72.2 0.9 %hot_sum.1 = (bf16[40,1792]{1,0:T(8,128)(2,1)}, bf16[40,1792]{1,0:T(8,128)(2,1)}, bf16[40,1792]{1,0:T(8,128)(2,1)}) custom-call(f32[120,1792]{1,0:T(8,128)S(1)} %get-tuple-element.86.own_ref, bf16[120,1792]{1,0:T(8,128)(2,1)S(1)} %collective-permute-done.16.a_ref, bf16[120,1792]{1,0:T(8,128)(2,1)S(1)} %collective-permute-done.17.b_ref, ...), custom_call_target="tpu_custom_call" | custom-call | flops 1024 | bytes 1024 | tf_op jit(solution)/shard_map/hot_sum/pallas_call | solution.py:397
  73.1 0.9 %collective-permute-done.24.xy_ref = bf16[16,1920]{1,0:T(8,128)(2,1)S(1)} collective-permute-done((bf16[16,1920]{1,0:T(8,128)(2,1)S(1)}, bf16[16,1920]{1,0:T(8,128)(2,1)S(1)}, u32[]{:S(2)}, u32[]{:S(2)}) %collective-permute-start.24) | collective-permute-done | bytes 61472 | tf_op jit(solution)/shard_map/ppermute | solution.py:450
  74.0 1.9 %collective-permute-done.23.x_ref = bf16[16,1920]{1,0:T(8,128)(2,1)S(1)} collective-permute-done((bf16[16,1920]{1,0:T(8,128)(2,1)S(1)}, bf16[16,1920]{1,0:T(8,128)(2,1)S(1)}, u32[]{:S(2)}, u32[]{:S(2)}) %collective-permute-start.23) | collective-permute-done | bytes 61472 | tf_op jit(solution)/shard_map/ppermute | solution.py:450
  75.9 0.0 collective-permute-done.22.y_ref
  75.9 1.4 %finish.1 = (bf16[96,1792]{1,0:T(8,128)(2,1)}, f32[2,96]{1,0:T(2,128)}) custom-call(f32[40,1920]{1,0:T(8,128)S(1)} %get-tuple-element.94.own_ref, bf16[40,1920]{1,0:T(8,128)(2,1)S(1)} %collective-permute-done.22.y_ref, bf16[16,1920]{1,0:T(8,128)(2,1)S(1)} %collective-permute-done.23.x_ref, bf16[16,1920]{1,0:T(8,128)(2,1)S(1)} %collective-permute-done.24.xy_ref, ...), custom_call_target="tpu_custom_call" | custom-call | flops 1024 | bytes 1024 | tf_op jit(solution)/shard_map/finish/pallas_call | solution.py:397
  (7 shorter events, 0.1 us)
Async XLA Ops:
  3.5 19.6 %collective-permute-start.9 = (bf16[120,1792]{1,0:T(8,128)(2,1)}, bf16[120,1792]{1,0:T(8,128)(2,1)S(1)}, u32[]{:S(2)}, u32[]{:S(2)}) collective-permute-start(bf16[120,1792]{1,0:T(8,128)(2,1)} %get-tuple-element.61.refs_1_), channel_id=1, source_target_pairs={{0,1},{1,0},{2,3},{3,2},{4,5},{5,4},{6,7},{7,6},{8,9},{9,8},{10,11... | collective-permute-start | bytes 1290248 | tf_op jit(solution)/shard_map/ppermute | solution.py:450
  6.5 13.9 %collective-permute-start.1 = (bf16[64,1920]{1,0:T(8,128)(2,1)}, bf16[64,1920]{1,0:T(8,128)(2,1)S(1)}, u32[]{:S(2)}, u32[]{:S(2)}) collective-permute-start(bf16[64,1920]{1,0:T(8,128)(2,1)} %get-tuple-element.63), channel_id=1, source_target_pairs={{0,16},{2,18},{4,20},{6,22},{8,24},{10,26},{12,28},{14,30},{16,0},... | collective-permute-start | bytes 737288 | tf_op jit(solution)/shard_map/ppermute | solution.py:454
  9.1 12.0 %collective-permute-start = (bf16[64,1920]{1,0:T(8,128)(2,1)}, bf16[64,1920]{1,0:T(8,128)(2,1)S(1)}, u32[]{:S(2)}, u32[]{:S(2)}) collective-permute-start(bf16[64,1920]{1,0:T(8,128)(2,1)} %get-tuple-element.59), channel_id=1, source_target_pairs={{0,8},{2,10},{4,12},{6,14},{8,0},{10,2},{12,4},{14,6},{16,24},{18,... | collective-permute-start | bytes 737288 | tf_op jit(solution)/shard_map/ppermute | solution.py:454
  10.6 20.7 %collective-permute-start.10 = (bf16[120,1792]{1,0:T(8,128)(2,1)}, bf16[120,1792]{1,0:T(8,128)(2,1)S(1)}, u32[]{:S(2)}, u32[]{:S(2)}) collective-permute-start(bf16[120,1792]{1,0:T(8,128)(2,1)} %get-tuple-element.61.refs_1_), channel_id=1, source_target_pairs={{0,4},{1,5},{2,6},{3,7},{4,0},{5,1},{6,2},{7,3},{8,12},{9,13},{10,... | collective-permute-start | bytes 1290248 | tf_op jit(solution)/shard_map/ppermute | solution.py:450
  20.4 11.5 %collective-permute-start.4 = (bf16[64,1920]{1,0:T(8,128)(2,1)S(1)}, bf16[64,1920]{1,0:T(8,128)(2,1)S(1)}, u32[]{:S(2)}, u32[]{:S(2)}) collective-permute-start(bf16[64,1920]{1,0:T(8,128)(2,1)S(1)} %collective-permute-done.1.refs_2_), channel_id=1, source_target_pairs={{0,8},{2,10},{4,12},{6,14},{8,0},{10,2},{12,4},{14,6},{16,24},{18,... | collective-permute-start | bytes 737288 | tf_op jit(solution)/shard_map/ppermute | solution.py:454
  21.0 1.0 %copy-start.3 = (bf16[120,1792]{1,0:T(8,128)(2,1)S(1)}, bf16[120,1792]{1,0:T(8,128)(2,1)}, u32[]{:S(2)}) copy-start(bf16[120,1792]{1,0:T(8,128)(2,1)} %get-tuple-element.61.refs_1_) | copy-start | bytes 1290244
  22.0 0.9 %copy-start.4 = (bf16[64,1920]{1,0:T(8,128)(2,1)S(1)}, bf16[64,1920]{1,0:T(8,128)(2,1)}, u32[]{:S(2)}) copy-start(bf16[64,1920]{1,0:T(8,128)(2,1)} %get-tuple-element.60.refs_0_) | copy-start | bytes 737284
  23.1 11.6 %collective-permute-start.11 = (bf16[120,1792]{1,0:T(8,128)(2,1)S(1)}, bf16[120,1792]{1,0:T(8,128)(2,1)S(1)}, u32[]{:S(2)}, u32[]{:S(2)}) collective-permute-start(bf16[120,1792]{1,0:T(8,128)(2,1)S(1)} %collective-permute-done.9.refs_10_), channel_id=1, source_target_pairs={{0,4},{1,5},{2,6},{3,7},{4,0},{5,1},{6,2},{7,3},{8,12},{9,13},{10,... | collective-permute-start | bytes 1290248 | tf_op jit(solution)/shard_map/ppermute | solution.py:450
  24.6 7.3 %collective-permute-start.6 = (bf16[64,1920]{1,0:T(8,128)(2,1)S(1)}, bf16[64,1920]{1,0:T(8,128)(2,1)S(1)}, u32[]{:S(2)}, u32[]{:S(2)}) collective-permute-start(bf16[64,1920]{1,0:T(8,128)(2,1)S(1)} %collective-permute-done.refs_1_), channel_id=1, source_target_pairs={{0,2},{2,0},{4,6},{6,4},{8,10},{10,8},{12,14},{14,12},{16,18},{18,... | collective-permute-start | bytes 737288 | tf_op jit(solution)/shard_map/ppermute | solution.py:462
  24.6 6.7 %collective-permute-start.2 = (bf16[16,1920]{1,0:T(8,128)(2,1)}, bf16[16,1920]{1,0:T(8,128)(2,1)S(1)}, u32[]{:S(2)}, u32[]{:S(2)}) collective-permute-start(bf16[16,1920]{1,0:T(8,128)(2,1)} %get-tuple-element.64), channel_id=1, source_target_pairs={{0,24},{2,26},{4,28},{6,30},{8,16},{10,18},{12,20},{14,22},{16,8},... | collective-permute-start | bytes 184328 | tf_op jit(solution)/shard_map/ppermute | solution.py:454
  31.3 2.1 %collective-permute-start.5 = (bf16[64,1920]{1,0:T(8,128)(2,1)S(1)}, bf16[64,1920]{1,0:T(8,128)(2,1)S(1)}, u32[]{:S(2)}, u32[]{:S(2)}) collective-permute-start(bf16[64,1920]{1,0:T(8,128)(2,1)S(1)} %get-tuple-element.62.refs_0_), channel_id=1, source_target_pairs={{0,2},{2,0},{4,6},{6,4},{8,10},{10,8},{12,14},{14,12},{16,18},{18,... | collective-permute-start | bytes 737288 | tf_op jit(solution)/shard_map/ppermute | solution.py:462
  31.3 2.1 %collective-permute-start.7 = (bf16[64,1920]{1,0:T(8,128)(2,1)S(1)}, bf16[64,1920]{1,0:T(8,128)(2,1)S(1)}, u32[]{:S(2)}, u32[]{:S(2)}) collective-permute-start(bf16[64,1920]{1,0:T(8,128)(2,1)S(1)} %collective-permute-done.1.refs_2_), channel_id=1, source_target_pairs={{0,2},{2,0},{4,6},{6,4},{8,10},{10,8},{12,14},{14,12},{16,18},{18,... | collective-permute-start | bytes 737288 | tf_op jit(solution)/shard_map/ppermute | solution.py:462
  31.8 1.7 %collective-permute-start.8 = (bf16[64,1920]{1,0:T(8,128)(2,1)S(1)}, bf16[64,1920]{1,0:T(8,128)(2,1)S(1)}, u32[]{:S(2)}, u32[]{:S(2)}) collective-permute-start(bf16[64,1920]{1,0:T(8,128)(2,1)S(1)} %collective-permute-done.4.refs_3_), channel_id=1, source_target_pairs={{0,2},{2,0},{4,6},{6,4},{8,10},{10,8},{12,14},{14,12},{16,18},{18,... | collective-permute-start | bytes 737288 | tf_op jit(solution)/shard_map/ppermute | solution.py:462
  31.9 9.6 %copy-start = (bf16[1,320,1792]{2,1,0:T(8,128)(2,1)S(1)}, bf16[1,320,1792]{2,1,0:T(8,128)(2,1)}, u32[]{:S(2)}) copy-start(bf16[1,320,1792]{2,1,0:T(8,128)(2,1)} %refs_10_.1) | copy-start | bytes 3440644
  31.9 9.6 %copy-start.1 = (bf16[1,320,1792]{2,1,0:T(8,128)(2,1)S(1)}, bf16[1,320,1792]{2,1,0:T(8,128)(2,1)}, u32[]{:S(2)}) copy-start(bf16[1,320,1792]{2,1,0:T(8,128)(2,1)} %refs_11_.1) | copy-start | bytes 3440644
  31.9 9.6 %copy-start.2 = (bf16[1,320,1792]{2,1,0:T(8,128)(2,1)S(1)}, bf16[1,320,1792]{2,1,0:T(8,128)(2,1)}, u32[]{:S(2)}) copy-start(bf16[1,320,1792]{2,1,0:T(8,128)(2,1)} %refs_12_.1) | copy-start | bytes 3440644
  31.9 5.7 %collective-permute-start.3 = (bf16[32,1920]{1,0:T(8,128)(2,1)S(1)}, bf16[32,1920]{1,0:T(8,128)(2,1)S(1)}, u32[]{:S(2)}, u32[]{:S(2)}) collective-permute-start(bf16[32,1920]{1,0:T(8,128)(2,1)S(1)} %cold_away.1), channel_id=1, source_target_pairs={{0,4},{1,5},{2,6},{3,7},{4,0},{5,1},{6,2},{7,3},{8,12},{9,13},{10,... | collective-permute-start | bytes 368648 | tf_op jit(solution)/shard_map/ppermute | solution.py:450
  37.7 11.5 %collective-permute-start.16 = (bf16[120,1792]{1,0:T(8,128)(2,1)S(1)}, bf16[120,1792]{1,0:T(8,128)(2,1)S(1)}, u32[]{:S(2)}, u32[]{:S(2)}) collective-permute-start(bf16[120,1792]{1,0:T(8,128)(2,1)S(1)} %get-tuple-element.79), channel_id=1, source_target_pairs={{0,4},{1,5},{2,6},{3,7},{4,0},{5,1},{6,2},{7,3},{8,12},{9,13},{10,... | collective-permute-start | bytes 1290248 | tf_op jit(solution)/shard_map/ppermute | solution.py:450
  39.1 20.4 %collective-permute-start.17 = (bf16[120,1792]{1,0:T(8,128)(2,1)S(1)}, bf16[120,1792]{1,0:T(8,128)(2,1)S(1)}, u32[]{:S(2)}, u32[]{:S(2)}) collective-permute-start(bf16[120,1792]{1,0:T(8,128)(2,1)S(1)} %get-tuple-element.80), channel_id=1, source_target_pairs={{0,1},{1,0},{2,3},{3,2},{4,5},{5,4},{6,7},{7,6},{8,9},{9,8},{10,11... | collective-permute-start | bytes 1290248 | tf_op jit(solution)/shard_map/ppermute | solution.py:450
  39.6 9.4 %collective-permute-start.12 = (bf16[96,1920]{1,0:T(8,128)(2,1)S(1)}, bf16[96,1920]{1,0:T(8,128)(2,1)S(1)}, u32[]{:S(2)}, u32[]{:S(2)}) collective-permute-start(bf16[96,1920]{1,0:T(8,128)(2,1)S(1)} %get-tuple-element.70), channel_id=1, source_target_pairs={{0,2},{2,0},{4,6},{6,4},{8,10},{10,8},{12,14},{14,12},{16,18},{18,... | collective-permute-start | bytes 1105928 | tf_op jit(solution)/shard_map/ppermute | solution.py:462
  39.6 2.0 %collective-permute-start.14 = (bf16[32,1920]{1,0:T(8,128)(2,1)S(1)}, bf16[32,1920]{1,0:T(8,128)(2,1)S(1)}, u32[]{:S(2)}, u32[]{:S(2)}) collective-permute-start(bf16[32,1920]{1,0:T(8,128)(2,1)S(1)} %collective-permute-done.3.refs_8_), channel_id=1, source_target_pairs={{0,2},{2,0},{4,6},{6,4},{8,10},{10,8},{12,14},{14,12},{16,18},{18,... | collective-permute-start | bytes 368648 | tf_op jit(solution)/shard_map/ppermute | solution.py:462
  40.1 1.4 %collective-permute-start.13 = (bf16[16,1920]{1,0:T(8,128)(2,1)S(1)}, bf16[16,1920]{1,0:T(8,128)(2,1)S(1)}, u32[]{:S(2)}, u32[]{:S(2)}) collective-permute-start(bf16[16,1920]{1,0:T(8,128)(2,1)S(1)} %collective-permute-done.2.refs_3_), channel_id=1, source_target_pairs={{0,2},{2,0},{4,6},{6,4},{8,10},{10,8},{12,14},{14,12},{16,18},{18,... | collective-permute-start | bytes 184328 | tf_op jit(solution)/shard_map/ppermute | solution.py:462
  45.9 26.2 %collective-permute-start.21 = (bf16[120,1792]{1,0:T(8,128)(2,1)S(1)}, bf16[120,1792]{1,0:T(8,128)(2,1)S(1)}, u32[]{:S(2)}, u32[]{:S(2)}) collective-permute-start(bf16[120,1792]{1,0:T(8,128)(2,1)S(1)} %get-tuple-element.90), channel_id=1, source_target_pairs={{0,5},{1,4},{2,7},{3,6},{4,1},{5,0},{6,3},{7,2},{8,13},{9,12},{10,... | collective-permute-start | bytes 1290248 | tf_op jit(solution)/shard_map/ppermute | solution.py:450
  47.6 1.3 %collective-permute-start.15 = (bf16[32,1920]{1,0:T(8,128)(2,1)S(1)}, bf16[32,1920]{1,0:T(8,128)(2,1)S(1)}, u32[]{:S(2)}, u32[]{:S(2)}) collective-permute-start(bf16[32,1920]{1,0:T(8,128)(2,1)S(1)} %get-tuple-element.73), channel_id=1, source_target_pairs={{0,2},{2,0},{4,6},{6,4},{8,10},{10,8},{12,14},{14,12},{16,18},{18,... | collective-permute-start | bytes 368648 | tf_op jit(solution)/shard_map/ppermute | solution.py:462
  59.5 4.9 %collective-permute-start.18 = (bf16[32,1920]{1,0:T(8,128)(2,1)S(1)}, bf16[32,1920]{1,0:T(8,128)(2,1)S(1)}, u32[]{:S(2)}, u32[]{:S(2)}) collective-permute-start(bf16[32,1920]{1,0:T(8,128)(2,1)S(1)} %get-tuple-element.82), channel_id=1, source_target_pairs={{0,8},{2,10},{4,12},{6,14},{8,0},{10,2},{12,4},{14,6},{16,24},{18,... | collective-permute-start | bytes 368648 | tf_op jit(solution)/shard_map/ppermute | solution.py:454
  59.9 8.4 %collective-permute-start.19 = (bf16[32,1920]{1,0:T(8,128)(2,1)S(1)}, bf16[32,1920]{1,0:T(8,128)(2,1)S(1)}, u32[]{:S(2)}, u32[]{:S(2)}) collective-permute-start(bf16[32,1920]{1,0:T(8,128)(2,1)S(1)} %get-tuple-element.83), channel_id=1, source_target_pairs={{0,16},{2,18},{4,20},{6,22},{8,24},{10,26},{12,28},{14,30},{16,0},... | collective-permute-start | bytes 368648 | tf_op jit(solution)/shard_map/ppermute | solution.py:454
  59.9 8.4 %collective-permute-start.20 = (bf16[32,1920]{1,0:T(8,128)(2,1)S(1)}, bf16[32,1920]{1,0:T(8,128)(2,1)S(1)}, u32[]{:S(2)}, u32[]{:S(2)}) collective-permute-start(bf16[32,1920]{1,0:T(8,128)(2,1)S(1)} %get-tuple-element.84), channel_id=1, source_target_pairs={{0,24},{2,26},{4,28},{6,30},{8,16},{10,18},{12,20},{14,22},{16,8},... | collective-permute-start | bytes 368648 | tf_op jit(solution)/shard_map/ppermute | solution.py:454
  68.6 7.3 %copy-start.5 = (s32[2,192]{1,0:T(2,128)S(1)}, s32[2,192]{1,0:T(2,128)}, u32[]{:S(2)}) copy-start(s32[2,192]{1,0:T(2,128)} %get-tuple-element.97.pos_ref) | copy-start | bytes 4612
  68.6 7.3 %collective-permute-start.22 = (bf16[40,1920]{1,0:T(8,128)(2,1)S(1)}, bf16[40,1920]{1,0:T(8,128)(2,1)S(1)}, u32[]{:S(2)}, u32[]{:S(2)}) collective-permute-start(bf16[40,1920]{1,0:T(8,128)(2,1)S(1)} %get-tuple-element.95), channel_id=1, source_target_pairs={{0,1},{1,0},{2,3},{3,2},{4,5},{5,4},{6,7},{7,6},{8,9},{9,8},{10,11... | collective-permute-start | bytes 460808 | tf_op jit(solution)/shard_map/ppermute | solution.py:450
  68.7 5.3 %collective-permute-start.24 = (bf16[16,1920]{1,0:T(8,128)(2,1)S(1)}, bf16[16,1920]{1,0:T(8,128)(2,1)S(1)}, u32[]{:S(2)}, u32[]{:S(2)}) collective-permute-start(bf16[16,1920]{1,0:T(8,128)(2,1)S(1)} %get-tuple-element.96), channel_id=1, source_target_pairs={{0,5},{1,4},{2,7},{3,6},{4,1},{5,0},{6,3},{7,2},{8,13},{9,12},{10,... | collective-permute-start | bytes 184328 | tf_op jit(solution)/shard_map/ppermute | solution.py:450
  71.7 4.2 %collective-permute-start.23 = (bf16[16,1920]{1,0:T(8,128)(2,1)S(1)}, bf16[16,1920]{1,0:T(8,128)(2,1)S(1)}, u32[]{:S(2)}, u32[]{:S(2)}) collective-permute-start(bf16[16,1920]{1,0:T(8,128)(2,1)S(1)} %get-tuple-element.96), channel_id=1, source_target_pairs={{0,4},{1,5},{2,6},{3,7},{4,0},{5,1},{6,2},{7,3},{8,12},{9,13},{10,... | collective-permute-start | bytes 184328 | tf_op jit(solution)/shard_map/ppermute | solution.py:450

commit v4 on v3

--- a/solution.py
+++ b/solution.py
@@ -15,6 +15,7 @@
 CHUNK_BLOCK = 8
 GATHER_BLOCK = 112
 COLD_PART = 4 * CAP
+MESSAGE = HCAP + COLD_PART
 COLD_ROWS = 128
 UNIT_BLOCK = 128
 BF = jnp.bfloat16
@@ -116,11 +117,11 @@
         gather_rows(rows_ref, start, target, is_grad, pos, prob, tok_ref, grad_ref)
 
     each_block(rows_ref.shape[0], GATHER_BLOCK, block)
-    for k, message in enumerate(messages):
-        rows = message.shape[0]
-        if rows > COLD_PART:
-            message[:HCAP, :] = rows_ref[:HCAP, :]
-        message[rows - COLD_PART :, :] = rows_ref[HCAP + k * COLD_PART : HCAP + (k + 1) * COLD_PART, :]
+    for message, k in zip(messages, [0, 1] + list(range(2, 2 * len(messages) - 2, 2))):
+        message[:COLD_PART, :] = rows_ref[HCAP + k * COLD_PART : HCAP + (k + 1) * COLD_PART, :]
+        message[COLD_PART:MESSAGE, :] = rows_ref[:HCAP, :]
+        if k > 1:
+            message[MESSAGE:, :] = rows_ref[HCAP + (k + 1) * COLD_PART : HCAP + (k + 2) * COLD_PART, :]
 
 
 def copy_kernel(*refs):
@@ -129,9 +130,14 @@
         out_ref[...] = in_ref[...]
 
 
+def relay_kernel(in_ref, out_ref):
+    out_ref[:COLD_PART, :] = in_ref[MESSAGE:, :]
+    out_ref[COLD_PART:, :] = in_ref[COLD_PART:MESSAGE, :]
+
+
 def away_kernel(*refs):
     *messages, out_ref = refs
-    rows = [ref[ref.shape[0] - COLD_PART :, :].astype(F32)[2 * CAP :] for ref in messages]
+    rows = [ref[:COLD_PART, :].astype(F32)[2 * CAP :] for ref in messages]
     out_ref[...] = jnp.concatenate(rows, axis=0).astype(BF)
 
 
@@ -164,8 +170,8 @@
     rows_ref, tail_ref, wide_ref, sum_ref = refs[chunk_count + 10 :]
     width = rows_ref.shape[1]
     for k, chunk in enumerate(chunks):
-        rows_ref[k * HCAP : (k + 1) * HCAP, :] = chunk[:HCAP, :width]
-        tail_ref[k * HCAP : (k + 1) * HCAP, :] = chunk[:HCAP, width:]
+        rows_ref[k * HCAP : (k + 1) * HCAP, :] = chunk[COLD_PART:MESSAGE, :width]
+        tail_ref[k * HCAP : (k + 1) * HCAP, :] = chunk[COLD_PART:MESSAGE, width:]
     used = 3 * units
     for j, w_ref in enumerate(weights):
         start = j * UNIT_BLOCK
@@ -244,7 +250,7 @@
     z_count = message_count // 2
     for flip, away_ref in enumerate((mine_x_ref, other_x_ref)):
         near = [
-            ref[ref.shape[0] - COLD_PART :, :].astype(F32)[: 2 * CAP]
+            ref[:COLD_PART, :].astype(F32)[: 2 * CAP]
             for ref in messages[flip * z_count :][:z_count]
         ]
         start = 2 * flip * quarter
@@ -465,12 +471,13 @@
     units_padded = units + pad
     used = 3 * units_padded
     cold_rows = z_count * COLD_PART
-    message = shape((HCAP + COLD_PART, lanes), BF)
-    by_relay = range(3, z_count, 2)
+    message = shape((MESSAGE, lanes), BF)
+    long_message = shape((MESSAGE + COLD_PART, lanes), BF)
     pos, hot_own, *messages = call(
         functools.partial(dispatch_kernel, base),
         [shape((TOP, token_count), jnp.int32), shape((used, width), BF)]
-        + [shape((COLD_PART, lanes), BF) if k in by_relay else message for k in range(z_count)],
+        + [message, message]
+        + [long_message] * (z_count // 2 - 1),
         "dispatch",
         scratch=[((HCAP + cold_rows, lanes), BF)],
         smem=(5, 6),
@@ -486,25 +493,19 @@
         *hot_weights,
     )
 
-    chunks = all_along_z(messages)
-    by_pair = swap(hot_own, 2)
-    by_x = swap(hot_own, 1)
-    first_out, hot_own, _ = lax.optimization_barrier((messages[0], hot_own, chunks[1]))
-    first_out, hot_own = call(
+    chunks = [messages[0], along_z(messages[1], 1)]
+    for index in range(2, len(messages)):
+        direct = along_z(messages[index], 2 * index - 2)
+        (onward,) = call(relay_kernel, [message], "relay_rows")(direct)
+        chunks += [direct, along_z(onward, 1)]
+    first_out, hot_out, _ = lax.optimization_barrier((messages[0], hot_own, chunks[1]))
+    first_out, hot_out = call(
         copy_kernel, [message, shape(hot_own.shape, BF)], "own_rows"
-    )(first_out, hot_own)
+    )(first_out, hot_out)
     chunks[0] = first_out
-    by_pair_out, first_out, hot_own = lax.optimization_barrier((by_pair, first_out, hot_own))
-    weights = [hot_own, by_x, by_pair, swap(by_pair_out, 1)]
+    weights = [hot_out] + [swap(hot_own, mask) for mask in (1, 2, 3)]
     (away,) = call(away_kernel, [shape((cold_rows // 2, lanes), BF)], "cold_away")(*chunks)
-    cold_chunks = list(chunks)
-    for k in by_relay:
-        chunks[k] = along_z(chunks[k - 1], 1)
-    other_chunks = [other_core(chunk) for chunk in chunks]
-    cold_chunks += [
-        other_core(cold_chunks[k]) if k in by_relay else other_chunks[k] for k in range(z_count)
-    ]
-    chunks = chunks + other_chunks
+    chunks = chunks + [other_core(chunk) for chunk in chunks]
     cold_mine = swap(away, 1)
     cold_other = other_core(cold_mine)
 
@@ -545,7 +546,7 @@
             pltpu.SemaphoreType.DMA((3,)),
         ],
         out_hbm=(2, 3, 4),
-    )(*cold_chunks, cold_mine, cold_other, cold_gate, cold_up, cold_down)
+    )(*chunks, cold_mine, cold_other, cold_gate, cold_up, cold_down)
 
     hot_got, cold_got = other_core(hot_dx_out), other_core(cold_out)
     part = (HALF + 2 * CAP, lanes)
@@ -554,8 +555,7 @@
     )(hot_dx, hot_got, cold_own, cold_got)
     term_x, _ = lax.optimization_barrier((sent_terms[0], cold_mine))
     got_x, got_y = swap(term_x, 1), swap(sent_terms[1], 2)
-    last_term, cold_out = lax.optimization_barrier((sent_terms[2], cold_out))
-    *parts, got_x, got_y = lax.optimization_barrier((*parts, got_x, got_y))
+    *parts, got_x, got_y, last_term = lax.optimization_barrier((*parts, got_x, got_y, sent_terms[2]))
     parts = all_along_z(parts)
     got_terms = [got_x, got_y, swap(last_term, 3)]
 

time: 77.6 us -> 71 us (0.915)
  waiting for transfers between devices: 34.1 us -> 29.4 us
  starting transfers between devices: 27.6 us -> 25.8 us
    ppermute x10, waiting for transfers between devices: 14.5 us -> 9.24 us  [swap(): return lax.ppermute(value, ('dp', 'pair'), perm)]
    ppermute x10, starting transfers between devices: 14.6 us -> 12.5 us  [swap(): return lax.ppermute(value, ('dp', 'pair'), perm)]
    ppermute x7 -> x6, waiting for transfers between devices: 16.7 us -> 17.6 us  [along_z(): return lax.ppermute(value, 'dp', perm)]
    ppermute x8 -> x7, starting transfers between devices: 1.1 us -> 1.79 us  [other_core(): return lax.ppermute(value, 'dp', [(i, i ^ 1) for i in range(count)])]
    ppermute x7 -> x6, starting transfers between devices: 11.9 us -> 11.5 us  [along_z(): return lax.ppermute(value, 'dp', perm)]
    ppermute x8 -> x7, waiting for transfers between devices: 2.9 us -> 2.57 us  [other_core(): return lax.ppermute(value, 'dp', [(i, i ^ 1) for i in range(count)])]
    pallas_call x9 -> x10, Pallas kernels: 12.9 us -> 12.9 us  [run(): pl.pallas_call(kernel, out_shape=outs, in_specs=[pl.BlockSpec(memory_spac...]
  transfers between devices with their start and end apart: 25 -> 23, of which waited for: 12 -> 12; matrix products, arithmetic and copies ran while one was open for 0% -> 0% of each run, Pallas kernels for 11% -> 12%
where the time goes in v4:
time: 71 us; the launch traced here: 70.8 us
  waiting for transfers between devices  29.4 us (41%)
  starting transfers between devices  25.8 us (36%)
  Pallas kernels  12.9 us (18%)
  local copies, waits for them, and re-layouts  1.98 us (3%)
  between operations  0.75 us (1%)
    ppermute x6, waiting for transfers between devices, along_z(): return lax.ppermute(value, 'dp', perm)  17.6 us
    pallas_call x10, Pallas kernels, run(): pl.pallas_call(kernel, out_shape=outs, in_specs=[pl.BlockSpec(memory_spac...  12.9 us
    ppermute x10, starting transfers between devices, swap(): return lax.ppermute(value, ('dp', 'pair'), perm)  12.5 us
    ppermute x6, starting transfers between devices, along_z(): return lax.ppermute(value, 'dp', perm)  11.5 us
    ppermute x10, waiting for transfers between devices, swap(): return lax.ppermute(value, ('dp', 'pair'), perm)  9.24 us
    ppermute x7, waiting for transfers between devices, other_core(): return lax.ppermute(value, 'dp', [(i, i ^ 1) for i in range(count)])  2.57 us
    unnamed x12, local copies, waits for them, and re-layouts  1.98 us
    ppermute x7, starting transfers between devices, other_core(): return lax.ppermute(value, 'dp', [(i, i ^ 1) for i in range(count)])  1.79 us
  transfers between devices with their start and end apart: 23, of which 12 were waited for; matrix products, arithmetic and copies ran while one was open for 0% of the time, Pallas kernels for 12%

profile of v4, /device:TPU:0, one launch (start us, length us, event | category | flops | bytes accessed | tf_op | source)
XLA Modules:
  0.0 70.8 jit_solution(14669861225209606997)
XLA Ops:
  0.6 2.9 %dispatch.1 = (s32[2,192]{1,0:T(2,128)}, bf16[120,1792]{1,0:T(8,128)(2,1)}, bf16[64,1920]{1,0:T(8,128)(2,1)}, bf16[64,1920]{1,0:T(8,128)(2,1)}, bf16[80,1920]{1,0:T(8,128)(2,1)}) custom-call(bf16[192,1792]{1,0:T(8,128)(2,1)} %refs_0_.1, bf16[192,1792]{1,0:T(8,128)(2,1)} %refs_1_.1, bf16[2,192]{1,0:T(2,128)(2,1)} %bitcast.6, s32[2,192]{1,0:T(2,128)} %bitcast.4, ...), custom_call_target="tpu_custom_call" | custom-call | flops 1024 | bytes 1024 | tf_op jit(solution)/shard_map/dispatch/pallas_call | solution.py:403
  3.5 4.0 %collective-permute-start.1 = (bf16[80,1920]{1,0:T(8,128)(2,1)}, bf16[80,1920]{1,0:T(8,128)(2,1)S(1)}, u32[]{:S(2)}, u32[]{:S(2)}) collective-permute-start(bf16[80,1920]{1,0:T(8,128)(2,1)} %get-tuple-element.60), channel_id=1, source_target_pairs={{0,16},{2,18},{4,20},{6,22},{8,24},{10,26},{12,28},{14,30},{16,0},... | collective-permute-start | bytes 921608 | tf_op jit(solution)/shard_map/ppermute | solution.py:460
  7.5 2.4 %collective-permute-start.10 = (bf16[120,1792]{1,0:T(8,128)(2,1)}, bf16[120,1792]{1,0:T(8,128)(2,1)S(1)}, u32[]{:S(2)}, u32[]{:S(2)}) collective-permute-start(bf16[120,1792]{1,0:T(8,128)(2,1)} %get-tuple-element.58.refs_1_), channel_id=1, source_target_pairs={{0,5},{1,4},{2,7},{3,6},{4,1},{5,0},{6,3},{7,2},{8,13},{9,12},{10,... | collective-permute-start | bytes 1290248 | tf_op jit(solution)/shard_map/ppermute | solution.py:456
  10.0 0.5 collective-permute-start.9
  10.5 1.6 %collective-permute-start = (bf16[64,1920]{1,0:T(8,128)(2,1)}, bf16[64,1920]{1,0:T(8,128)(2,1)S(1)}, u32[]{:S(2)}, u32[]{:S(2)}) collective-permute-start(bf16[64,1920]{1,0:T(8,128)(2,1)} %get-tuple-element.56), channel_id=1, source_target_pairs={{0,8},{2,10},{4,12},{6,14},{8,0},{10,2},{12,4},{14,6},{16,24},{18,... | collective-permute-start | bytes 737288 | tf_op jit(solution)/shard_map/ppermute | solution.py:460
  12.1 0.5 collective-permute-start.8
  12.6 9.1 %collective-permute-done.1.in_ref.refs_2_ = bf16[80,1920]{1,0:T(8,128)(2,1)S(1)} collective-permute-done((bf16[80,1920]{1,0:T(8,128)(2,1)}, bf16[80,1920]{1,0:T(8,128)(2,1)S(1)}, u32[]{:S(2)}, u32[]{:S(2)}) %collective-permute-start.1) | collective-permute-done | bytes 307232 | tf_op jit(solution)/shard_map/ppermute | solution.py:460
  21.7 0.8 %collective-permute-start.2 = (bf16[64,1920]{1,0:T(8,128)(2,1)S(1)}, bf16[64,1920]{1,0:T(8,128)(2,1)S(1)}, u32[]{:S(2)}, u32[]{:S(2)}) collective-permute-start(bf16[64,1920]{1,0:T(8,128)(2,1)S(1)} %relay_rows.1), channel_id=1, source_target_pairs={{0,8},{2,10},{4,12},{6,14},{8,0},{10,2},{12,4},{14,6},{16,24},{18,... | collective-permute-start | bytes 737288 | tf_op jit(solution)/shard_map/ppermute | solution.py:460
  22.6 0.4 collective-permute-done.refs_1_
  23.0 0.0 collective-permute-start.6
  23.0 0.0 copy-start.3
  23.0 1.0 %copy-done.3 = bf16[120,1792]{1,0:T(8,128)(2,1)S(1)} copy-done((bf16[120,1792]{1,0:T(8,128)(2,1)S(1)}, bf16[120,1792]{1,0:T(8,128)(2,1)}, u32[]{:S(2)}) %copy-start.3) | copy-done | bytes 430104
  24.0 0.0 copy-start.4
  24.0 0.9 %copy-done.4 = bf16[64,1920]{1,0:T(8,128)(2,1)S(1)} copy-done((bf16[64,1920]{1,0:T(8,128)(2,1)S(1)}, bf16[64,1920]{1,0:T(8,128)(2,1)}, u32[]{:S(2)}) %copy-start.4) | copy-done | bytes 245784
  25.0 0.0 collective-permute-done.10.refs_11_
  25.0 0.6 collective-permute-start.5
  25.6 3.7 %collective-permute-done.9.refs_10_ = bf16[120,1792]{1,0:T(8,128)(2,1)S(1)} collective-permute-done((bf16[120,1792]{1,0:T(8,128)(2,1)}, bf16[120,1792]{1,0:T(8,128)(2,1)S(1)}, u32[]{:S(2)}, u32[]{:S(2)}) %collective-permute-start.9) | collective-permute-done | bytes 430112 | tf_op jit(solution)/shard_map/ppermute | solution.py:456
  29.2 0.0 collective-permute-start.4
  29.3 0.0 collective-permute-done.2.refs_3_
  29.3 0.5 collective-permute-start.7
  29.8 0.0 collective-permute-done.8.refs_9_
  29.8 1.6 %collective-permute-start.3 = (bf16[32,1920]{1,0:T(8,128)(2,1)S(1)}, bf16[32,1920]{1,0:T(8,128)(2,1)S(1)}, u32[]{:S(2)}, u32[]{:S(2)}) collective-permute-start(bf16[32,1920]{1,0:T(8,128)(2,1)S(1)} %cold_away.1), channel_id=1, source_target_pairs={{0,4},{1,5},{2,6},{3,7},{4,0},{5,1},{6,2},{7,3},{8,12},{9,13},{10,... | collective-permute-start | bytes 368648 | tf_op jit(solution)/shard_map/ppermute | solution.py:456
  31.3 0.0 collective-permute-done.5.refs_5_
  31.3 0.0 collective-permute-done.4.refs_4_
  31.3 0.0 collective-permute-done.6.refs_6_
  31.3 0.0 collective-permute-done.7.refs_7_
  31.4 0.0 copy-start
  31.4 0.0 copy-start.1
  31.4 0.0 copy-start.2
  31.4 2.7 %hot.1 = (f32[96,1920]{1,0:T(8,128)S(1)}, bf16[96,1920]{1,0:T(8,128)(2,1)S(1)}, f32[120,1792]{1,0:T(8,128)S(1)}, bf16[120,1792]{1,0:T(8,128)(2,1)S(1)}, bf16[120...) custom-call(bf16[64,1920]{1,0:T(8,128)(2,1)S(1)} %get-tuple-element.59.refs_0_, ...), custom_call_target="tpu_custom_call" | custom-call | flops 1024 | bytes 1024 | tf_op jit(solution)/shard_map/hot/pallas_call | solution.py:403
  34.1 1.0 %collective-permute-done.3.refs_8_ = bf16[32,1920]{1,0:T(8,128)(2,1)S(1)} collective-permute-done((bf16[32,1920]{1,0:T(8,128)(2,1)S(1)}, bf16[32,1920]{1,0:T(8,128)(2,1)S(1)}, u32[]{:S(2)}, u32[]{:S(2)}) %collective-permute-start.3) | collective-permute-done | bytes 122912 | tf_op jit(solution)/shard_map/ppermute | solution.py:456
  35.1 1.5 %collective-permute-start.14 = (bf16[120,1792]{1,0:T(8,128)(2,1)S(1)}, bf16[120,1792]{1,0:T(8,128)(2,1)S(1)}, u32[]{:S(2)}, u32[]{:S(2)}) collective-permute-start(bf16[120,1792]{1,0:T(8,128)(2,1)S(1)} %get-tuple-element.73), channel_id=1, source_target_pairs={{0,4},{1,5},{2,6},{3,7},{4,0},{5,1},{6,2},{7,3},{8,12},{9,13},{10,... | collective-permute-start | bytes 1290248 | tf_op jit(solution)/shard_map/ppermute | solution.py:456
  36.6 0.9 %collective-permute-start.15 = (bf16[120,1792]{1,0:T(8,128)(2,1)S(1)}, bf16[120,1792]{1,0:T(8,128)(2,1)S(1)}, u32[]{:S(2)}, u32[]{:S(2)}) collective-permute-start(bf16[120,1792]{1,0:T(8,128)(2,1)S(1)} %get-tuple-element.74), channel_id=1, source_target_pairs={{0,1},{1,0},{2,3},{3,2},{4,5},{5,4},{6,7},{7,6},{8,9},{9,8},{10,11... | collective-permute-start | bytes 1290248 | tf_op jit(solution)/shard_map/ppermute | solution.py:456
  37.5 0.0 collective-permute-start.11
  37.5 0.5 collective-permute-start.12
  38.0 1.4 %collective-permute-done.12.refs_9_ = bf16[32,1920]{1,0:T(8,128)(2,1)S(1)} collective-permute-done((bf16[32,1920]{1,0:T(8,128)(2,1)S(1)}, bf16[32,1920]{1,0:T(8,128)(2,1)S(1)}, u32[]{:S(2)}, u32[]{:S(2)}) %collective-permute-start.12) | collective-permute-done | bytes 122912 | tf_op jit(solution)/shard_map/ppermute | solution.py:468
  39.4 0.0 copy-done
  39.4 0.0 copy-done.1
  39.4 0.0 copy-done.2
  39.4 4.4 %cold.1 = (f32[32,1920]{1,0:T(8,128)S(1)}, bf16[32,1920]{1,0:T(8,128)(2,1)S(1)}, bf16[1,320,1792]{2,1,0:T(8,128)(2,1)}, bf16[1,320,1792]{2,1,0:T(8,128)(2,1)}, bf16[1,320,1792]{2,1,0:T(8,128)(2,1)}) custom-call(bf16[64,1920]{1,0:T(8,128)(2,1)S(1)} %get-tuple-element.59.refs_0_, bf16[64,1920]{1,0:T(8,128)(2,1)S(1)} %collective-permute-done.refs_1_, ...), custom_call_target="tpu_custom_call" | custom-call | flops 1024 | bytes 1024 | tf_op jit(solution)/shard_map/cold/pallas_call | solution.py:403
  43.8 0.2 collective-permute-start.13
  44.0 1.2 %collective-permute-done.13.cold_got_ref = bf16[32,1920]{1,0:T(8,128)(2,1)S(1)} collective-permute-done((bf16[32,1920]{1,0:T(8,128)(2,1)S(1)}, bf16[32,1920]{1,0:T(8,128)(2,1)S(1)}, u32[]{:S(2)}, u32[]{:S(2)}) %collective-permute-start.13) | collective-permute-done | bytes 122912 | tf_op jit(solution)/shard_map/ppermute | solution.py:468
  45.2 0.0 collective-permute-done.11.hot_got_ref
  45.2 0.3 add_cores.1
  45.5 0.6 collective-permute-done.14.a_ref
  46.1 1.2 %collective-permute-done.15.b_ref = bf16[120,1792]{1,0:T(8,128)(2,1)S(1)} collective-permute-done((bf16[120,1792]{1,0:T(8,128)(2,1)S(1)}, bf16[120,1792]{1,0:T(8,128)(2,1)S(1)}, u32[]{:S(2)}, u32[]{:S(2)}) %collective-permute-start.15) | collective-permute-done | bytes 430112 | tf_op jit(solution)/shard_map/ppermute | solution.py:456
  47.3 1.5 %collective-permute-start.19 = (bf16[120,1792]{1,0:T(8,128)(2,1)S(1)}, bf16[120,1792]{1,0:T(8,128)(2,1)S(1)}, u32[]{:S(2)}, u32[]{:S(2)}) collective-permute-start(bf16[120,1792]{1,0:T(8,128)(2,1)S(1)} %get-tuple-element.84), channel_id=1, source_target_pairs={{0,5},{1,4},{2,7},{3,6},{4,1},{5,0},{6,3},{7,2},{8,13},{9,12},{10,... | collective-permute-start | bytes 1290248 | tf_op jit(solution)/shard_map/ppermute | solution.py:456
  48.8 1.6 %collective-permute-start.16 = (bf16[32,1920]{1,0:T(8,128)(2,1)S(1)}, bf16[32,1920]{1,0:T(8,128)(2,1)S(1)}, u32[]{:S(2)}, u32[]{:S(2)}) collective-permute-start(bf16[32,1920]{1,0:T(8,128)(2,1)S(1)} %get-tuple-element.77), channel_id=1, source_target_pairs={{0,8},{2,10},{4,12},{6,14},{8,0},{10,2},{12,4},{14,6},{16,24},{18,... | collective-permute-start | bytes 368648 | tf_op jit(solution)/shard_map/ppermute | solution.py:460
  50.3 3.4 %collective-permute-start.17 = (bf16[32,1920]{1,0:T(8,128)(2,1)S(1)}, bf16[32,1920]{1,0:T(8,128)(2,1)S(1)}, u32[]{:S(2)}, u32[]{:S(2)}) collective-permute-start(bf16[32,1920]{1,0:T(8,128)(2,1)S(1)} %get-tuple-element.78), channel_id=1, source_target_pairs={{0,16},{2,18},{4,20},{6,22},{8,24},{10,26},{12,28},{14,30},{16,0},... | collective-permute-start | bytes 368648 | tf_op jit(solution)/shard_map/ppermute | solution.py:460
  53.8 0.0 collective-permute-start.18
  53.8 0.9 %collective-permute-done.16.refs_1_ = bf16[32,1920]{1,0:T(8,128)(2,1)S(1)} collective-permute-done((bf16[32,1920]{1,0:T(8,128)(2,1)S(1)}, bf16[32,1920]{1,0:T(8,128)(2,1)S(1)}, u32[]{:S(2)}, u32[]{:S(2)}) %collective-permute-start.16) | collective-permute-done | bytes 122912 | tf_op jit(solution)/shard_map/ppermute | solution.py:460
  54.7 7.1 %collective-permute-done.17.refs_2_ = bf16[32,1920]{1,0:T(8,128)(2,1)S(1)} collective-permute-done((bf16[32,1920]{1,0:T(8,128)(2,1)S(1)}, bf16[32,1920]{1,0:T(8,128)(2,1)S(1)}, u32[]{:S(2)}, u32[]{:S(2)}) %collective-permute-start.17) | collective-permute-done | bytes 122912 | tf_op jit(solution)/shard_map/ppermute | solution.py:460
  61.9 0.0 collective-permute-done.18.refs_3_
  61.9 0.3 combine.1
  62.2 0.6 collective-permute-start.20
  62.7 2.4 %collective-permute-start.22 = (bf16[16,1920]{1,0:T(8,128)(2,1)S(1)}, bf16[16,1920]{1,0:T(8,128)(2,1)S(1)}, u32[]{:S(2)}, u32[]{:S(2)}) collective-permute-start(bf16[16,1920]{1,0:T(8,128)(2,1)S(1)} %get-tuple-element.90), channel_id=1, source_target_pairs={{0,5},{1,4},{2,7},{3,6},{4,1},{5,0},{6,3},{7,2},{8,13},{9,12},{10,... | collective-permute-start | bytes 184328 | tf_op jit(solution)/shard_map/ppermute | solution.py:456
  65.1 0.6 collective-permute-start.21
  65.7 0.0 collective-permute-done.19.c_ref
  65.7 0.9 %hot_sum.1 = (bf16[40,1792]{1,0:T(8,128)(2,1)}, bf16[40,1792]{1,0:T(8,128)(2,1)}, bf16[40,1792]{1,0:T(8,128)(2,1)}) custom-call(f32[120,1792]{1,0:T(8,128)S(1)} %get-tuple-element.81.own_ref, bf16[120,1792]{1,0:T(8,128)(2,1)S(1)} %collective-permute-done.14.a_ref, bf16[120,1792]{1,0:T(8,128)(2,1)S(1)} %collective-permute-done.15.b_ref, ...), custom_call_target="tpu_custom_call" | custom-call | flops 1024 | bytes 1024 | tf_op jit(solution)/shard_map/hot_sum/pallas_call | solution.py:403
  66.6 1.4 %collective-permute-done.22.xy_ref = bf16[16,1920]{1,0:T(8,128)(2,1)S(1)} collective-permute-done((bf16[16,1920]{1,0:T(8,128)(2,1)S(1)}, bf16[16,1920]{1,0:T(8,128)(2,1)S(1)}, u32[]{:S(2)}, u32[]{:S(2)}) %collective-permute-start.22) | collective-permute-done | bytes 61472 | tf_op jit(solution)/shard_map/ppermute | solution.py:456
  68.0 1.4 %collective-permute-done.21.x_ref = bf16[16,1920]{1,0:T(8,128)(2,1)S(1)} collective-permute-done((bf16[16,1920]{1,0:T(8,128)(2,1)S(1)}, bf16[16,1920]{1,0:T(8,128)(2,1)S(1)}, u32[]{:S(2)}, u32[]{:S(2)}) %collective-permute-start.21) | collective-permute-done | bytes 61472 | tf_op jit(solution)/shard_map/ppermute | solution.py:456
  69.3 0.0 collective-permute-done.20.y_ref
  69.3 0.0 copy-done.5
  69.3 1.4 %finish.1 = (bf16[96,1792]{1,0:T(8,128)(2,1)}, f32[2,96]{1,0:T(2,128)}) custom-call(f32[40,1920]{1,0:T(8,128)S(1)} %get-tuple-element.88.own_ref, bf16[40,1920]{1,0:T(8,128)(2,1)S(1)} %collective-permute-done.20.y_ref, bf16[16,1920]{1,0:T(8,128)(2,1)S(1)} %collective-permute-done.21.x_ref, bf16[16,1920]{1,0:T(8,128)(2,1)S(1)} %collective-permute-done.22.xy_ref, ...), custom_call_target="tpu_custom_call" | custom-call | flops 1024 | bytes 1024 | tf_op jit(solution)/shard_map/finish/pallas_call | solution.py:403
  (4 shorter events, 0.1 us)
Async XLA Ops:
  3.5 18.2 %collective-permute-start.1 = (bf16[80,1920]{1,0:T(8,128)(2,1)}, bf16[80,1920]{1,0:T(8,128)(2,1)S(1)}, u32[]{:S(2)}, u32[]{:S(2)}) collective-permute-start(bf16[80,1920]{1,0:T(8,128)(2,1)} %get-tuple-element.60), channel_id=1, source_target_pairs={{0,16},{2,18},{4,20},{6,22},{8,24},{10,26},{12,28},{14,30},{16,0},... | collective-permute-start | bytes 921608 | tf_op jit(solution)/shard_map/ppermute | solution.py:460
  7.5 17.4 %collective-permute-start.10 = (bf16[120,1792]{1,0:T(8,128)(2,1)}, bf16[120,1792]{1,0:T(8,128)(2,1)S(1)}, u32[]{:S(2)}, u32[]{:S(2)}) collective-permute-start(bf16[120,1792]{1,0:T(8,128)(2,1)} %get-tuple-element.58.refs_1_), channel_id=1, source_target_pairs={{0,5},{1,4},{2,7},{3,6},{4,1},{5,0},{6,3},{7,2},{8,13},{9,12},{10,... | collective-permute-start | bytes 1290248 | tf_op jit(solution)/shard_map/ppermute | solution.py:456
  10.0 19.2 %collective-permute-start.9 = (bf16[120,1792]{1,0:T(8,128)(2,1)}, bf16[120,1792]{1,0:T(8,128)(2,1)S(1)}, u32[]{:S(2)}, u32[]{:S(2)}) collective-permute-start(bf16[120,1792]{1,0:T(8,128)(2,1)} %get-tuple-element.58.refs_1_), channel_id=1, source_target_pairs={{0,1},{1,0},{2,3},{3,2},{4,5},{5,4},{6,7},{7,6},{8,9},{9,8},{10,11... | collective-permute-start | bytes 1290248 | tf_op jit(solution)/shard_map/ppermute | solution.py:456
  10.5 12.5 %collective-permute-start = (bf16[64,1920]{1,0:T(8,128)(2,1)}, bf16[64,1920]{1,0:T(8,128)(2,1)S(1)}, u32[]{:S(2)}, u32[]{:S(2)}) collective-permute-start(bf16[64,1920]{1,0:T(8,128)(2,1)} %get-tuple-element.56), channel_id=1, source_target_pairs={{0,8},{2,10},{4,12},{6,14},{8,0},{10,2},{12,4},{14,6},{16,24},{18,... | collective-permute-start | bytes 737288 | tf_op jit(solution)/shard_map/ppermute | solution.py:460
  12.1 17.7 %collective-permute-start.8 = (bf16[120,1792]{1,0:T(8,128)(2,1)}, bf16[120,1792]{1,0:T(8,128)(2,1)S(1)}, u32[]{:S(2)}, u32[]{:S(2)}) collective-permute-start(bf16[120,1792]{1,0:T(8,128)(2,1)} %get-tuple-element.58.refs_1_), channel_id=1, source_target_pairs={{0,4},{1,5},{2,6},{3,7},{4,0},{5,1},{6,2},{7,3},{8,12},{9,13},{10,... | collective-permute-start | bytes 1290248 | tf_op jit(solution)/shard_map/ppermute | solution.py:456
  21.7 7.5 %collective-permute-start.2 = (bf16[64,1920]{1,0:T(8,128)(2,1)S(1)}, bf16[64,1920]{1,0:T(8,128)(2,1)S(1)}, u32[]{:S(2)}, u32[]{:S(2)}) collective-permute-start(bf16[64,1920]{1,0:T(8,128)(2,1)S(1)} %relay_rows.1), channel_id=1, source_target_pairs={{0,8},{2,10},{4,12},{6,14},{8,0},{10,2},{12,4},{14,6},{16,24},{18,... | collective-permute-start | bytes 737288 | tf_op jit(solution)/shard_map/ppermute | solution.py:460
  23.0 8.4 %collective-permute-start.6 = (bf16[80,1920]{1,0:T(8,128)(2,1)S(1)}, bf16[80,1920]{1,0:T(8,128)(2,1)S(1)}, u32[]{:S(2)}, u32[]{:S(2)}) collective-permute-start(bf16[80,1920]{1,0:T(8,128)(2,1)S(1)} %collective-permute-done.1.in_ref.refs_2_), channel_id=1, source_target_pairs={{0,2},{2,0},{4,6},{6,4},{8,10},{10,8},{12,14},{14,12},{16,18},{18,... | collective-permute-start | bytes 921608 | tf_op jit(solution)/shard_map/ppermute | solution.py:468
  23.0 1.0 %copy-start.3 = (bf16[120,1792]{1,0:T(8,128)(2,1)S(1)}, bf16[120,1792]{1,0:T(8,128)(2,1)}, u32[]{:S(2)}) copy-start(bf16[120,1792]{1,0:T(8,128)(2,1)} %get-tuple-element.58.refs_1_) | copy-start | bytes 1290244
  24.0 0.9 %copy-start.4 = (bf16[64,1920]{1,0:T(8,128)(2,1)S(1)}, bf16[64,1920]{1,0:T(8,128)(2,1)}, u32[]{:S(2)}) copy-start(bf16[64,1920]{1,0:T(8,128)(2,1)} %get-tuple-element.57.refs_0_) | copy-start | bytes 737284
  25.0 6.3 %collective-permute-start.5 = (bf16[64,1920]{1,0:T(8,128)(2,1)S(1)}, bf16[64,1920]{1,0:T(8,128)(2,1)S(1)}, u32[]{:S(2)}, u32[]{:S(2)}) collective-permute-start(bf16[64,1920]{1,0:T(8,128)(2,1)S(1)} %collective-permute-done.refs_1_), channel_id=1, source_target_pairs={{0,2},{2,0},{4,6},{6,4},{8,10},{10,8},{12,14},{14,12},{16,18},{18,... | collective-permute-start | bytes 737288 | tf_op jit(solution)/shard_map/ppermute | solution.py:468
  29.2 2.1 %collective-permute-start.4 = (bf16[64,1920]{1,0:T(8,128)(2,1)S(1)}, bf16[64,1920]{1,0:T(8,128)(2,1)S(1)}, u32[]{:S(2)}, u32[]{:S(2)}) collective-permute-start(bf16[64,1920]{1,0:T(8,128)(2,1)S(1)} %get-tuple-element.59.refs_0_), channel_id=1, source_target_pairs={{0,2},{2,0},{4,6},{6,4},{8,10},{10,8},{12,14},{14,12},{16,18},{18,... | collective-permute-start | bytes 737288 | tf_op jit(solution)/shard_map/ppermute | solution.py:468
  29.3 2.1 %collective-permute-start.7 = (bf16[64,1920]{1,0:T(8,128)(2,1)S(1)}, bf16[64,1920]{1,0:T(8,128)(2,1)S(1)}, u32[]{:S(2)}, u32[]{:S(2)}) collective-permute-start(bf16[64,1920]{1,0:T(8,128)(2,1)S(1)} %collective-permute-done.2.refs_3_), channel_id=1, source_target_pairs={{0,2},{2,0},{4,6},{6,4},{8,10},{10,8},{12,14},{14,12},{16,18},{18,... | collective-permute-start | bytes 737288 | tf_op jit(solution)/shard_map/ppermute | solution.py:468
  29.8 5.3 %collective-permute-start.3 = (bf16[32,1920]{1,0:T(8,128)(2,1)S(1)}, bf16[32,1920]{1,0:T(8,128)(2,1)S(1)}, u32[]{:S(2)}, u32[]{:S(2)}) collective-permute-start(bf16[32,1920]{1,0:T(8,128)(2,1)S(1)} %cold_away.1), channel_id=1, source_target_pairs={{0,4},{1,5},{2,6},{3,7},{4,0},{5,1},{6,2},{7,3},{8,12},{9,13},{10,... | collective-permute-start | bytes 368648 | tf_op jit(solution)/shard_map/ppermute | solution.py:456
  31.4 8.0 %copy-start = (bf16[1,320,1792]{2,1,0:T(8,128)(2,1)S(1)}, bf16[1,320,1792]{2,1,0:T(8,128)(2,1)}, u32[]{:S(2)}) copy-start(bf16[1,320,1792]{2,1,0:T(8,128)(2,1)} %refs_10_.1) | copy-start | bytes 3440644
  31.4 8.0 %copy-start.1 = (bf16[1,320,1792]{2,1,0:T(8,128)(2,1)S(1)}, bf16[1,320,1792]{2,1,0:T(8,128)(2,1)}, u32[]{:S(2)}) copy-start(bf16[1,320,1792]{2,1,0:T(8,128)(2,1)} %refs_11_.1) | copy-start | bytes 3440644
  31.4 8.0 %copy-start.2 = (bf16[1,320,1792]{2,1,0:T(8,128)(2,1)S(1)}, bf16[1,320,1792]{2,1,0:T(8,128)(2,1)}, u32[]{:S(2)}) copy-start(bf16[1,320,1792]{2,1,0:T(8,128)(2,1)} %refs_12_.1) | copy-start | bytes 3440644
  35.1 11.0 %collective-permute-start.14 = (bf16[120,1792]{1,0:T(8,128)(2,1)S(1)}, bf16[120,1792]{1,0:T(8,128)(2,1)S(1)}, u32[]{:S(2)}, u32[]{:S(2)}) collective-permute-start(bf16[120,1792]{1,0:T(8,128)(2,1)S(1)} %get-tuple-element.73), channel_id=1, source_target_pairs={{0,4},{1,5},{2,6},{3,7},{4,0},{5,1},{6,2},{7,3},{8,12},{9,13},{10,... | collective-permute-start | bytes 1290248 | tf_op jit(solution)/shard_map/ppermute | solution.py:456
  36.6 10.7 %collective-permute-start.15 = (bf16[120,1792]{1,0:T(8,128)(2,1)S(1)}, bf16[120,1792]{1,0:T(8,128)(2,1)S(1)}, u32[]{:S(2)}, u32[]{:S(2)}) collective-permute-start(bf16[120,1792]{1,0:T(8,128)(2,1)S(1)} %get-tuple-element.74), channel_id=1, source_target_pairs={{0,1},{1,0},{2,3},{3,2},{4,5},{5,4},{6,7},{7,6},{8,9},{9,8},{10,11... | collective-permute-start | bytes 1290248 | tf_op jit(solution)/shard_map/ppermute | solution.py:456
  37.5 7.7 %collective-permute-start.11 = (bf16[96,1920]{1,0:T(8,128)(2,1)S(1)}, bf16[96,1920]{1,0:T(8,128)(2,1)S(1)}, u32[]{:S(2)}, u32[]{:S(2)}) collective-permute-start(bf16[96,1920]{1,0:T(8,128)(2,1)S(1)} %get-tuple-element.64), channel_id=1, source_target_pairs={{0,2},{2,0},{4,6},{6,4},{8,10},{10,8},{12,14},{14,12},{16,18},{18,... | collective-permute-start | bytes 1105928 | tf_op jit(solution)/shard_map/ppermute | solution.py:468
  37.5 1.9 %collective-permute-start.12 = (bf16[32,1920]{1,0:T(8,128)(2,1)S(1)}, bf16[32,1920]{1,0:T(8,128)(2,1)S(1)}, u32[]{:S(2)}, u32[]{:S(2)}) collective-permute-start(bf16[32,1920]{1,0:T(8,128)(2,1)S(1)} %collective-permute-done.3.refs_8_), channel_id=1, source_target_pairs={{0,2},{2,0},{4,6},{6,4},{8,10},{10,8},{12,14},{14,12},{16,18},{18,... | collective-permute-start | bytes 368648 | tf_op jit(solution)/shard_map/ppermute | solution.py:468
  43.8 1.4 %collective-permute-start.13 = (bf16[32,1920]{1,0:T(8,128)(2,1)S(1)}, bf16[32,1920]{1,0:T(8,128)(2,1)S(1)}, u32[]{:S(2)}, u32[]{:S(2)}) collective-permute-start(bf16[32,1920]{1,0:T(8,128)(2,1)S(1)} %get-tuple-element.67), channel_id=1, source_target_pairs={{0,2},{2,0},{4,6},{6,4},{8,10},{10,8},{12,14},{14,12},{16,18},{18,... | collective-permute-start | bytes 368648 | tf_op jit(solution)/shard_map/ppermute | solution.py:468
  47.3 18.4 %collective-permute-start.19 = (bf16[120,1792]{1,0:T(8,128)(2,1)S(1)}, bf16[120,1792]{1,0:T(8,128)(2,1)S(1)}, u32[]{:S(2)}, u32[]{:S(2)}) collective-permute-start(bf16[120,1792]{1,0:T(8,128)(2,1)S(1)} %get-tuple-element.84), channel_id=1, source_target_pairs={{0,5},{1,4},{2,7},{3,6},{4,1},{5,0},{6,3},{7,2},{8,13},{9,12},{10,... | collective-permute-start | bytes 1290248 | tf_op jit(solution)/shard_map/ppermute | solution.py:456
  48.8 6.0 %collective-permute-start.16 = (bf16[32,1920]{1,0:T(8,128)(2,1)S(1)}, bf16[32,1920]{1,0:T(8,128)(2,1)S(1)}, u32[]{:S(2)}, u32[]{:S(2)}) collective-permute-start(bf16[32,1920]{1,0:T(8,128)(2,1)S(1)} %get-tuple-element.77), channel_id=1, source_target_pairs={{0,8},{2,10},{4,12},{6,14},{8,0},{10,2},{12,4},{14,6},{16,24},{18,... | collective-permute-start | bytes 368648 | tf_op jit(solution)/shard_map/ppermute | solution.py:460
  50.3 11.5 %collective-permute-start.17 = (bf16[32,1920]{1,0:T(8,128)(2,1)S(1)}, bf16[32,1920]{1,0:T(8,128)(2,1)S(1)}, u32[]{:S(2)}, u32[]{:S(2)}) collective-permute-start(bf16[32,1920]{1,0:T(8,128)(2,1)S(1)} %get-tuple-element.78), channel_id=1, source_target_pairs={{0,16},{2,18},{4,20},{6,22},{8,24},{10,26},{12,28},{14,30},{16,0},... | collective-permute-start | bytes 368648 | tf_op jit(solution)/shard_map/ppermute | solution.py:460
  53.8 8.1 %collective-permute-start.18 = (bf16[32,1920]{1,0:T(8,128)(2,1)S(1)}, bf16[32,1920]{1,0:T(8,128)(2,1)S(1)}, u32[]{:S(2)}, u32[]{:S(2)}) collective-permute-start(bf16[32,1920]{1,0:T(8,128)(2,1)S(1)} %get-tuple-element.79), channel_id=1, source_target_pairs={{0,24},{2,26},{4,28},{6,30},{8,16},{10,18},{12,20},{14,22},{16,8},... | collective-permute-start | bytes 368648 | tf_op jit(solution)/shard_map/ppermute | solution.py:460
  62.2 7.2 %copy-start.5 = (s32[2,192]{1,0:T(2,128)S(1)}, s32[2,192]{1,0:T(2,128)}, u32[]{:S(2)}) copy-start(s32[2,192]{1,0:T(2,128)} %get-tuple-element.91.pos_ref) | copy-start | bytes 4612
  62.2 7.2 %collective-permute-start.20 = (bf16[40,1920]{1,0:T(8,128)(2,1)S(1)}, bf16[40,1920]{1,0:T(8,128)(2,1)S(1)}, u32[]{:S(2)}, u32[]{:S(2)}) collective-permute-start(bf16[40,1920]{1,0:T(8,128)(2,1)S(1)} %get-tuple-element.89), channel_id=1, source_target_pairs={{0,1},{1,0},{2,3},{3,2},{4,5},{5,4},{6,7},{7,6},{8,9},{9,8},{10,11... | collective-permute-start | bytes 460808 | tf_op jit(solution)/shard_map/ppermute | solution.py:456
  62.7 5.2 %collective-permute-start.22 = (bf16[16,1920]{1,0:T(8,128)(2,1)S(1)}, bf16[16,1920]{1,0:T(8,128)(2,1)S(1)}, u32[]{:S(2)}, u32[]{:S(2)}) collective-permute-start(bf16[16,1920]{1,0:T(8,128)(2,1)S(1)} %get-tuple-element.90), channel_id=1, source_target_pairs={{0,5},{1,4},{2,7},{3,6},{4,1},{5,0},{6,3},{7,2},{8,13},{9,12},{10,... | collective-permute-start | bytes 184328 | tf_op jit(solution)/shard_map/ppermute | solution.py:456
  65.1 4.2 %collective-permute-start.21 = (bf16[16,1920]{1,0:T(8,128)(2,1)S(1)}, bf16[16,1920]{1,0:T(8,128)(2,1)S(1)}, u32[]{:S(2)}, u32[]{:S(2)}) collective-permute-start(bf16[16,1920]{1,0:T(8,128)(2,1)S(1)} %get-tuple-element.90), channel_id=1, source_target_pairs={{0,4},{1,5},{2,6},{3,7},{4,0},{5,1},{6,2},{7,3},{8,12},{9,13},{10,... | collective-permute-start | bytes 184328 | tf_op jit(solution)/shard_map/ppermute | solution.py:456

commit v5 on v4

--- a/solution.py
+++ b/solution.py
@@ -80,18 +80,13 @@
 
 
 def gather_rows(out_ref, start, target, is_grad, pos, prob, tok_ref, grad_ref):
-    width = tok_ref.shape[1]
-    at = pl.ds(start, target.shape[0])
     first = pos[0:1, :] == target
     second = pos[1:2, :] == target
-    chosen = jnp.where(first | second, 1.0, 0.0)
-    rows = dot(jnp.where(is_grad, 0.0, chosen).astype(BF), tok_ref[...]) + dot(
-        jnp.where(is_grad, chosen, 0.0).astype(BF), grad_ref[...]
-    )
-    out_ref[at, :width] = rows.astype(BF)
+    chosen = jnp.where((first | second) & ~is_grad, 1.0, 0.0)
     weight = jnp.where(first, prob[0:1, :], 0.0) + jnp.where(second, prob[1:2, :], 0.0)
-    weight = jnp.sum(jnp.where(is_grad, 0.0, weight), axis=1, keepdims=True)
-    out_ref[at, width:] = tail_lanes(weight).astype(BF)
+    weight = jnp.where(is_grad, weight, 0.0)
+    rows = dot(chosen.astype(BF), tok_ref[...]) + dot(weight.astype(BF), grad_ref[...])
+    out_ref[pl.ds(start, target.shape[0]), :] = rows.astype(BF)
 
 
 def dispatch_kernel(base, *refs):
@@ -141,13 +136,12 @@
     out_ref[...] = jnp.concatenate(rows, axis=0).astype(BF)
 
 
-def swiglu_back(pre_gate, pre_up, back, prob):
+def swiglu_back(pre_gate, pre_up, back):
     sig = 1.0 / (1.0 + jnp.exp(-pre_gate))
     act = pre_gate * sig
     hidden = act * pre_up
-    scaled = prob * back
-    gate_grad = scaled * pre_up * sig * (1.0 + pre_gate * (1.0 - sig))
-    return gate_grad, scaled * act, prob * hidden, hidden * back
+    gate_grad = back * pre_up * sig * (1.0 + pre_gate * (1.0 - sig))
+    return gate_grad, back * act, hidden, hidden * back
 
 
 def write_rows(out_ref, rows, prob):
@@ -167,11 +161,10 @@
     chunks = refs[:chunk_count]
     weights = refs[chunk_count : chunk_count + 4]
     own_ref, send_ref, *terms = refs[chunk_count + 4 : chunk_count + 10]
-    rows_ref, tail_ref, wide_ref, sum_ref = refs[chunk_count + 10 :]
+    rows_ref, wide_ref, sum_ref = refs[chunk_count + 10 :]
     width = rows_ref.shape[1]
     for k, chunk in enumerate(chunks):
-        rows_ref[k * HCAP : (k + 1) * HCAP, :] = chunk[COLD_PART:MESSAGE, :width]
-        tail_ref[k * HCAP : (k + 1) * HCAP, :] = chunk[COLD_PART:MESSAGE, width:]
+        rows_ref[k * HCAP : (k + 1) * HCAP, :] = chunk[COLD_PART:MESSAGE, :]
     used = 3 * units
     for j, w_ref in enumerate(weights):
         start = j * UNIT_BLOCK
@@ -187,8 +180,6 @@
 
     def block(start):
         at = pl.ds(start, block_rows)
-        prob = tail_ref[at, :].astype(F32).reshape(block_chunks, HCAP, TAIL)[:, :HALF, 0:1]
-        prob = prob.reshape(half_rows, 1)
         pre = dot(rows_ref[at, :], wide_ref[...], NT).reshape(block_chunks, HCAP, columns)
         pre_x = pre[:, :HALF].reshape(half_rows, columns)
         pre_g = pre[:, HALF:].reshape(half_rows, columns)
@@ -197,7 +188,6 @@
             pre_x,
             pltpu.roll(pre_x, columns - units, 1),
             pltpu.roll(pre_g, columns - 2 * units, 1),
-            prob,
         )
         gate_grad, up_grad, weighted, prob_term = (
             jnp.where(first, value, 0.0) for value in (gate_grad, up_grad, weighted, prob_term)
@@ -240,7 +230,7 @@
     mine_x_ref, other_x_ref, gate_ref, up_ref, down_ref = refs[message_count : message_count + 5]
     own_ref, send_ref, *outs = refs[message_count + 5 : message_count + 10]
     data_ref, dx_ref, grad_ref, sum_ref, out_sem = refs[message_count + 10 :]
-    total, width = data_ref.shape[0], gate_ref.shape[2]
+    total = data_ref.shape[0]
     rows = COLD_ROWS
     single = rows == total
     stores = [
@@ -261,13 +251,11 @@
 
     def block(start):
         at = pl.ds(start, rows)
-        data = data_ref[at, :width]
-        first = jnp.where((iota((8, TAIL), 0) == 0) & (iota((8, TAIL), 1) == 0), 1.0, 0.0)
-        prob = dot(first.astype(BF), data_ref[at, width:], NT)[0:1, :]
+        data = data_ref[at, :]
         pre_gate = dot(gate_ref[0], data, NT)
         pre_up = dot(up_ref[0], data, NT)
         back = pltpu.roll(dot(down_ref[0], data, NT), rows - CAP, 1)
-        gate_grad, up_grad, weighted, prob_term = swiglu_back(pre_gate, pre_up, back, prob)
+        gate_grad, up_grad, weighted, prob_term = swiglu_back(pre_gate, pre_up, back)
         x_lane = (iota(pre_gate.shape, 1) & 4) == 0
         gate_grad = jnp.where(x_lane, gate_grad, 0.0)
         up_grad = jnp.where(x_lane, up_grad, 0.0)
@@ -351,7 +339,9 @@
     write_rows(send_x_ref, away[:, :width], away[:, width : width + 1])
 
 
-def finish_kernel(base, own_ref, y_ref, x_ref, xy_ref, pos_ref, dx_ref, prob_ref):
+def finish_kernel(
+    base, own_ref, y_ref, x_ref, xy_ref, pos_ref, weight_ref, dx_ref, prob_ref
+):
     pair = lax.axis_index("pair")
     me = lax.axis_index("dp")
     z, x = me // 4, (me // 2) % 2
@@ -385,8 +375,10 @@
             terms = jnp.sum(jnp.where(routes[k], prob, 0.0), axis=0, keepdims=True)
             grad_prob[k] = grad_prob[k] + terms
     dx_ref[...] = total.astype(BF)
+    weight = weight_ref[...].astype(F32)
+    weight = jnp.where(pair == 0, weight[:, :half], weight[:, half:])
     for k in range(TOP):
-        prob_ref[k : k + 1, :] = grad_prob[k]
+        prob_ref[k : k + 1, :] = grad_prob[k] / weight[k : k + 1, :]
 
 
 def sum_kernel(own_ref, a_ref, b_ref, c_ref, gate_ref, up_ref, down_ref):
@@ -471,15 +463,15 @@
     units_padded = units + pad
     used = 3 * units_padded
     cold_rows = z_count * COLD_PART
-    message = shape((MESSAGE, lanes), BF)
-    long_message = shape((MESSAGE + COLD_PART, lanes), BF)
+    message = shape((MESSAGE, width), BF)
+    long_message = shape((MESSAGE + COLD_PART, width), BF)
     pos, hot_own, *messages = call(
         functools.partial(dispatch_kernel, base),
         [shape((TOP, token_count), jnp.int32), shape((used, width), BF)]
         + [message, message]
         + [long_message] * (z_count // 2 - 1),
         "dispatch",
-        scratch=[((HCAP + cold_rows, lanes), BF)],
+        scratch=[((HCAP + cold_rows, width), BF)],
         smem=(5, 6),
         limit=VMEM_LIMIT,
     )(
@@ -504,7 +496,7 @@
     )(first_out, hot_out)
     chunks[0] = first_out
     weights = [hot_out] + [swap(hot_own, mask) for mask in (1, 2, 3)]
-    (away,) = call(away_kernel, [shape((cold_rows // 2, lanes), BF)], "cold_away")(*chunks)
+    (away,) = call(away_kernel, [shape((cold_rows // 2, width), BF)], "cold_away")(*chunks)
     chunks = chunks + [other_core(chunk) for chunk in chunks]
     cold_mine = swap(away, 1)
     cold_other = other_core(cold_mine)
@@ -527,7 +519,6 @@
         "hot",
         scratch=[
             ((all_rows, width), BF),
-            ((all_rows, TAIL), BF),
             ((4 * UNIT_BLOCK, width), BF),
             ((4, used, width) if chunk_count > CHUNK_BLOCK else (8, 128), F32),
         ],
@@ -539,7 +530,7 @@
         [shape((cold_rows // 2, lanes), F32), shape((cold_rows // 2, lanes), BF)] + [cold_shape] * 3,
         "cold",
         scratch=[
-            ((2 * cold_rows, lanes), BF),
+            ((2 * cold_rows, width), BF),
             ((cold_rows, lanes), F32),
             ((3, cold_units, width), BF),
             ((3, cold_units, width) if 2 * cold_rows > COLD_ROWS else (8, 128), F32),
@@ -555,7 +546,8 @@
     )(hot_dx, hot_got, cold_own, cold_got)
     term_x, _ = lax.optimization_barrier((sent_terms[0], cold_mine))
     got_x, got_y = swap(term_x, 1), swap(sent_terms[1], 2)
-    *parts, got_x, got_y, last_term = lax.optimization_barrier((*parts, got_x, got_y, sent_terms[2]))
+    *parts, last_term = lax.optimization_barrier((*parts, sent_terms[2]))
+    *parts, got_x, got_y = lax.optimization_barrier((*parts, got_x, got_y))
     parts = all_along_z(parts)
     got_terms = [got_x, got_y, swap(last_term, 3)]
 
@@ -579,7 +571,7 @@
         functools.partial(finish_kernel, base),
         [shape((half, width), BF), shape((TOP, half), F32)],
         "finish",
-    )(own_rows, rows_y, rows_x, rows_xy, pos)
+    )(own_rows, rows_y, rows_x, rows_xy, pos, gate_probs.T)
 
     if pad:
         hot_grads = [value[:units] for value in hot_grads]

time: 71 us -> 72.2 us (1.017)
  waiting for transfers between devices: 29.4 us -> 30.9 us
    ppermute x10, waiting for transfers between devices: 9.24 us -> 11.6 us  [swap(): return lax.ppermute(value, ('dp', 'pair'), perm)]
    ppermute x6, waiting for transfers between devices: 17.6 us -> 16.8 us  [along_z(): return lax.ppermute(value, 'dp', perm)]
    unnamed x12 -> x14, local copies, waits for them, and re-layouts: 1.98 us -> 2 us
where the time goes in v5:
time: 72.2 us; the launch traced here: 71.9 us
  waiting for transfers between devices  30.9 us (43%)
  starting transfers between devices  25.5 us (35%)
  Pallas kernels  12.8 us (18%)
  local copies, waits for them, and re-layouts  2 us (3%)
  between operations  0.76 us (1%)
    ppermute x6, waiting for transfers between devices, along_z(): return lax.ppermute(value, 'dp', perm)  16.8 us
    ppermute x10, starting transfers between devices, swap(): return lax.ppermute(value, ('dp', 'pair'), perm)  13 us
    pallas_call x10, Pallas kernels, run(): pl.pallas_call(kernel, out_shape=outs, in_specs=[pl.BlockSpec(memory_spac...  12.8 us
    ppermute x10, waiting for transfers between devices, swap(): return lax.ppermute(value, ('dp', 'pair'), perm)  11.6 us
    ppermute x6, starting transfers between devices, along_z(): return lax.ppermute(value, 'dp', perm)  11.2 us
    ppermute x7, waiting for transfers between devices, other_core(): return lax.ppermute(value, 'dp', [(i, i ^ 1) for i in range(count)])  2.52 us
    unnamed x14, local copies, waits for them, and re-layouts  2 us
  transfers between devices with their start and end apart: 23, of which 12 were waited for; matrix products, arithmetic and copies ran while one was open for 0% of the time, Pallas kernels for 12%

profile of v5, /device:TPU:0, one launch (start us, length us, event | category | flops | bytes accessed | tf_op | source)
XLA Modules:
  0.0 71.9 jit_solution(5801401257527033975)
XLA Ops:
  0.6 2.8 %dispatch.1 = (s32[2,192]{1,0:T(2,128)}, bf16[120,1792]{1,0:T(8,128)(2,1)}, bf16[64,1792]{1,0:T(8,128)(2,1)}, bf16[64,1792]{1,0:T(8,128)(2,1)}, bf16[80,1792]{1,0:T(8,128)(2,1)}) custom-call(bf16[192,1792]{1,0:T(8,128)(2,1)} %refs_0_.1, bf16[192,1792]{1,0:T(8,128)(2,1)} %refs_1_.1, bf16[2,192]{1,0:T(2,128)(2,1)} %bitcast.4, s32[2,192]{1,0:T(2,128)} %bitcast.6, ...), custom_call_target="tpu_custom_call" | custom-call | flops 1024 | bytes 1024 | tf_op jit(solution)/shard_map/dispatch/pallas_call | solution.py:395
  3.5 4.0 %collective-permute-start.1 = (bf16[80,1792]{1,0:T(8,128)(2,1)}, bf16[80,1792]{1,0:T(8,128)(2,1)S(1)}, u32[]{:S(2)}, u32[]{:S(2)}) collective-permute-start(bf16[80,1792]{1,0:T(8,128)(2,1)} %get-tuple-element.64), channel_id=1, source_target_pairs={{0,16},{2,18},{4,20},{6,22},{8,24},{10,26},{12,28},{14,30},{16,0},... | collective-permute-start | bytes 860168 | tf_op jit(solution)/shard_map/ppermute | solution.py:452
  7.5 2.4 %collective-permute-start.10 = (bf16[120,1792]{1,0:T(8,128)(2,1)}, bf16[120,1792]{1,0:T(8,128)(2,1)S(1)}, u32[]{:S(2)}, u32[]{:S(2)}) collective-permute-start(bf16[120,1792]{1,0:T(8,128)(2,1)} %get-tuple-element.62.refs_1_), channel_id=1, source_target_pairs={{0,5},{1,4},{2,7},{3,6},{4,1},{5,0},{6,3},{7,2},{8,13},{9,12},{10,... | collective-permute-start | bytes 1290248 | tf_op jit(solution)/shard_map/ppermute | solution.py:448
  10.0 0.5 collective-permute-start.9
  10.5 1.6 %collective-permute-start = (bf16[64,1792]{1,0:T(8,128)(2,1)}, bf16[64,1792]{1,0:T(8,128)(2,1)S(1)}, u32[]{:S(2)}, u32[]{:S(2)}) collective-permute-start(bf16[64,1792]{1,0:T(8,128)(2,1)} %get-tuple-element.60), channel_id=1, source_target_pairs={{0,8},{2,10},{4,12},{6,14},{8,0},{10,2},{12,4},{14,6},{16,24},{18,... | collective-permute-start | bytes 688136 | tf_op jit(solution)/shard_map/ppermute | solution.py:452
  12.0 8.8 %collective-permute-done.1.in_ref.refs_2_ = bf16[80,1792]{1,0:T(8,128)(2,1)S(1)} collective-permute-done((bf16[80,1792]{1,0:T(8,128)(2,1)}, bf16[80,1792]{1,0:T(8,128)(2,1)S(1)}, u32[]{:S(2)}, u32[]{:S(2)}) %collective-permute-start.1) | collective-permute-done | bytes 286752 | tf_op jit(solution)/shard_map/ppermute | solution.py:452
  20.8 0.8 %collective-permute-start.2 = (bf16[64,1792]{1,0:T(8,128)(2,1)S(1)}, bf16[64,1792]{1,0:T(8,128)(2,1)S(1)}, u32[]{:S(2)}, u32[]{:S(2)}) collective-permute-start(bf16[64,1792]{1,0:T(8,128)(2,1)S(1)} %relay_rows.1), channel_id=1, source_target_pairs={{0,8},{2,10},{4,12},{6,14},{8,0},{10,2},{12,4},{14,6},{16,24},{18,... | collective-permute-start | bytes 688136 | tf_op jit(solution)/shard_map/ppermute | solution.py:452
  21.7 1.4 %collective-permute-start.8 = (bf16[120,1792]{1,0:T(8,128)(2,1)}, bf16[120,1792]{1,0:T(8,128)(2,1)S(1)}, u32[]{:S(2)}, u32[]{:S(2)}) collective-permute-start(bf16[120,1792]{1,0:T(8,128)(2,1)} %get-tuple-element.62.refs_1_), channel_id=1, source_target_pairs={{0,4},{1,5},{2,6},{3,7},{4,0},{5,1},{6,2},{7,3},{8,12},{9,13},{10,... | collective-permute-start | bytes 1290248 | tf_op jit(solution)/shard_map/ppermute | solution.py:448
  23.1 0.0 collective-permute-done.refs_1_
  23.1 0.0 collective-permute-start.6
  23.1 0.0 copy-start.3
  23.1 1.0 %copy-done.3 = bf16[120,1792]{1,0:T(8,128)(2,1)S(1)} copy-done((bf16[120,1792]{1,0:T(8,128)(2,1)S(1)}, bf16[120,1792]{1,0:T(8,128)(2,1)}, u32[]{:S(2)}) %copy-start.3) | copy-done | bytes 430104
  24.1 0.9 %copy-done.4 = bf16[64,1792]{1,0:T(8,128)(2,1)S(1)} copy-done((bf16[64,1792]{1,0:T(8,128)(2,1)S(1)}, bf16[64,1792]{1,0:T(8,128)(2,1)}, u32[]{:S(2)}) %copy-start.4) | copy-done | bytes 229400
  25.1 0.0 collective-permute-done.10.refs_11_
  25.1 0.5 collective-permute-start.5
  25.7 3.5 %collective-permute-done.9.refs_10_ = bf16[120,1792]{1,0:T(8,128)(2,1)S(1)} collective-permute-done((bf16[120,1792]{1,0:T(8,128)(2,1)}, bf16[120,1792]{1,0:T(8,128)(2,1)S(1)}, u32[]{:S(2)}, u32[]{:S(2)}) %collective-permute-start.9) | collective-permute-done | bytes 430112 | tf_op jit(solution)/shard_map/ppermute | solution.py:448
  29.2 0.0 collective-permute-start.4
  29.2 0.0 collective-permute-done.2.refs_3_
  29.2 0.5 collective-permute-start.7
  29.7 3.7 %collective-permute-done.8.refs_9_ = bf16[120,1792]{1,0:T(8,128)(2,1)S(1)} collective-permute-done((bf16[120,1792]{1,0:T(8,128)(2,1)}, bf16[120,1792]{1,0:T(8,128)(2,1)S(1)}, u32[]{:S(2)}, u32[]{:S(2)}) %collective-permute-start.8) | collective-permute-done | bytes 430112 | tf_op jit(solution)/shard_map/ppermute | solution.py:448
  33.4 1.4 %collective-permute-start.3 = (bf16[32,1792]{1,0:T(8,128)(2,1)S(1)}, bf16[32,1792]{1,0:T(8,128)(2,1)S(1)}, u32[]{:S(2)}, u32[]{:S(2)}) collective-permute-start(bf16[32,1792]{1,0:T(8,128)(2,1)S(1)} %cold_away.1), channel_id=1, source_target_pairs={{0,4},{1,5},{2,6},{3,7},{4,0},{5,1},{6,2},{7,3},{8,12},{9,13},{10,... | collective-permute-start | bytes 344072 | tf_op jit(solution)/shard_map/ppermute | solution.py:448
  34.9 0.0 collective-permute-done.5.refs_5_
  34.9 0.0 collective-permute-done.4.refs_4_
  34.9 0.0 collective-permute-done.6.refs_6_
  34.9 0.0 collective-permute-done.7.refs_7_
  34.9 0.0 copy-start
  34.9 0.0 copy-start.1
  34.9 0.0 copy-start.2
  34.9 2.6 %hot.1 = (f32[96,1920]{1,0:T(8,128)S(1)}, bf16[96,1920]{1,0:T(8,128)(2,1)S(1)}, f32[120,1792]{1,0:T(8,128)S(1)}, bf16[120,1792]{1,0:T(8,128)(2,1)S(1)}, bf16[120...) custom-call(bf16[64,1792]{1,0:T(8,128)(2,1)S(1)} %get-tuple-element.63.refs_0_, ...), custom_call_target="tpu_custom_call" | custom-call | flops 1024 | bytes 1024 | tf_op jit(solution)/shard_map/hot/pallas_call | solution.py:395
  37.6 0.1 collective-permute-start.11
  37.6 0.6 collective-permute-done.3.refs_8_
  38.2 1.4 %collective-permute-start.14 = (bf16[120,1792]{1,0:T(8,128)(2,1)S(1)}, bf16[120,1792]{1,0:T(8,128)(2,1)S(1)}, u32[]{:S(2)}, u32[]{:S(2)}) collective-permute-start(bf16[120,1792]{1,0:T(8,128)(2,1)S(1)} %get-tuple-element.82), channel_id=1, source_target_pairs={{0,4},{1,5},{2,6},{3,7},{4,0},{5,1},{6,2},{7,3},{8,12},{9,13},{10,... | collective-permute-start | bytes 1290248 | tf_op jit(solution)/shard_map/ppermute | solution.py:448
  39.6 1.5 %collective-permute-start.15 = (bf16[120,1792]{1,0:T(8,128)(2,1)S(1)}, bf16[120,1792]{1,0:T(8,128)(2,1)S(1)}, u32[]{:S(2)}, u32[]{:S(2)}) collective-permute-start(bf16[120,1792]{1,0:T(8,128)(2,1)S(1)} %get-tuple-element.83), channel_id=1, source_target_pairs={{0,1},{1,0},{2,3},{3,2},{4,5},{5,4},{6,7},{7,6},{8,9},{9,8},{10,11... | collective-permute-start | bytes 1290248 | tf_op jit(solution)/shard_map/ppermute | solution.py:448
  41.2 0.0 collective-permute-start.12
  41.2 1.3 %collective-permute-done.12.refs_9_ = bf16[32,1792]{1,0:T(8,128)(2,1)S(1)} collective-permute-done((bf16[32,1792]{1,0:T(8,128)(2,1)S(1)}, bf16[32,1792]{1,0:T(8,128)(2,1)S(1)}, u32[]{:S(2)}, u32[]{:S(2)}) %collective-permute-start.12) | collective-permute-done | bytes 114720 | tf_op jit(solution)/shard_map/ppermute | solution.py:460
  42.5 0.0 copy-done
  42.5 0.0 copy-done.1
  42.5 0.0 copy-done.2
  42.5 4.4 %cold.1 = (f32[32,1920]{1,0:T(8,128)S(1)}, bf16[32,1920]{1,0:T(8,128)(2,1)S(1)}, bf16[1,320,1792]{2,1,0:T(8,128)(2,1)}, bf16[1,320,1792]{2,1,0:T(8,128)(2,1)}, bf16[1,320,1792]{2,1,0:T(8,128)(2,1)}) custom-call(bf16[64,1792]{1,0:T(8,128)(2,1)S(1)} %get-tuple-element.63.refs_0_, bf16[64,1792]{1,0:T(8,128)(2,1)S(1)} %collective-permute-done.refs_1_, ...), custom_call_target="tpu_custom_call" | custom-call | flops 1024 | bytes 1024 | tf_op jit(solution)/shard_map/cold/pallas_call | solution.py:395
  46.9 0.2 collective-permute-start.13
  47.1 1.2 %collective-permute-done.13.cold_got_ref = bf16[32,1920]{1,0:T(8,128)(2,1)S(1)} collective-permute-done((bf16[32,1920]{1,0:T(8,128)(2,1)S(1)}, bf16[32,1920]{1,0:T(8,128)(2,1)S(1)}, u32[]{:S(2)}, u32[]{:S(2)}) %collective-permute-start.13) | collective-permute-done | bytes 122912 | tf_op jit(solution)/shard_map/ppermute | solution.py:460
  48.3 0.0 collective-permute-done.11.hot_got_ref
  48.3 0.3 add_cores.1
  48.6 0.6 collective-permute-start.19
  49.2 0.8 %collective-permute-done.14.a_ref = bf16[120,1792]{1,0:T(8,128)(2,1)S(1)} collective-permute-done((bf16[120,1792]{1,0:T(8,128)(2,1)S(1)}, bf16[120,1792]{1,0:T(8,128)(2,1)S(1)}, u32[]{:S(2)}, u32[]{:S(2)}) %collective-permute-start.14) | collective-permute-done | bytes 430112 | tf_op jit(solution)/shard_map/ppermute | solution.py:448
  50.0 0.3 collective-permute-done.15.b_ref
  50.3 0.5 collective-permute-start.16
  50.7 3.2 %collective-permute-start.17 = (bf16[32,1920]{1,0:T(8,128)(2,1)S(1)}, bf16[32,1920]{1,0:T(8,128)(2,1)S(1)}, u32[]{:S(2)}, u32[]{:S(2)}) collective-permute-start(bf16[32,1920]{1,0:T(8,128)(2,1)S(1)} %get-tuple-element.86), channel_id=1, source_target_pairs={{0,16},{2,18},{4,20},{6,22},{8,24},{10,26},{12,28},{14,30},{16,0},... | collective-permute-start | bytes 368648 | tf_op jit(solution)/shard_map/ppermute | solution.py:452
  53.9 1.1 %collective-permute-start.18 = (bf16[32,1920]{1,0:T(8,128)(2,1)S(1)}, bf16[32,1920]{1,0:T(8,128)(2,1)S(1)}, u32[]{:S(2)}, u32[]{:S(2)}) collective-permute-start(bf16[32,1920]{1,0:T(8,128)(2,1)S(1)} %get-tuple-element.87), channel_id=1, source_target_pairs={{0,24},{2,26},{4,28},{6,30},{8,16},{10,18},{12,20},{14,22},{16,8},... | collective-permute-start | bytes 368648 | tf_op jit(solution)/shard_map/ppermute | solution.py:452
  55.0 1.2 %collective-permute-done.16.refs_1_ = bf16[32,1920]{1,0:T(8,128)(2,1)S(1)} collective-permute-done((bf16[32,1920]{1,0:T(8,128)(2,1)S(1)}, bf16[32,1920]{1,0:T(8,128)(2,1)S(1)}, u32[]{:S(2)}, u32[]{:S(2)}) %collective-permute-start.16) | collective-permute-done | bytes 122912 | tf_op jit(solution)/shard_map/ppermute | solution.py:452
  56.2 6.8 %collective-permute-done.17.refs_2_ = bf16[32,1920]{1,0:T(8,128)(2,1)S(1)} collective-permute-done((bf16[32,1920]{1,0:T(8,128)(2,1)S(1)}, bf16[32,1920]{1,0:T(8,128)(2,1)S(1)}, u32[]{:S(2)}, u32[]{:S(2)}) %collective-permute-start.17) | collective-permute-done | bytes 122912 | tf_op jit(solution)/shard_map/ppermute | solution.py:452
  63.0 0.0 collective-permute-done.18.refs_3_
  63.0 0.3 combine.1
  63.3 1.6 %collective-permute-start.20 = (bf16[40,1920]{1,0:T(8,128)(2,1)S(1)}, bf16[40,1920]{1,0:T(8,128)(2,1)S(1)}, u32[]{:S(2)}, u32[]{:S(2)}) collective-permute-start(bf16[40,1920]{1,0:T(8,128)(2,1)S(1)} %get-tuple-element.97), channel_id=1, source_target_pairs={{0,1},{1,0},{2,3},{3,2},{4,5},{5,4},{6,7},{7,6},{8,9},{9,8},{10,11... | collective-permute-start | bytes 460808 | tf_op jit(solution)/shard_map/ppermute | solution.py:448
  64.9 1.4 %collective-permute-start.22 = (bf16[16,1920]{1,0:T(8,128)(2,1)S(1)}, bf16[16,1920]{1,0:T(8,128)(2,1)S(1)}, u32[]{:S(2)}, u32[]{:S(2)}) collective-permute-start(bf16[16,1920]{1,0:T(8,128)(2,1)S(1)} %get-tuple-element.98), channel_id=1, source_target_pairs={{0,5},{1,4},{2,7},{3,6},{4,1},{5,0},{6,3},{7,2},{8,13},{9,12},{10,... | collective-permute-start | bytes 184328 | tf_op jit(solution)/shard_map/ppermute | solution.py:448
  66.3 0.6 collective-permute-start.21
  66.9 0.0 collective-permute-done.19.c_ref
  66.9 0.9 %hot_sum.1 = (bf16[40,1792]{1,0:T(8,128)(2,1)}, bf16[40,1792]{1,0:T(8,128)(2,1)}, bf16[40,1792]{1,0:T(8,128)(2,1)}) custom-call(f32[120,1792]{1,0:T(8,128)S(1)} %get-tuple-element.89.own_ref, bf16[120,1792]{1,0:T(8,128)(2,1)S(1)} %collective-permute-done.14.a_ref, bf16[120,1792]{1,0:T(8,128)(2,1)S(1)} %collective-permute-done.15.b_ref, ...), custom_call_target="tpu_custom_call" | custom-call | flops 1024 | bytes 1024 | tf_op jit(solution)/shard_map/hot_sum/pallas_call | solution.py:395
  67.8 2.2 %collective-permute-done.22.xy_ref = bf16[16,1920]{1,0:T(8,128)(2,1)S(1)} collective-permute-done((bf16[16,1920]{1,0:T(8,128)(2,1)S(1)}, bf16[16,1920]{1,0:T(8,128)(2,1)S(1)}, u32[]{:S(2)}, u32[]{:S(2)}) %collective-permute-start.22) | collective-permute-done | bytes 61472 | tf_op jit(solution)/shard_map/ppermute | solution.py:448
  70.0 0.5 collective-permute-done.21.x_ref
  70.5 0.0 collective-permute-done.20.y_ref
  70.5 0.0 copy-done.5
  70.5 0.0 copy-done.6
  70.5 1.4 %finish.1 = (bf16[96,1792]{1,0:T(8,128)(2,1)}, f32[2,96]{1,0:T(2,128)}) custom-call(f32[40,1920]{1,0:T(8,128)S(1)} %get-tuple-element.96.own_ref, bf16[40,1920]{1,0:T(8,128)(2,1)S(1)} %collective-permute-done.20.y_ref, bf16[16,1920]{1,0:T(8,128)(2,1)S(1)} %collective-permute-done.21.x_ref, bf16[16,1920]{1,0:T(8,128)(2,1)S(1)} %collective-permute-done.22.xy_ref, ...), custom_call_target="tpu_custom_call" | custom-call | flops 1024 | bytes 1024 | tf_op jit(solution)/shard_map/finish/pallas_call | solution.py:395
  (6 shorter events, 0.1 us)
Async XLA Ops:
  3.5 17.3 %collective-permute-start.1 = (bf16[80,1792]{1,0:T(8,128)(2,1)}, bf16[80,1792]{1,0:T(8,128)(2,1)S(1)}, u32[]{:S(2)}, u32[]{:S(2)}) collective-permute-start(bf16[80,1792]{1,0:T(8,128)(2,1)} %get-tuple-element.64), channel_id=1, source_target_pairs={{0,16},{2,18},{4,20},{6,22},{8,24},{10,26},{12,28},{14,30},{16,0},... | collective-permute-start | bytes 860168 | tf_op jit(solution)/shard_map/ppermute | solution.py:452
  7.5 17.6 %collective-permute-start.10 = (bf16[120,1792]{1,0:T(8,128)(2,1)}, bf16[120,1792]{1,0:T(8,128)(2,1)S(1)}, u32[]{:S(2)}, u32[]{:S(2)}) collective-permute-start(bf16[120,1792]{1,0:T(8,128)(2,1)} %get-tuple-element.62.refs_1_), channel_id=1, source_target_pairs={{0,5},{1,4},{2,7},{3,6},{4,1},{5,0},{6,3},{7,2},{8,13},{9,12},{10,... | collective-permute-start | bytes 1290248 | tf_op jit(solution)/shard_map/ppermute | solution.py:448
  10.0 19.2 %collective-permute-start.9 = (bf16[120,1792]{1,0:T(8,128)(2,1)}, bf16[120,1792]{1,0:T(8,128)(2,1)S(1)}, u32[]{:S(2)}, u32[]{:S(2)}) collective-permute-start(bf16[120,1792]{1,0:T(8,128)(2,1)} %get-tuple-element.62.refs_1_), channel_id=1, source_target_pairs={{0,1},{1,0},{2,3},{3,2},{4,5},{5,4},{6,7},{7,6},{8,9},{9,8},{10,11... | collective-permute-start | bytes 1290248 | tf_op jit(solution)/shard_map/ppermute | solution.py:448
  10.5 12.6 %collective-permute-start = (bf16[64,1792]{1,0:T(8,128)(2,1)}, bf16[64,1792]{1,0:T(8,128)(2,1)S(1)}, u32[]{:S(2)}, u32[]{:S(2)}) collective-permute-start(bf16[64,1792]{1,0:T(8,128)(2,1)} %get-tuple-element.60), channel_id=1, source_target_pairs={{0,8},{2,10},{4,12},{6,14},{8,0},{10,2},{12,4},{14,6},{16,24},{18,... | collective-permute-start | bytes 688136 | tf_op jit(solution)/shard_map/ppermute | solution.py:452
  20.8 8.4 %collective-permute-start.2 = (bf16[64,1792]{1,0:T(8,128)(2,1)S(1)}, bf16[64,1792]{1,0:T(8,128)(2,1)S(1)}, u32[]{:S(2)}, u32[]{:S(2)}) collective-permute-start(bf16[64,1792]{1,0:T(8,128)(2,1)S(1)} %relay_rows.1), channel_id=1, source_target_pairs={{0,8},{2,10},{4,12},{6,14},{8,0},{10,2},{12,4},{14,6},{16,24},{18,... | collective-permute-start | bytes 688136 | tf_op jit(solution)/shard_map/ppermute | solution.py:452
  21.7 11.8 %collective-permute-start.8 = (bf16[120,1792]{1,0:T(8,128)(2,1)}, bf16[120,1792]{1,0:T(8,128)(2,1)S(1)}, u32[]{:S(2)}, u32[]{:S(2)}) collective-permute-start(bf16[120,1792]{1,0:T(8,128)(2,1)} %get-tuple-element.62.refs_1_), channel_id=1, source_target_pairs={{0,4},{1,5},{2,6},{3,7},{4,0},{5,1},{6,2},{7,3},{8,12},{9,13},{10,... | collective-permute-start | bytes 1290248 | tf_op jit(solution)/shard_map/ppermute | solution.py:448
  23.1 11.8 %collective-permute-start.6 = (bf16[80,1792]{1,0:T(8,128)(2,1)S(1)}, bf16[80,1792]{1,0:T(8,128)(2,1)S(1)}, u32[]{:S(2)}, u32[]{:S(2)}) collective-permute-start(bf16[80,1792]{1,0:T(8,128)(2,1)S(1)} %collective-permute-done.1.in_ref.refs_2_), channel_id=1, source_target_pairs={{0,2},{2,0},{4,6},{6,4},{8,10},{10,8},{12,14},{14,12},{16,18},{18,... | collective-permute-start | bytes 860168 | tf_op jit(solution)/shard_map/ppermute | solution.py:460
  23.1 1.0 %copy-start.3 = (bf16[120,1792]{1,0:T(8,128)(2,1)S(1)}, bf16[120,1792]{1,0:T(8,128)(2,1)}, u32[]{:S(2)}) copy-start(bf16[120,1792]{1,0:T(8,128)(2,1)} %get-tuple-element.62.refs_1_) | copy-start | bytes 1290244
  24.1 0.9 %copy-start.4 = (bf16[64,1792]{1,0:T(8,128)(2,1)S(1)}, bf16[64,1792]{1,0:T(8,128)(2,1)}, u32[]{:S(2)}) copy-start(bf16[64,1792]{1,0:T(8,128)(2,1)} %get-tuple-element.61.refs_0_) | copy-start | bytes 688132
  25.1 9.7 %collective-permute-start.5 = (bf16[64,1792]{1,0:T(8,128)(2,1)S(1)}, bf16[64,1792]{1,0:T(8,128)(2,1)S(1)}, u32[]{:S(2)}, u32[]{:S(2)}) collective-permute-start(bf16[64,1792]{1,0:T(8,128)(2,1)S(1)} %collective-permute-done.refs_1_), channel_id=1, source_target_pairs={{0,2},{2,0},{4,6},{6,4},{8,10},{10,8},{12,14},{14,12},{16,18},{18,... | collective-permute-start | bytes 688136 | tf_op jit(solution)/shard_map/ppermute | solution.py:460
  29.2 5.7 %collective-permute-start.4 = (bf16[64,1792]{1,0:T(8,128)(2,1)S(1)}, bf16[64,1792]{1,0:T(8,128)(2,1)S(1)}, u32[]{:S(2)}, u32[]{:S(2)}) collective-permute-start(bf16[64,1792]{1,0:T(8,128)(2,1)S(1)} %get-tuple-element.63.refs_0_), channel_id=1, source_target_pairs={{0,2},{2,0},{4,6},{6,4},{8,10},{10,8},{12,14},{14,12},{16,18},{18,... | collective-permute-start | bytes 688136 | tf_op jit(solution)/shard_map/ppermute | solution.py:460
  29.2 5.7 %collective-permute-start.7 = (bf16[64,1792]{1,0:T(8,128)(2,1)S(1)}, bf16[64,1792]{1,0:T(8,128)(2,1)S(1)}, u32[]{:S(2)}, u32[]{:S(2)}) collective-permute-start(bf16[64,1792]{1,0:T(8,128)(2,1)S(1)} %collective-permute-done.2.refs_3_), channel_id=1, source_target_pairs={{0,2},{2,0},{4,6},{6,4},{8,10},{10,8},{12,14},{14,12},{16,18},{18,... | collective-permute-start | bytes 688136 | tf_op jit(solution)/shard_map/ppermute | solution.py:460
  33.4 4.8 %collective-permute-start.3 = (bf16[32,1792]{1,0:T(8,128)(2,1)S(1)}, bf16[32,1792]{1,0:T(8,128)(2,1)S(1)}, u32[]{:S(2)}, u32[]{:S(2)}) collective-permute-start(bf16[32,1792]{1,0:T(8,128)(2,1)S(1)} %cold_away.1), channel_id=1, source_target_pairs={{0,4},{1,5},{2,6},{3,7},{4,0},{5,1},{6,2},{7,3},{8,12},{9,13},{10,... | collective-permute-start | bytes 344072 | tf_op jit(solution)/shard_map/ppermute | solution.py:448
  34.9 7.6 %copy-start = (bf16[1,320,1792]{2,1,0:T(8,128)(2,1)S(1)}, bf16[1,320,1792]{2,1,0:T(8,128)(2,1)}, u32[]{:S(2)}) copy-start(bf16[1,320,1792]{2,1,0:T(8,128)(2,1)} %refs_10_.1) | copy-start | bytes 3440644
  34.9 7.6 %copy-start.1 = (bf16[1,320,1792]{2,1,0:T(8,128)(2,1)S(1)}, bf16[1,320,1792]{2,1,0:T(8,128)(2,1)}, u32[]{:S(2)}) copy-start(bf16[1,320,1792]{2,1,0:T(8,128)(2,1)} %refs_11_.1) | copy-start | bytes 3440644
  34.9 7.6 %copy-start.2 = (bf16[1,320,1792]{2,1,0:T(8,128)(2,1)S(1)}, bf16[1,320,1792]{2,1,0:T(8,128)(2,1)}, u32[]{:S(2)}) copy-start(bf16[1,320,1792]{2,1,0:T(8,128)(2,1)} %refs_12_.1) | copy-start | bytes 3440644
  37.6 10.7 %collective-permute-start.11 = (bf16[96,1920]{1,0:T(8,128)(2,1)S(1)}, bf16[96,1920]{1,0:T(8,128)(2,1)S(1)}, u32[]{:S(2)}, u32[]{:S(2)}) collective-permute-start(bf16[96,1920]{1,0:T(8,128)(2,1)S(1)} %get-tuple-element.68), channel_id=1, source_target_pairs={{0,2},{2,0},{4,6},{6,4},{8,10},{10,8},{12,14},{14,12},{16,18},{18,... | collective-permute-start | bytes 1105928 | tf_op jit(solution)/shard_map/ppermute | solution.py:460
  38.2 11.8 %collective-permute-start.14 = (bf16[120,1792]{1,0:T(8,128)(2,1)S(1)}, bf16[120,1792]{1,0:T(8,128)(2,1)S(1)}, u32[]{:S(2)}, u32[]{:S(2)}) collective-permute-start(bf16[120,1792]{1,0:T(8,128)(2,1)S(1)} %get-tuple-element.82), channel_id=1, source_target_pairs={{0,4},{1,5},{2,6},{3,7},{4,0},{5,1},{6,2},{7,3},{8,12},{9,13},{10,... | collective-permute-start | bytes 1290248 | tf_op jit(solution)/shard_map/ppermute | solution.py:448
  39.6 10.6 %collective-permute-start.15 = (bf16[120,1792]{1,0:T(8,128)(2,1)S(1)}, bf16[120,1792]{1,0:T(8,128)(2,1)S(1)}, u32[]{:S(2)}, u32[]{:S(2)}) collective-permute-start(bf16[120,1792]{1,0:T(8,128)(2,1)S(1)} %get-tuple-element.83), channel_id=1, source_target_pairs={{0,1},{1,0},{2,3},{3,2},{4,5},{5,4},{6,7},{7,6},{8,9},{9,8},{10,11... | collective-permute-start | bytes 1290248 | tf_op jit(solution)/shard_map/ppermute | solution.py:448
  41.2 1.3 %collective-permute-start.12 = (bf16[32,1792]{1,0:T(8,128)(2,1)S(1)}, bf16[32,1792]{1,0:T(8,128)(2,1)S(1)}, u32[]{:S(2)}, u32[]{:S(2)}) collective-permute-start(bf16[32,1792]{1,0:T(8,128)(2,1)S(1)} %collective-permute-done.3.refs_8_), channel_id=1, source_target_pairs={{0,2},{2,0},{4,6},{6,4},{8,10},{10,8},{12,14},{14,12},{16,18},{18,... | collective-permute-start | bytes 344072 | tf_op jit(solution)/shard_map/ppermute | solution.py:460
  46.9 1.4 %collective-permute-start.13 = (bf16[32,1920]{1,0:T(8,128)(2,1)S(1)}, bf16[32,1920]{1,0:T(8,128)(2,1)S(1)}, u32[]{:S(2)}, u32[]{:S(2)}) collective-permute-start(bf16[32,1920]{1,0:T(8,128)(2,1)S(1)} %get-tuple-element.71), channel_id=1, source_target_pairs={{0,2},{2,0},{4,6},{6,4},{8,10},{10,8},{12,14},{14,12},{16,18},{18,... | collective-permute-start | bytes 368648 | tf_op jit(solution)/shard_map/ppermute | solution.py:460
  48.6 18.3 %collective-permute-start.19 = (bf16[120,1792]{1,0:T(8,128)(2,1)S(1)}, bf16[120,1792]{1,0:T(8,128)(2,1)S(1)}, u32[]{:S(2)}, u32[]{:S(2)}) collective-permute-start(bf16[120,1792]{1,0:T(8,128)(2,1)S(1)} %get-tuple-element.92), channel_id=1, source_target_pairs={{0,5},{1,4},{2,7},{3,6},{4,1},{5,0},{6,3},{7,2},{8,13},{9,12},{10,... | collective-permute-start | bytes 1290248 | tf_op jit(solution)/shard_map/ppermute | solution.py:448
  50.3 6.0 %collective-permute-start.16 = (bf16[32,1920]{1,0:T(8,128)(2,1)S(1)}, bf16[32,1920]{1,0:T(8,128)(2,1)S(1)}, u32[]{:S(2)}, u32[]{:S(2)}) collective-permute-start(bf16[32,1920]{1,0:T(8,128)(2,1)S(1)} %get-tuple-element.85), channel_id=1, source_target_pairs={{0,8},{2,10},{4,12},{6,14},{8,0},{10,2},{12,4},{14,6},{16,24},{18,... | collective-permute-start | bytes 368648 | tf_op jit(solution)/shard_map/ppermute | solution.py:452
  50.7 12.3 %collective-permute-start.17 = (bf16[32,1920]{1,0:T(8,128)(2,1)S(1)}, bf16[32,1920]{1,0:T(8,128)(2,1)S(1)}, u32[]{:S(2)}, u32[]{:S(2)}) collective-permute-start(bf16[32,1920]{1,0:T(8,128)(2,1)S(1)} %get-tuple-element.86), channel_id=1, source_target_pairs={{0,16},{2,18},{4,20},{6,22},{8,24},{10,26},{12,28},{14,30},{16,0},... | collective-permute-start | bytes 368648 | tf_op jit(solution)/shard_map/ppermute | solution.py:452
  53.9 9.1 %collective-permute-start.18 = (bf16[32,1920]{1,0:T(8,128)(2,1)S(1)}, bf16[32,1920]{1,0:T(8,128)(2,1)S(1)}, u32[]{:S(2)}, u32[]{:S(2)}) collective-permute-start(bf16[32,1920]{1,0:T(8,128)(2,1)S(1)} %get-tuple-element.87), channel_id=1, source_target_pairs={{0,24},{2,26},{4,28},{6,30},{8,16},{10,18},{12,20},{14,22},{16,8},... | collective-permute-start | bytes 368648 | tf_op jit(solution)/shard_map/ppermute | solution.py:452
  63.3 7.2 %copy-start.5 = (bf16[192,2]{0,1:T(2,128)(2,1)S(1)}, bf16[192,2]{0,1:T(2,128)(2,1)}, u32[]{:S(2)}) copy-start(bf16[192,2]{0,1:T(2,128)(2,1)} %param.15) | copy-start | bytes 2308
  63.3 7.2 %copy-start.6 = (s32[2,192]{1,0:T(2,128)S(1)}, s32[2,192]{1,0:T(2,128)}, u32[]{:S(2)}) copy-start(s32[2,192]{1,0:T(2,128)} %get-tuple-element.99.pos_ref) | copy-start | bytes 4612
  63.3 7.2 %collective-permute-start.20 = (bf16[40,1920]{1,0:T(8,128)(2,1)S(1)}, bf16[40,1920]{1,0:T(8,128)(2,1)S(1)}, u32[]{:S(2)}, u32[]{:S(2)}) collective-permute-start(bf16[40,1920]{1,0:T(8,128)(2,1)S(1)} %get-tuple-element.97), channel_id=1, source_target_pairs={{0,1},{1,0},{2,3},{3,2},{4,5},{5,4},{6,7},{7,6},{8,9},{9,8},{10,11... | collective-permute-start | bytes 460808 | tf_op jit(solution)/shard_map/ppermute | solution.py:448
  64.9 5.1 %collective-permute-start.22 = (bf16[16,1920]{1,0:T(8,128)(2,1)S(1)}, bf16[16,1920]{1,0:T(8,128)(2,1)S(1)}, u32[]{:S(2)}, u32[]{:S(2)}) collective-permute-start(bf16[16,1920]{1,0:T(8,128)(2,1)S(1)} %get-tuple-element.98), channel_id=1, source_target_pairs={{0,5},{1,4},{2,7},{3,6},{4,1},{5,0},{6,3},{7,2},{8,13},{9,12},{10,... | collective-permute-start | bytes 184328 | tf_op jit(solution)/shard_map/ppermute | solution.py:448
  66.3 4.2 %collective-permute-start.21 = (bf16[16,1920]{1,0:T(8,128)(2,1)S(1)}, bf16[16,1920]{1,0:T(8,128)(2,1)S(1)}, u32[]{:S(2)}, u32[]{:S(2)}) collective-permute-start(bf16[16,1920]{1,0:T(8,128)(2,1)S(1)} %get-tuple-element.98), channel_id=1, source_target_pairs={{0,4},{1,5},{2,6},{3,7},{4,0},{5,1},{6,2},{7,3},{8,12},{9,13},{10,... | collective-permute-start | bytes 184328 | tf_op jit(solution)/shard_map/ppermute | solution.py:448
